TPU v7x, 32 devices: a whole 2x2x4 slice. The times are simulated.
32 devices in a mesh: clip: 4 (over x, core), tok: 8 (over z, y).
Axes of the slice: x: 2, y: 2, z: 4, core: 2. Of those that a mesh axis runs over, the one named last changes fastest.
Arguments:
- tokens: bfloat16 [16384, 1024], P(('clip', 'tok')), may hold values from -80 to 80
- slot_keys: bfloat16 [1024, 512], replicated, may hold values from -64 to 64
- w_in: bfloat16 [8, 1024, 4096], P('tok', None, 'clip'), may hold values from -0.1875 to 0.1875
- w_back: bfloat16 [8, 4096, 1024], P('tok', 'clip'), may hold values from -0.09375 to 0.09375
- w_proj: bfloat16 [1024, 512], replicated, may hold values from -0.1875 to 0.1875
- dec_source: int32 [4, 2048], P('clip'), may hold values from 0 to 4096, as said below
- mask_token: bfloat16 [512], replicated, may hold values from -80 to 80
- w_qkv: bfloat16 [512, 1536], replicated, may hold values from -8 to 8
- w_out: bfloat16 [512, 512], replicated, may hold values from -9 to 9
Outputs:
- decoded: bfloat16 [8192, 512], P(('clip', 'tok'))
Inputs may be any that keep to these rules, and one draw needn't show every extreme that they name: `dec_source`: within a clip no visible index appears twice. For each aligned block of 256 decoder positions and each aligned block of 512 visible tokens, at most 32 positions of the first show tokens of the second, and some pair of blocks reaches 32 in every clip.
All inputs are finite; a program needn't handle non-finite values.
Results may differ from a plain program's by a relative error of at most 0.025.
Values may be sent and summed in bfloat16 or wider, within the bound.
No kernel may reach another device: no remote copies, remote signals or barrier semaphores. Data moves between devices by JAX's collectives and lax.ppermute only.
A program may use at most 64 MiB of HBM per device.

v0:
```python
import math

import jax
import jax.numpy as jnp
from jax import lax
from jax.sharding import PartitionSpec as P

HEADS = 16


def layer_norm(values):
    centre = values - jnp.mean(values, axis=-1, keepdims=True)
    spread = jnp.mean(centre * centre, axis=-1, keepdims=True)
    return centre * lax.rsqrt(spread + 1e-05)


def sinusoid(places, width):
    half = width // 2
    speeds = jnp.exp(-math.log(10000.0) * jnp.arange(half).astype(jnp.float32) / half)
    angles = places.astype(jnp.float32)[:, None] * speeds[None, :]
    return jnp.concatenate([jnp.sin(angles), jnp.cos(angles)], axis=1)


def attend(queries, key_rows, value_rows):
    heads_here, head_dim, count = queries.shape
    block = math.gcd(count, 512)
    scale = 1.0 / math.sqrt(head_dim)
    blocks = queries.reshape(heads_here, head_dim, count // block, block).transpose(2, 0, 1, 3)

    def one_block(query_block):
        scores = (
            jnp.einsum("hkq,hkn->hqn", query_block, key_rows, preferred_element_type=jnp.float32)
            * scale
        )
        highest = jnp.max(scores, axis=-1)
        raised = jnp.exp(scores - highest[..., None]).astype(jnp.bfloat16)
        totals = jnp.sum(raised.astype(jnp.float32), axis=-1)
        summed = jnp.einsum("hqn,hkn->hkq", raised, value_rows, preferred_element_type=jnp.float32)
        return (summed / totals[:, None, :]).astype(jnp.bfloat16)

    outcome = lax.map(one_block, blocks)
    return outcome.transpose(1, 2, 0, 3).reshape(heads_here, head_dim, count)


def per_device(tokens, slot_keys, w_in, w_back, w_proj, dec_source, mask_token, w_qkv, w_out):
    vis_dev, width = tokens.shape
    n_tok = lax.axis_size("tok")
    dec_width = w_proj.shape[1]
    normed = layer_norm(tokens.astype(jnp.float32)).astype(jnp.bfloat16)
    logits = jnp.dot(normed, slot_keys, preferred_element_type=jnp.float32)
    col_top = lax.pmax(jnp.max(logits, axis=0), "tok")
    dispatch = jnp.exp(logits - col_top[None, :]).astype(jnp.bfloat16)
    slot_sums = lax.dot_general(
        dispatch, normed, (((0,), (0,)), ((), ())), preferred_element_type=jnp.float32
    )
    slot_totals = jnp.sum(dispatch.astype(jnp.float32), axis=0)
    mine_sums, mine_totals = (
        lax.psum_scatter(slot_sums, "tok", scatter_dimension=0, tiled=True),
        lax.psum_scatter(slot_totals, "tok", scatter_dimension=0, tiled=True),
    )
    slot_in = (mine_sums / mine_totals[:, None]).astype(jnp.bfloat16)
    first_proj = w_in[0]
    second_proj = w_back[0]
    hidden = jax.nn.gelu(
        jnp.dot(
            lax.all_gather(slot_in, "clip", axis=0, tiled=True),
            first_proj,
            preferred_element_type=jnp.float32,
        )
    ).astype(jnp.bfloat16)
    partial_out = jnp.dot(hidden, second_proj, preferred_element_type=jnp.float32)
    slot_out = lax.psum_scatter(partial_out, "clip", scatter_dimension=0, tiled=True).astype(
        jnp.bfloat16
    )
    row_top = jnp.max(logits, axis=1, keepdims=True)
    raised = jnp.exp(logits - row_top)
    combine = (raised / jnp.sum(raised, axis=1, keepdims=True)).astype(jnp.bfloat16)
    moe = jnp.dot(
        combine,
        lax.all_gather(slot_out, "tok", axis=0, tiled=True),
        preferred_element_type=jnp.float32,
    ).astype(jnp.bfloat16)
    projected = jnp.dot(moe, w_proj, preferred_element_type=jnp.float32).astype(jnp.bfloat16)
    listing = dec_source[0]
    dec_total = listing.shape[0]
    dec_dev = dec_total // n_tok
    vis_all = vis_dev * n_tok
    myself = lax.axis_index("tok")
    own_list = lax.dynamic_slice_in_dim(listing, myself * dec_dev, dec_dev)
    visible = own_list < vis_all
    places = myself * dec_dev + jnp.arange(dec_dev)
    filler = (mask_token.astype(jnp.float32)[None, :] + sinusoid(places, dec_width)).astype(
        jnp.bfloat16
    )
    capacity = dec_dev // n_tok
    blocks = listing.reshape(n_tok, dec_dev)
    from_self = (blocks // vis_dev == myself).astype(jnp.int32)
    ranking = jnp.cumsum(from_self, axis=1) - 1
    slot_ids = jnp.arange(capacity)
    matched = (from_self[:, None, :] == 1) & (ranking[:, None, :] == slot_ids[None, :, None])
    local_rows = blocks - myself * vis_dev
    source_rows = jnp.sum(jnp.where(matched, local_rows[:, None, :], 0), axis=2)
    occupied = jnp.any(matched, axis=2)
    outgoing = jnp.where(
        occupied[..., None], jnp.take(projected, source_rows, axis=0), jnp.zeros((), jnp.bfloat16)
    )
    incoming = lax.all_to_all(outgoing, "tok", split_axis=0, concat_axis=0, tiled=True)
    own_owner = jnp.minimum(own_list // vis_dev, n_tok - 1)
    owner_marks = ((own_owner[:, None] == jnp.arange(n_tok)[None, :]) & visible[:, None]).astype(
        jnp.int32
    )
    owner_rank = jnp.cumsum(owner_marks, axis=0) - 1
    own_rank = jnp.take_along_axis(owner_rank, own_owner[:, None], axis=1)[:, 0]
    flat_index = own_owner * capacity + jnp.clip(own_rank, 0, capacity - 1)
    picked = jnp.take(incoming.reshape(n_tok * capacity, dec_width), flat_index, axis=0)
    dec_in = jnp.where(visible[:, None], picked, filler)
    head_dim = dec_width // HEADS
    dec_normed = layer_norm(dec_in.astype(jnp.float32)).astype(jnp.bfloat16)
    qkv = jnp.einsum(
        "pd,dchk->chkp",
        dec_normed,
        w_qkv.reshape(dec_width, 3, HEADS, head_dim),
        preferred_element_type=jnp.float32,
    ).astype(jnp.bfloat16)
    spread = lax.all_to_all(qkv, "tok", split_axis=1, concat_axis=3, tiled=True)
    attended = attend(spread[0], spread[1], spread[2])
    attended = lax.all_to_all(attended, "tok", split_axis=2, concat_axis=0, tiled=True)
    mixed = jnp.einsum(
        "hkp,hke->pe",
        attended,
        w_out.reshape(HEADS, head_dim, dec_width),
        preferred_element_type=jnp.float32,
    )
    return (mixed + dec_in.astype(jnp.float32)).astype(jnp.bfloat16)


def solution(mesh):
    placed = (
        P(("clip", "tok"), None),
        P(),
        P("tok", None, "clip"),
        P("tok", "clip", None),
        P(),
        P("clip", None),
        P(),
        P(),
        P(),
    )
    return jax.shard_map(
        per_device, mesh=mesh, in_specs=placed, out_specs=P(("clip", "tok"), None), check_vma=False
    )
```

profile of v0, /device:TPU:0, one launch (start us, length us, event | category | flops | bytes accessed | tf_op | source)
XLA Modules:
  0.0 278.5 jit_solution(15598185059574611517)
XLA Ops:
  6.5 1.6 convert_reduce_fusion.1
  8.1 1.6 fusion.10
  9.8 1.7 fusion.77
  11.6 23.1 %pmax.7 = f32[512]{0:T(512)S(1)} all-reduce(f32[512]{0:T(512)S(1)} %get-tuple-element.51), channel_id=1, replica_groups=mesh['clip'=4,'tok'=8] {'tok'}, use_global_device_ids=true, to_apply=%region_11.12 | all-reduce | flops 512 | bytes 4096 | tf_op jit(solution)/shard_map/pmax | solution.py:51
  34.7 3.4 %fusion.53 = f32[512,1024]{1,0:T(8,128)} fusion(f32[512,512]{1,0:T(8,128)} %get-tuple-element.75, f32[512]{0:T(512)S(1)} %pmax.7, bf16[512,1024]{1,0:T(8,128)(2,1)S(1)} %copy-done.1, f32[512]{0:T(512)S(1)} %add_rsqrt_fusion, f32[512]{0:T(512)S(1)} %broadcast_multiply_fusion), kind=kOutput, calls=%fused_computation.72 | convolution fusion | flops 539492352 | bytes 4200448 | tf_op jit(solution)/shard_map/dot_general | solution.py:53
  38.2 0.6 copy-done.6
  38.8 0.6 dynamic-slice.1
  40.0 0.4 fusion.32
  40.4 17.3 %all-reduce = f32[512]{0:T(512)S(1)} all-reduce(f32[512]{0:T(512)S(1)} %get-tuple-element.49), channel_id=3, replica_groups=mesh['clip'=4,'tok'=8] {'tok'}, use_global_device_ids=true, to_apply=%region_14.15.clone | all-reduce | flops 512 | bytes 4096
  57.7 0.1 dynamic-slice.2
  57.8 45.8 %reduce-scatter.3.cloned.1.call-done = f32[64,1024]{1,0:T(8,128)} async-done(((f32[512,1024]{1,0:T(8,128)}), f32[64,1024]{1,0:T(8,128)}) %reduce-scatter.3.cloned.1.call-update) | async-done | bytes 262160 | tf_op jit(solution)/shard_map/reduce_scatter | solution.py:58
  103.6 1.0 divide_convert_fusion.3
  104.6 7.1 %all_gather.6 = bf16[256,1024]{1,0:T(8,128)(2,1)S(1)} all-gather(bf16[64,1024]{1,0:T(8,128)(2,1)S(1)} %divide_convert_fusion.3), channel_id=1, replica_groups=mesh['clip'=4,'tok'=8] {'clip'}, dimensions={0}, use_global_device_ids=true | all-gather | bytes 655360 | tf_op jit(solution)/shard_map/all_gather | solution.py:66
  111.8 4.1 %fusion.12 = f32[256,1024]{1,0:T(8,128)} fusion(bf16[1,1024,1024]{2,1,0:T(8,128)(2,1)S(1)} %copy-done, bf16[256,1024]{1,0:T(8,128)(2,1)S(1)} %all_gather.6, bf16[1,1024,1024]{2,1,0:T(8,128)(2,1)} %param.13), kind=kOutput, calls=%fused_computation.21 | convolution fusion | flops 1076101120 | bytes 5767168 | tf_op jit(solution)/shard_map/dot_general | solution.py:71
  115.9 0.6 reduce-window.16
  116.5 0.2 slice_reduce_fusion
  116.8 0.5 broadcast.702
  117.3 0.7 reduce.7
  118.1 0.2 select_reduce_fusion
  118.3 0.1 reshape.428
  118.4 20.8 %reduce-scatter.5.cloned.1.call-done = f32[64,1024]{1,0:T(8,128)} async-done(((f32[256,1024]{1,0:T(8,128)}), f32[64,1024]{1,0:T(8,128)}) %reduce-scatter.5.cloned.1.call-update) | async-done | bytes 262160 | tf_op jit(solution)/shard_map/reduce_scatter | solution.py:72
  139.3 1.6 convert_element_type.103
  140.9 0.6 reduce-window.14
  141.5 0.2 slice_reduce_fusion.1
  141.9 1.8 gather_fusion.2
  143.8 0.2 fusion.52
  144.0 37.9 %all-gather.2.cloned.1.call-done = bf16[512,1024]{1,0:T(8,128)(2,1)} async-done(((bf16[64,1024]{1,0:T(8,128)(2,1)}), bf16[512,1024]{1,0:T(8,128)(2,1)}) %all-gather.2.cloned.1.call-update) | async-done | bytes 1048592 | tf_op jit(solution)/shard_map/all_gather | solution.py:80
  181.9 3.2 %convolution_convert_fusion.1 = bf16[512,512]{1,0:T(8,128)(2,1)S(1)} fusion(bf16[1024,512]{1,0:T(8,128)(2,1)} %param.15, bf16[512,1024]{1,0:T(8,128)(2,1)} %all-gather.2.cloned.1.call-done, f32[512,512]{1,0:T(8,128)} %get-tuple-element.75, f32[512]{0:T(512)S(1)} %get-tuple-element.48, f32[512]{0:T(512)S(1)} %get-tuple-element.50), kind=kOutput, calls=%fused_computation.27 | convolution fusion | flops 1075314688 | bytes 3674112 | tf_op jit(solution)/shard_map/dot_general | solution.py:83
  185.1 1.2 gather_fusion
  186.3 0.8 select_select_fusion
  187.1 3.4 %all-to-all-start = ((bf16[8,32,512]{2,1,0:T(8,128)(2,1)}), bf16[8,32,512]{2,1,0:T(8,128)(2,1)S(1)}, u32[]{:S(2)}, u32[]{:S(2)}) async-start(bf16[8,32,512]{2,1,0:T(8,128)(2,1)} %select_select_fusion), calls=%async_computation.2 | async-start | bytes 524288 | tf_op jit(solution)/shard_map/all_to_all | solution.py:107
  190.5 1.0 multiply_sine_fusion
  191.5 7.3 %all-to-all-done = bf16[8,32,512]{2,1,0:T(8,128)(2,1)S(1)} async-done(((bf16[8,32,512]{2,1,0:T(8,128)(2,1)}), bf16[8,32,512]{2,1,0:T(8,128)(2,1)S(1)}, u32[]{:S(2)}, u32[]{:S(2)}) %all-to-all-start) | async-done | bytes 262176 | tf_op jit(solution)/shard_map/all_to_all | solution.py:107
  198.8 1.2 gather_fusion.1
  199.9 0.2 convert_reduce_fusion.3
  200.2 0.2 fusion.35
  200.4 2.2 fusion.47
  202.7 0.1 convert_bitcast_fusion
  202.8 0.9 copy.39
  203.7 3.7 %all-to-all-start.1 = ((bf16[3,16,32,256]{3,2,0,1:T(8,128)(2,1)}), bf16[3,16,32,256]{3,2,0,1:T(8,128)(2,1)S(1)}, u32[]{:S(2)}, u32[]{:S(2)}) async-start(bf16[3,16,32,256]{3,2,0,1:T(8,128)(2,1)} %copy.39), calls=%async_computation.3 | async-start | bytes 1572864 | tf_op jit(solution)/shard_map/all_to_all | solution.py:125
  207.5 19.3 %all-to-all-done.1 = bf16[3,16,32,256]{3,2,0,1:T(8,128)(2,1)S(1)} async-done(((bf16[3,16,32,256]{3,2,0,1:T(8,128)(2,1)}), bf16[3,16,32,256]{3,2,0,1:T(8,128)(2,1)S(1)}, u32[]{:S(2)}, u32[]{:S(2)}) %all-to-all-start.1) | async-done | bytes 786464 | tf_op jit(solution)/shard_map/all_to_all | solution.py:125
  226.8 0.5 copy.52
  227.3 0.2 reshape_squeeze.10
  227.5 0.1 squeeze.20
  227.7 0.1 squeeze.21
  227.8 20.7 %while.10 = (s32[]{:T(128)}, bf16[4,2,32,512]{3,2,1,0:T(8,128)(2,1)}, bf16[4,2,32,512]{3,2,1,0:T(8,128)(2,1)S(1)}, bf16[2,32,2048]{2,1,0:T(8,128)(2,1)S(1)}, bf16[2,32,2048]{2,1,0:T(8,128)(2,1)S(1)}, /*index=5*/s32[]{:T(128)}) while((s32[]{:T(128)}, bf16[4,2,32,512]{3,2,1,0:T(8,128)(2,1)}, bf16[4,2,32,512]{3,2,1,0:T(8,128)(2,1)S(1)}, ...), condition=%wide.region_21.22_spmd, body=%wide.region_18.21_spmd.sunk | while | flops 289470464 | bytes 25842248 | solution.py:41
  227.8 1.4 multiply_reduce_fusion.2
  229.2 1.6 convert_reduce_fusion.5
  230.8 2.1 fusion.94
  233.0 1.4 multiply_reduce_fusion.2
  234.4 1.6 convert_reduce_fusion.5
  236.0 2.1 fusion.94
  238.2 1.4 multiply_reduce_fusion.2
  239.5 1.6 convert_reduce_fusion.5
  241.2 2.1 fusion.94
  243.3 1.4 multiply_reduce_fusion.2
  244.7 1.6 convert_reduce_fusion.5
  246.3 2.1 fusion.94
  248.5 2.2 copy.46
  250.7 1.7 reshape.467
  252.4 12.7 %all_to_all.38 = bf16[8,2,8192]{2,1,0:T(2,128)(2,1)} all-to-all(bf16[8,2,8192]{2,1,0:T(2,128)(2,1)} %reshape.467), channel_id=1, replica_groups=mesh['clip'=4,'tok'=8] {'tok'}, dimensions={0} | all-to-all | bytes 524288 | tf_op jit(solution)/shard_map/all_to_all | solution.py:127
  265.1 3.0 %reshape.468 = bf16[2048,2,32]{2,1,0:T(2,128)(2,1)S(1)} reshape(bf16[8,2,8192]{2,1,0:T(2,128)(2,1)} %all_to_all.38) | data formatting | bytes 524288
  268.1 1.7 copy.48
  269.8 2.1 fusion.17
  (52 shorter events, 0.7 us)
Async XLA Ops:
  6.5 105.2 %copy-start = (bf16[1,1024,1024]{2,1,0:T(8,128)(2,1)S(1)}, bf16[1,1024,1024]{2,1,0:T(8,128)(2,1)}, u32[]{:S(2)}) copy-start(bf16[1,1024,1024]{2,1,0:T(8,128)(2,1)} %param.14) | copy-start | bytes 6291460
  6.5 3.3 %copy-start.1 = (bf16[512,1024]{1,0:T(8,128)(2,1)S(1)}, bf16[512,1024]{1,0:T(8,128)(2,1)}, u32[]{:S(2)}) copy-start(bf16[512,1024]{1,0:T(8,128)(2,1)} %param.11) | copy-start | bytes 3145732
  6.5 97.0 %reduce-scatter.3.cloned.1.call-start = ((), (), s32[]{:S(2)}) async-start(), calls=%async_computation.5 | async-start | bytes 2359296 | tf_op jit(solution)/shard_map/reduce_scatter | solution.py:58
  6.5 3.3 %copy-start.5 = (bf16[1024,512]{1,0:T(8,128)(2,1)S(1)}, bf16[1024,512]{1,0:T(8,128)(2,1)}, u32[]{:S(2)}) copy-start(bf16[1024,512]{1,0:T(8,128)(2,1)} %param.12) | copy-start | bytes 3145732
  38.1 0.7 copy-start.6
  38.1 1.9 copy-start.2
  38.1 101.1 %reduce-scatter.5.cloned.1.call-start = ((), (), s32[]{:S(2)}) async-start(), calls=%async_computation.6 | async-start | bytes 1310720 | tf_op jit(solution)/shard_map/reduce_scatter | solution.py:72
  111.7 4.2 %copy-start.3 = (s32[1,2048]{1,0:T(1,128)S(1)}, s32[1,2048]{1,0:T(1,128)}, u32[]{:S(2)}) copy-start(s32[1,2048]{1,0:T(1,128)} %param.16) | copy-start | bytes 24580
  111.7 30.0 %copy-start.4 = (bf16[512]{0:T(512)(128)(2,1)S(1)}, bf16[512]{0:T(512)(128)(2,1)}, u32[]{:S(2)}) copy-start(bf16[512]{0:T(512)(128)(2,1)} %param.17) | copy-start | bytes 3076
  115.8 66.1 %all-gather.2.cloned.1.call-start = ((), (), s32[]{:S(2)}) async-start(), calls=%async_computation.7 | async-start | bytes 1179648 | tf_op jit(solution)/shard_map/all_gather | solution.py:80
  187.1 11.7 %all-to-all-start = ((bf16[8,32,512]{2,1,0:T(8,128)(2,1)}), bf16[8,32,512]{2,1,0:T(8,128)(2,1)S(1)}, u32[]{:S(2)}, u32[]{:S(2)}) async-start(bf16[8,32,512]{2,1,0:T(8,128)(2,1)} %select_select_fusion), calls=%async_computation.2 | async-start | bytes 524288 | tf_op jit(solution)/shard_map/all_to_all | solution.py:107
  203.7 23.1 %all-to-all-start.1 = ((bf16[3,16,32,256]{3,2,0,1:T(8,128)(2,1)}), bf16[3,16,32,256]{3,2,0,1:T(8,128)(2,1)S(1)}, u32[]{:S(2)}, u32[]{:S(2)}) async-start(bf16[3,16,32,256]{3,2,0,1:T(8,128)(2,1)} %copy.39), calls=%async_computation.3 | async-start | bytes 1572864 | tf_op jit(solution)/shard_map/all_to_all | solution.py:125
Sparse Core Ops, SparseCore 0:
  38.2 65.2 reduce-scatter.2
  116.0 23.2 reduce-scatter.4
  141.6 40.2 all-gather.1
where the time goes:
time: 279 us; the launch traced here: 278 us
  waiting for transfers between devices  131 us (47%)
  blocking collectives  60.3 us (22%)
  matrix products  30.9 us (11%)
  other arithmetic  17.9 us (6%)
  local copies, waits for them, and re-layouts  16.9 us (6%)
  between operations  14.1 us (5%)
  starting transfers between devices  7.22 us (3%)
    reduce_scatter x1, waiting for transfers between devices, per_device(): lax.psum_scatter(slot_sums, 'tok', scatter_dimension=0, tiled=True)  45.8 us
    all_gather x1, waiting for transfers between devices, per_device(): lax.all_gather(slot_out, 'tok', axis=0, tiled=True)  37.9 us
    pmax x1, blocking collectives, per_device(): col_top = lax.pmax(jnp.max(logits, axis=0), 'tok')  23.1 us
    reduce_scatter x1, waiting for transfers between devices, per_device(): lax.psum_scatter(partial_out, 'clip', scatter_dimension=0, tiled=True)  20.8 us
    all_to_all x1, waiting for transfers between devices, per_device(): spread = lax.all_to_all(qkv, 'tok', split_axis=1, concat_axis=3, tiled=True)  19.3 us
    unnamed x1, blocking collectives  17.3 us
    all_to_all x1, blocking collectives, per_device(): lax.all_to_all(attended, 'tok', split_axis=2, concat_axis=0, tiled=True)  12.7 us
    dot_general x4, matrix products, one_block(): jnp.einsum('hqn,hkn->hkq', raised, value_rows, preferred_element_type=jnp...  8.57 us
  transfers between devices with their start and end apart: 5, of which 5 were waited for; matrix products, arithmetic and copies ran while one was open for 3% of the time, Pallas kernels for 0%

commit v1 on v0

v1 whole, which is shorter than its diff:
```python
import math

import jax
import jax.numpy as jnp
from jax import lax
from jax.experimental import pallas as pl
from jax.experimental.pallas import tpu as pltpu
from jax.sharding import PartitionSpec as P

HEADS = 16
LANES = 128
F32 = jnp.float32
BF16 = jnp.bfloat16


def normalise(values):
    centre = values - jnp.mean(values, axis=-1, keepdims=True)
    spread = jnp.mean(centre * centre, axis=-1, keepdims=True)
    return centre * lax.rsqrt(spread + 1e-05)


def thirds(column):
    high = column.astype(BF16)
    rest = column - high.astype(F32)
    middle = rest.astype(BF16)
    low = (rest - middle.astype(F32)).astype(BF16)
    return high, middle, low


def front_kernel(tokens_ref, keys_ref, sums_ref, combine_ref):
    rows, width = tokens_ref.shape
    slots = keys_ref.shape[1]
    normed = normalise(tokens_ref[...].astype(F32)).astype(BF16)
    logits = jnp.dot(normed, keys_ref[...], preferred_element_type=F32)
    top = jnp.max(logits, axis=0, keepdims=True)
    dispatch = jnp.exp(logits - top).astype(BF16)
    turned = dispatch.T
    sums_ref[:, :width] = jnp.dot(turned, normed, preferred_element_type=F32).astype(BF16)
    totals = jnp.dot(turned, jnp.ones((rows, LANES), BF16), preferred_element_type=F32)
    tops = jnp.broadcast_to(top, (LANES, slots)).T
    lane = lax.broadcasted_iota(jnp.int32, (slots, LANES), 1)
    packed = jnp.zeros((slots, LANES), F32)
    for place, piece in enumerate(thirds(tops) + thirds(totals)):
        packed = jnp.where(lane == place, piece.astype(F32), packed)
    sums_ref[:, width:] = packed.astype(BF16)
    raised = jnp.exp(logits - jnp.max(logits, axis=1, keepdims=True))
    combine_ref[...] = (raised / jnp.sum(raised, axis=1, keepdims=True)).astype(BF16)


def front(tokens, slot_keys):
    rows, width = tokens.shape
    slots = slot_keys.shape[1]
    return pl.pallas_call(
        front_kernel,
        out_shape=(
            jax.ShapeDtypeStruct((slots, width + LANES), BF16),
            jax.ShapeDtypeStruct((rows, slots), BF16),
        ),
        compiler_params=pltpu.CompilerParams(vmem_limit_bytes=40 << 20),
    )(tokens, slot_keys)


def tail_kernel(place_ref, combine_ref, slot_ref, filler_ref, w_qkv_ref, w_out_ref, out_ref, k_ref, v_ref, a_ref):
    mine, width = out_ref.shape
    total = combine_ref.shape[0]
    head_dim = width // HEADS
    groups = width // LANES
    in_group = LANES // head_dim
    slot_rows = slot_ref[...]
    w_kv = w_qkv_ref[:, width:]

    def positions(block):
        rows = pl.ds(pl.multiple_of(block * mine, mine), mine)
        shown = jnp.dot(combine_ref[rows, :], slot_rows, preferred_element_type=F32).astype(BF16)
        dec_in = shown.astype(F32) + filler_ref[rows, :].astype(F32)
        return rows, dec_in, normalise(dec_in).astype(BF16)

    ones = jnp.ones((mine, LANES), BF16)

    @pl.loop(0, total // mine)
    def _(block):
        rows, _, normed = positions(block)
        kv = jnp.dot(normed, w_kv, preferred_element_type=F32).astype(BF16)
        for group in range(groups):
            k_ref[group, rows, :] = kv[:, group * LANES : (group + 1) * LANES]
            v_ref[group, rows, :LANES] = kv[:, width + group * LANES : width + (group + 1) * LANES]
            v_ref[group, rows, LANES:] = ones

    _, dec_in, normed = positions(place_ref[0])
    queries = jnp.dot(normed, w_qkv_ref[:, :width], preferred_element_type=F32).astype(BF16)
    for group in range(groups):
        a_ref[group] = queries[:, group * LANES : (group + 1) * LANES]
    head_of = lax.broadcasted_iota(jnp.int32, (mine, LANES), 1) // head_dim
    factor = math.log2(math.e) / math.sqrt(head_dim)

    @pl.loop(0, groups)
    def _(group):
        q_group = a_ref[group]
        result = jnp.zeros((mine, LANES), F32)
        for head in range(in_group):
            q_head = jnp.where(head_of == head, q_group, jnp.zeros_like(q_group))
            scores = lax.dot_general(
                q_head, k_ref[group], (((1,), (1,)), ((), ())), preferred_element_type=F32
            )
            highest = jnp.max(scores, axis=1, keepdims=True)
            raised = jnp.exp2((scores - highest) * factor).astype(BF16)
            both = jnp.dot(raised, v_ref[group], preferred_element_type=F32)
            result = jnp.where(head_of == head, both[:, :LANES] / both[:, LANES:], result)
        a_ref[group] = result.astype(BF16)

    attended = jnp.concatenate([a_ref[group] for group in range(groups)], axis=1)
    mixed = jnp.dot(attended, w_out_ref[...], preferred_element_type=F32)
    out_ref[...] = (mixed + dec_in).astype(BF16)


def tail(place, combine, slot_rows, filler, w_qkv, w_out, mine):
    total, width = filler.shape
    groups = width // LANES
    vmem = pl.BlockSpec(memory_space=pltpu.VMEM)
    return pl.pallas_call(
        tail_kernel,
        out_shape=jax.ShapeDtypeStruct((mine, width), BF16),
        in_specs=[pl.BlockSpec(memory_space=pltpu.SMEM)] + [vmem] * 5,
        out_specs=vmem,
        scratch_shapes=[
            pltpu.VMEM((groups, total, LANES), BF16),
            pltpu.VMEM((groups, total, 2 * LANES), BF16),
            pltpu.VMEM((groups, mine, LANES), BF16),
        ],
        compiler_params=pltpu.CompilerParams(vmem_limit_bytes=48 << 20),
    )(place, combine, slot_rows, filler, w_qkv, w_out)


def sinusoid_table(count, block, width):
    half = width // 2
    speeds = jnp.exp(-math.log(10000.0) * jnp.arange(half).astype(F32) / half)
    far = (jnp.arange(count // block) * block).astype(F32)[:, None] * speeds[None, :]
    near = jnp.arange(block).astype(F32)[:, None] * speeds[None, :]
    far_sin, far_cos = jnp.sin(far)[:, None, :], jnp.cos(far)[:, None, :]
    near_sin, near_cos = jnp.sin(near)[None], jnp.cos(near)[None]
    sines = far_sin * near_cos + far_cos * near_sin
    cosines = far_cos * near_cos - far_sin * near_sin
    return jnp.concatenate([sines, cosines], axis=2).reshape(count, width)


def unpack(stats):
    parts = stats[..., :6].astype(F32)
    top = parts[..., 0:1] + parts[..., 1:2] + parts[..., 2:3]
    total = parts[..., 3:4] + parts[..., 4:5] + parts[..., 5:6]
    return top, total


def per_device(tokens, slot_keys, w_in, w_back, w_proj, dec_source, mask_token, w_qkv, w_out):
    vis_dev, width = tokens.shape
    n_tok = lax.axis_size("tok")
    n_clip = lax.axis_size("clip")
    slots = slot_keys.shape[1]
    slots_e = slots // n_tok
    dec_width = w_proj.shape[1]
    listing = dec_source[0]
    dec_total = listing.shape[0]
    dec_dev = dec_total // n_tok
    vis_all = vis_dev * n_tok
    myself = lax.axis_index("tok")
    capacity = dec_dev // n_tok

    blocks = listing.reshape(n_tok, dec_dev)
    owners = blocks // vis_dev
    earlier = jnp.arange(dec_dev)[:, None] > jnp.arange(dec_dev)[None, :]
    same = (owners[:, :, None] == owners[:, None, :]) & earlier[None]
    ranks = jnp.sum(same.astype(jnp.int32), axis=2)
    visible = blocks < vis_all
    places = jnp.where(visible, owners * capacity + jnp.minimum(ranks, capacity - 1), -1)
    wanted = myself * capacity + jnp.arange(capacity)
    matched = places[:, None, :] == wanted[None, :, None]
    local = blocks - myself * vis_dev + 1
    source_rows = jnp.sum(jnp.where(matched, local[:, None, :], 0), axis=2) - 1
    picker = (source_rows.reshape(-1)[:, None] == jnp.arange(vis_dev)[None, :]).astype(BF16)
    placer = (places[:, :, None] == jnp.arange(dec_dev)[None, None, :]).astype(BF16)
    filler = jnp.where(
        visible.reshape(-1)[:, None],
        0.0,
        mask_token.astype(F32)[None, :] + sinusoid_table(dec_total, dec_dev, dec_width),
    ).astype(BF16)

    partial_sums, combine = front(tokens, slot_keys)
    outgoing = jnp.dot(picker, combine, preferred_element_type=F32).astype(BF16)
    spread = lax.all_gather(outgoing, "tok", axis=0)
    arrived = lax.all_to_all(
        partial_sums.reshape(n_tok, slots_e, width + LANES), "tok", split_axis=0, concat_axis=0, tiled=True
    )
    tops, totals = unpack(arrived[..., width:])
    scales = jnp.exp(tops - jnp.max(tops, axis=0, keepdims=True))
    slot_in = (
        jnp.sum(arrived[..., :width].astype(F32) * scales, axis=0) / jnp.sum(totals * scales, axis=0)
    ).astype(BF16)
    hidden = jax.nn.gelu(
        jnp.dot(
            lax.all_gather(slot_in, "clip", axis=0, tiled=True), w_in[0], preferred_element_type=F32
        )
    ).astype(BF16)
    partial_out = jnp.dot(hidden, w_back[0], preferred_element_type=F32).astype(BF16)
    partial_proj = jnp.dot(partial_out, w_proj, preferred_element_type=F32).astype(BF16)
    pieces = lax.all_to_all(
        partial_proj.reshape(n_clip, slots_e, dec_width), "clip", split_axis=0, concat_axis=0, tiled=True
    )
    slot_proj = jnp.sum(pieces.astype(F32), axis=0).astype(BF16)
    slot_rows = lax.all_to_all(
        jnp.broadcast_to(slot_proj[None], (n_tok, slots_e, dec_width)), "tok", split_axis=0, concat_axis=0, tiled=True
    ).reshape(slots, dec_width)
    by_block = spread.reshape(n_tok, n_tok, capacity, slots).transpose(1, 0, 2, 3)
    ordered = jnp.einsum(
        "bps,bsw->bpw", placer, by_block.reshape(n_tok, dec_dev, slots), preferred_element_type=F32
    ).astype(BF16)
    return tail(
        myself.reshape(1).astype(jnp.int32), ordered.reshape(dec_total, slots), slot_rows, filler, w_qkv, w_out, dec_dev
    )


def solution(mesh):
    placed = (
        P(("clip", "tok"), None),
        P(),
        P("tok", None, "clip"),
        P("tok", "clip", None),
        P(),
        P("clip", None),
        P(),
        P(),
        P(),
    )
    return jax.shard_map(
        per_device, mesh=mesh, in_specs=placed, out_specs=P(("clip", "tok"), None), check_vma=False
    )
```

time: 279 us -> 133 us (0.48)
  waiting for transfers between devices: 131 us -> 43 us
  blocking collectives: 60.3 us -> 7.18 us
  Pallas kernels: 0 us -> 26.5 us
  matrix products: 30.9 us -> 7.62 us
  other arithmetic: 17.9 us -> 10.6 us
  starting transfers between devices: 7.22 us -> 14.5 us
  local copies, waits for them, and re-layouts: 16.9 us -> 9.97 us
    reduce_scatter x2 -> x0, waiting for transfers between devices: 66.6 us -> none  [the longest x1 45.8 us: per_device(): lax.psum_scatter(slot_sums, 'tok', scatter_dimension=0, tiled=True)]
    all_gather x1, waiting for transfers between devices: 37.9 us -> 0.01 us  [per_device(): spread = lax.all_gather(outgoing, 'tok', axis=0)]
    pallas_call x0 -> x2, Pallas kernels: none -> 26.5 us  [the longest x1 23 us: tail(): pl.pallas_call(tail_kernel, out_shape=jax.ShapeDtypeStruct((mine, width),...]
    pmax x1 -> x0, blocking collectives: 23.1 us -> none  [per_device(): col_top = lax.pmax(jnp.max(logits, axis=0), 'tok')]
    dot_general x13 -> x4, matrix products: 28.7 us -> 7.62 us  [the longest x1 3.6 us: per_device(): jnp.dot(partial_out, w_proj, preferred_element_type=F32).astype(BF16)]
    unnamed x1 -> x0, blocking collectives: 17.3 us -> none
    all_to_all x2 -> x3, waiting for transfers between devices: 26.6 us -> 42.9 us  [the longest x1 32.4 us: per_device(): lax.all_to_all(partial_sums.reshape(n_tok, slots_e, width + LANES), 'tok'...]
    all_to_all x1 -> x0, blocking collectives: 12.7 us -> none  [per_device(): lax.all_to_all(attended, 'tok', split_axis=2, concat_axis=0, tiled=True)]
  transfers between devices with their start and end apart: 5 -> 4, of which waited for: 5 -> 3; matrix products, arithmetic and copies ran while one was open for 3% -> 17% of each run, Pallas kernels for 0% -> 0%
where the time goes in v1:
time: 133 us
  waiting for transfers between devices  43 us (32%)
  Pallas kernels  26.5 us (20%)
  starting transfers between devices  14.5 us (11%)
  between operations  13.6 us (10%)
  other arithmetic  10.6 us (8%)
  local copies, waits for them, and re-layouts  9.97 us (7%)
  matrix products  7.62 us (6%)
  blocking collectives  7.18 us (5%)
    all_to_all x1, waiting for transfers between devices, per_device(): lax.all_to_all(partial_sums.reshape(n_tok, slots_e, width + LANES), 'tok'...  32.4 us
    pallas_call x1, Pallas kernels, tail(): pl.pallas_call(tail_kernel, out_shape=jax.ShapeDtypeStruct((mine, width),...  23 us
    all_to_all x1, starting transfers between devices, per_device(): lax.all_to_all(partial_sums.reshape(n_tok, slots_e, width + LANES), 'tok'...  7.42 us
    all_gather x1, blocking collectives, per_device(): lax.all_gather(slot_in, 'clip', axis=0, tiled=True)  7.18 us
    all_to_all x1, waiting for transfers between devices, per_device(): lax.all_to_all(jnp.broadcast_to(slot_proj[None], (n_tok, slots_e, dec_wid...  7.06 us
    unnamed x18, local copies, waits for them, and re-layouts  6.26 us
    all_to_all x1, starting transfers between devices, per_device(): lax.all_to_all(jnp.broadcast_to(slot_proj[None], (n_tok, slots_e, dec_wid...  3.67 us
    dot_general x1, matrix products, per_device(): jnp.dot(partial_out, w_proj, preferred_element_type=F32).astype(BF16)  3.6 us
  transfers between devices with their start and end apart: 4, of which 3 were waited for; matrix products, arithmetic and copies ran while one was open for 17% of the time, Pallas kernels for 0%

profile of v1, /device:TPU:0, one launch (start us, length us, event | category | flops | bytes accessed | tf_op | source)
XLA Modules:
  0.0 132.9 jit_solution(2048896497051336398)
XLA Ops:
  6.5 0.0 copy-start
  6.5 0.0 copy-start.3
  6.5 1.4 %copy-done.3 = bf16[512,1024]{1,0:T(8,128)(2,1)S(1)} copy-done((bf16[512,1024]{1,0:T(8,128)(2,1)S(1)}, bf16[512,1024]{1,0:T(8,128)(2,1)}, u32[]{:S(2)}) %copy-start.3) | copy-done | bytes 1048600
  7.9 0.0 copy-start.4
  7.9 1.2 copy-done.4
  9.1 0.0 copy-start.6
  9.1 3.4 %shard_map.91 = (bf16[512,1152]{1,0:T(8,128)(2,1)}, bf16[512,512]{1,0:T(8,128)(2,1)S(1)}) custom-call(bf16[512,1024]{1,0:T(8,128)(2,1)S(1)} %copy-done.3, bf16[1024,512]{1,0:T(8,128)(2,1)S(1)} %copy-done.4), custom_call_target="tpu_custom_call" | custom-call | tf_op jit(solution)/shard_map/pallas_call | solution.py:53
  12.6 0.0 copy-start.7
  12.6 7.4 %all-to-all-start = ((bf16[8,64,1152]{2,1,0:T(8,128)(2,1)}), bf16[8,64,1152]{2,1,0:T(8,128)(2,1)}, u32[]{:S(2)}, u32[]{:S(2)}) async-start(bf16[8,64,1152]{2,1,0:T(8,128)(2,1)} %bitcast.5), calls=%async_computation | async-start | bytes 2359296 | tf_op jit(solution)/shard_map/all_to_all | solution.py:189
  20.0 0.0 all-gather.3.cloned.1.call-start
  20.1 0.5 broadcast.269
  20.6 0.0 copy-done.6
  20.6 0.7 reduce.8
  21.3 0.8 convert_reduce_fusion
  22.1 0.3 select_reduce_fusion
  22.4 0.1 sub.41
  22.5 1.1 convolution_convert_fusion.1
  23.5 0.0 all-gather.3.cloned.1.call-update
  23.6 0.0 copy-done.7
  23.6 0.1 multiply_sine_fusion.1
  23.7 1.0 multiply_cosine_fusion
  24.7 32.4 %all-to-all-done = bf16[8,64,1152]{2,1,0:T(8,128)(2,1)} async-done(((bf16[8,64,1152]{2,1,0:T(8,128)(2,1)}), bf16[8,64,1152]{2,1,0:T(8,128)(2,1)}, u32[]{:S(2)}, u32[]{:S(2)}) %all-to-all-start) | async-done | bytes 1179680 | tf_op jit(solution)/shard_map/all_to_all | solution.py:189
  57.1 0.9 slice.35
  58.1 0.1 copy.29
  58.3 1.5 %multiply_reduce_fusion = f32[64,1024]{1,0:T(8,128)S(1)} fusion(bf16[8,64,1152]{2,1,0:T(8,128)(2,1)} %all-to-all-done, f32[8,64]{1,0:T(8,128)S(1)} %get-tuple-element.16), kind=kLoop, calls=%fused_computation.9 | loop fusion | flops 1507328 | bytes 1312768 | tf_op jit(solution)/shard_map/reduce_sum | solution.py:195
  59.8 0.1 divide_convert_fusion
  59.9 7.2 %all_gather.11 = bf16[256,1024]{1,0:T(8,128)(2,1)S(1)} all-gather(bf16[64,1024]{1,0:T(8,128)(2,1)S(1)} %divide_convert_fusion), channel_id=1, replica_groups=mesh['clip'=4,'tok'=8] {'clip'}, dimensions={0}, use_global_device_ids=true | all-gather | bytes 655360 | tf_op jit(solution)/shard_map/all_gather | solution.py:199
  67.1 0.0 copy-done
  67.1 0.9 fusion.22
  68.0 3.6 %convolution_convert_fusion = bf16[256,512]{1,0:T(8,128)(2,1)} fusion(bf16[1024,512]{1,0:T(8,128)(2,1)} %param.13, bf16[256,1024]{1,0:T(8,128)(2,1)S(1)} %fusion.22, bf16[1,1024,1024]{2,1,0:T(8,128)(2,1)} %param.12), kind=kOutput, calls=%fused_computation.16 | convolution fusion | flops 805699584 | bytes 3932160 | tf_op jit(solution)/shard_map/dot_general | solution.py:203
  71.6 3.4 %all-to-all-start.1 = ((bf16[4,64,512]{2,1,0:T(8,128)(2,1)}), bf16[4,64,512]{2,1,0:T(8,128)(2,1)S(1)}, u32[]{:S(2)}, u32[]{:S(2)}) async-start(bf16[4,64,512]{2,1,0:T(8,128)(2,1)} %bitcast.9), calls=%async_computation.1 | async-start | bytes 524288 | tf_op jit(solution)/shard_map/all_to_all | solution.py:204
  75.0 2.5 %multiply_add_fusion = (f32[8,256,256]{2,1,0:T(8,128)}, f32[8,256,256]{2,1,0:T(8,128)}) fusion(f32[256,256]{1,0:T(8,128)S(1)} %get-tuple-element.18, f32[8,256]{1,0:T(8,128)S(1)} %get-tuple-element.20, f32[256,256]{1,0:T(8,128)S(1)} %get-tuple-element.17, f32[8,256]{1,0:T(8,128)S(1)} %get-tuple-element.19), kind=kLoop, calls=%fused_computation.8 | loop fusion | flops 3145728 | bytes 4734976 | tf_op jit(solution)/shard_map/add | solution.py:141
  77.5 3.5 %all-to-all-done.1 = bf16[4,64,512]{2,1,0:T(8,128)(2,1)S(1)} async-done(((bf16[4,64,512]{2,1,0:T(8,128)(2,1)}), bf16[4,64,512]{2,1,0:T(8,128)(2,1)S(1)}, u32[]{:S(2)}, u32[]{:S(2)}) %all-to-all-start.1) | async-done | bytes 262176 | tf_op jit(solution)/shard_map/all_to_all | solution.py:204
  81.0 0.9 broadcast_in_dim.26
  81.9 3.7 %all-to-all-start.2 = ((bf16[8,64,512]{2,1,0:T(8,128)(2,1)}), bf16[8,64,512]{2,1,0:T(8,128)(2,1)S(1)}, u32[]{:S(2)}, u32[]{:S(2)}) async-start(bf16[8,64,512]{2,1,0:T(8,128)(2,1)} %broadcast_in_dim.26), calls=%async_computation.2 | async-start | bytes 1048576 | tf_op jit(solution)/shard_map/all_to_all | solution.py:208
  85.7 3.4 %fusion.1.filler_ref = bf16[2048,512]{1,0:T(8,128)(2,1)} fusion(f32[2048,256]{1,0:T(8,128)} %bitcast.36, f32[2048,256]{1,0:T(8,128)} %bitcast.35, f32[512]{0:T(512)S(1)} %convert_element_type.69, pred[2048]{0:T(1024)(128)(4,1)S(1)} %compare_reduce_fusion), kind=kLoop, calls=%fused_computation.2 | loop fusion | flops 4194304 | bytes 6295552 | tf_op jit(solution)/shard_map/convert_element_type | solution.py:184
  89.1 0.0 all-gather.3.cloned.1.call-done
  89.1 1.8 %copy.24 = bf16[8,8,32,512]{3,2,1,0:T(8,128)(2,1)S(1)} copy(bf16[8,8,32,512]{3,2,0,1:T(8,128)(2,1)} %bitcast.37) | data formatting | bytes 4194304 | tf_op jit(solution)/shard_map/transpose | solution.py:211
  90.9 0.0 copy-start.5
  90.9 2.0 %fusion.7 = bf16[8,256,512]{2,1,0:T(8,128)(2,1)} fusion(bf16[8,256,512]{2,1,0:T(8,128)(2,1)S(1)} %bitcast.34, s32[8,256]{1,0:T(8,128)S(1)} %get-tuple-element.13), kind=kOutput, calls=%fused_computation.13 | convolution fusion | flops 538443776 | bytes 4202496 | tf_op jit(solution)/shard_map/bps,bsw->bpw/dot_general | solution.py:212
  93.0 7.1 %all-to-all-done.2 = bf16[8,64,512]{2,1,0:T(8,128)(2,1)S(1)} async-done(((bf16[8,64,512]{2,1,0:T(8,128)(2,1)}), bf16[8,64,512]{2,1,0:T(8,128)(2,1)S(1)}, u32[]{:S(2)}, u32[]{:S(2)}) %all-to-all-start.2) | async-done | bytes 524320 | tf_op jit(solution)/shard_map/all_to_all | solution.py:208
  100.0 0.0 copy-done.5
  100.0 0.0 copy-start.1
  100.0 1.6 %copy-done.1 = bf16[8,256,512]{2,1,0:T(8,128)(2,1)S(1)} copy-done((bf16[8,256,512]{2,1,0:T(8,128)(2,1)S(1)}, bf16[8,256,512]{2,1,0:T(8,128)(2,1)}, u32[]{:S(2)}) %copy-start.1) | copy-done | bytes 2097176
  101.6 0.0 copy-start.2
  101.6 1.4 %copy-done.2 = bf16[512,1536]{1,0:T(8,128)(2,1)S(1)} copy-done((bf16[512,1536]{1,0:T(8,128)(2,1)S(1)}, bf16[512,1536]{1,0:T(8,128)(2,1)}, u32[]{:S(2)}) %copy-start.2) | copy-done | bytes 1572888
  103.0 23.0 %shard_map.92 = bf16[256,512]{1,0:T(8,128)(2,1)} custom-call(s32[1]{0:T(128)} %bitcast.place_ref, bf16[2048,512]{1,0:T(8,128)(2,1)S(1)} %bitcast.32, bf16[512,512]{1,0:T(8,128)(2,1)S(1)} %bitcast.33, bf16[2048,512]{1,0:T(8,128)(2,1)} %fusion.1.filler_ref, bf16[512,1536]{1,0:T(8,128)(2,1)S(1)} %copy-done.2, bf16[512,512]{1,0:T(8,128)(2,1)S(1)} %copy-done.5), custom_call_target="tpu_custom_call" | custom-call | tf_op jit(solution)/shard_map/pallas_call | solution.py:120
  (15 shorter events, 0.2 us)
Async XLA Ops:
  6.5 60.5 %copy-start = (bf16[1,1024,1024]{2,1,0:T(8,128)(2,1)S(1)}, bf16[1,1024,1024]{2,1,0:T(8,128)(2,1)}, u32[]{:S(2)}) copy-start(bf16[1,1024,1024]{2,1,0:T(8,128)(2,1)} %param.11) | copy-start | bytes 6291460
  6.5 1.4 %copy-start.3 = (bf16[512,1024]{1,0:T(8,128)(2,1)S(1)}, bf16[512,1024]{1,0:T(8,128)(2,1)}, u32[]{:S(2)}) copy-start(bf16[512,1024]{1,0:T(8,128)(2,1)} %tokens_ref.1) | copy-start | bytes 3145732
  7.9 1.2 copy-start.4
  9.1 11.4 %copy-start.6 = (s32[1,2048]{1,0:T(1,128)S(1)}, s32[1,2048]{1,0:T(1,128)}, u32[]{:S(2)}) copy-start(s32[1,2048]{1,0:T(1,128)} %param.14) | copy-start | bytes 24580
  12.6 11.0 %copy-start.7 = (bf16[512]{0:T(512)(128)(2,1)S(1)}, bf16[512]{0:T(512)(128)(2,1)}, u32[]{:S(2)}) copy-start(bf16[512]{0:T(512)(128)(2,1)} %param.15) | copy-start | bytes 3076
  12.6 44.6 %all-to-all-start = ((bf16[8,64,1152]{2,1,0:T(8,128)(2,1)}), bf16[8,64,1152]{2,1,0:T(8,128)(2,1)}, u32[]{:S(2)}, u32[]{:S(2)}) async-start(bf16[8,64,1152]{2,1,0:T(8,128)(2,1)} %bitcast.5), calls=%async_computation | async-start | bytes 2359296 | tf_op jit(solution)/shard_map/all_to_all | solution.py:189
  20.0 69.1 %all-gather.3.cloned.1.call-start = ((), (), s32[]{:S(2)}) async-start(), calls=%async_computation.3 | async-start | bytes 2359296 | tf_op jit(solution)/shard_map/all_gather | solution.py:188
  71.6 9.4 %all-to-all-start.1 = ((bf16[4,64,512]{2,1,0:T(8,128)(2,1)}), bf16[4,64,512]{2,1,0:T(8,128)(2,1)S(1)}, u32[]{:S(2)}, u32[]{:S(2)}) async-start(bf16[4,64,512]{2,1,0:T(8,128)(2,1)} %bitcast.9), calls=%async_computation.1 | async-start | bytes 524288 | tf_op jit(solution)/shard_map/all_to_all | solution.py:204
  81.9 18.1 %all-to-all-start.2 = ((bf16[8,64,512]{2,1,0:T(8,128)(2,1)}), bf16[8,64,512]{2,1,0:T(8,128)(2,1)S(1)}, u32[]{:S(2)}, u32[]{:S(2)}) async-start(bf16[8,64,512]{2,1,0:T(8,128)(2,1)} %broadcast_in_dim.26), calls=%async_computation.2 | async-start | bytes 1048576 | tf_op jit(solution)/shard_map/all_to_all | solution.py:208
  90.9 9.1 %copy-start.5 = (bf16[512,512]{1,0:T(8,128)(2,1)S(1)}, bf16[512,512]{1,0:T(8,128)(2,1)}, u32[]{:S(2)}) copy-start(bf16[512,512]{1,0:T(8,128)(2,1)} %w_out_ref.1) | copy-start | bytes 1572868
  100.0 1.6 %copy-start.1 = (bf16[8,256,512]{2,1,0:T(8,128)(2,1)S(1)}, bf16[8,256,512]{2,1,0:T(8,128)(2,1)}, u32[]{:S(2)}) copy-start(bf16[8,256,512]{2,1,0:T(8,128)(2,1)} %fusion.7) | copy-start | bytes 6291460
  101.6 1.4 %copy-start.2 = (bf16[512,1536]{1,0:T(8,128)(2,1)S(1)}, bf16[512,1536]{1,0:T(8,128)(2,1)}, u32[]{:S(2)}) copy-start(bf16[512,1536]{1,0:T(8,128)(2,1)} %w_qkv_ref.1) | copy-start | bytes 4718596
Sparse Core Ops, SparseCore 0:
  23.7 59.3 all-gather.2

commit v2 on v1

v2 whole, which is shorter than its diff:
```python
import math

import jax
import jax.numpy as jnp
from jax import lax
from jax.experimental import pallas as pl
from jax.experimental.pallas import tpu as pltpu
from jax.sharding import PartitionSpec as P

HEADS = 16
LANES = 128
F32 = jnp.float32
BF16 = jnp.bfloat16
VMEM = pl.BlockSpec(memory_space=pltpu.VMEM)
SMEM = pl.BlockSpec(memory_space=pltpu.SMEM)
HBM = pl.BlockSpec(memory_space=pltpu.HBM)


def normalise(values):
    centre = values - jnp.mean(values, axis=-1, keepdims=True)
    spread = jnp.mean(centre * centre, axis=-1, keepdims=True)
    return centre * lax.rsqrt(spread + 1e-05)


def thirds(column):
    high = column.astype(BF16)
    rest = column - high.astype(F32)
    middle = rest.astype(BF16)
    low = (rest - middle.astype(F32)).astype(BF16)
    return high, middle, low


def pack(tops, totals):
    rows = max(tops.shape[0], totals.shape[0])
    lane = lax.broadcasted_iota(jnp.int32, (rows, LANES), 1)
    packed = jnp.zeros((rows, LANES), F32)
    for place, piece in enumerate(thirds(tops) + thirds(totals)):
        packed = jnp.where(lane == place, piece.astype(F32), packed)
    return packed.astype(BF16)


def unpack(stats):
    parts = stats.astype(F32)
    top = parts[:, 0:1] + parts[:, 1:2] + parts[:, 2:3]
    total = parts[:, 3:4] + parts[:, 4:5] + parts[:, 5:6]
    return top, total


def swap(values, axis, mask):
    count = lax.axis_size(axis)
    return lax.ppermute(values, axis, [(index, index ^ mask) for index in range(count)])


def bit_orders(count):
    bits = list(range(count.bit_length() - 1))
    first = bits[1:2] + bits[0:1] + bits[2:]
    second = bits
    return first, second


def ranks_of(order):
    steps = len(order)
    return [
        sum(((place >> (steps - 1 - step)) & 1) << bit for step, bit in enumerate(order))
        for place in range(1 << steps)
    ]


def gather_bits(values, axis, order):
    pieces = [values]
    for bit in order:
        held = pieces[0] if len(pieces) == 1 else jnp.concatenate(pieces, axis=0)
        pieces.append(swap(held, axis, 1 << bit))
    return pieces


def gathered_ranks(order):
    held = [0]
    for bit in order:
        held = held + [index ^ (1 << bit) for index in held]
    return held


def front_kernel(orders, place_ref, tokens_hbm, keys_hbm, *refs):
    outs, combine_ref = refs[:4], refs[4]
    tokens_ref, keys_ref, turned_ref, tops_ref, picked_ref, picked_tops_ref, sems = refs[5:]
    rows, width = tokens_ref.shape
    slots = keys_ref.shape[1]
    pieces = sems.shape[1]
    token_step, key_step = rows // pieces, width // pieces
    copies = []
    for piece in range(pieces):
        part = pl.ds(piece * token_step, token_step)
        copies.append(pltpu.make_async_copy(tokens_hbm.at[part], tokens_ref.at[part], sems.at[0, piece]))
    for piece in range(pieces):
        part = pl.ds(piece * key_step, key_step)
        copies.append(pltpu.make_async_copy(keys_hbm.at[part], keys_ref.at[part], sems.at[1, piece]))
    for copy in copies:
        copy.start()
    parts = []
    for piece in range(pieces):
        copies[piece].wait()
        part = tokens_ref[piece * token_step : (piece + 1) * token_step, :].astype(F32)
        parts.append(normalise(part).astype(BF16))
    normed = jnp.concatenate(parts, axis=0)
    for copy in copies[pieces:]:
        copy.wait()
    logits = jnp.dot(normed, keys_ref[...], preferred_element_type=F32)
    top = jnp.max(logits, axis=0, keepdims=True)
    turned_ref[...] = jnp.exp(logits - top).astype(BF16).T
    tops_ref[...] = jnp.broadcast_to(top, (LANES, slots)).T
    myself = place_ref[0]
    count = 1 << len(orders[0])
    block = slots // count
    half = block // 2
    for path, order in enumerate(orders):
        for place, relative in enumerate(ranks_of(order)):
            source = pl.ds(pl.multiple_of((myself ^ relative) * block + path * half, half), half)
            target = pl.ds((path * count + place) * half, half)
            picked_ref[target, :] = turned_ref[source, :]
            picked_tops_ref[target, :] = tops_ref[source, :]
    picked = picked_ref[...]
    sums = jnp.dot(picked, normed, preferred_element_type=F32).astype(BF16)
    totals = jnp.dot(picked, jnp.ones((rows, LANES), BF16), preferred_element_type=F32)
    stats = pack(picked_tops_ref[...], totals)
    quarter = slots // 4
    for index, out_ref in enumerate(outs):
        out_ref[:, :width] = sums[index * quarter : (index + 1) * quarter, :]
        out_ref[:, width:] = stats[index * quarter : (index + 1) * quarter, :]
    raised = jnp.exp(logits - jnp.max(logits, axis=1, keepdims=True))
    combine_ref[...] = (raised / jnp.sum(raised, axis=1, keepdims=True)).astype(BF16)


def front(place, tokens, slot_keys, orders):
    rows, width = tokens.shape
    slots = slot_keys.shape[1]
    quarter = jax.ShapeDtypeStruct((slots // 4, width + LANES), BF16)
    pieces = 4
    return pl.pallas_call(
        lambda *refs: front_kernel(orders, *refs),
        out_shape=(quarter,) * 4 + (jax.ShapeDtypeStruct((rows, slots), BF16),),
        in_specs=[SMEM, HBM, HBM],
        out_specs=(VMEM,) * 5,
        scratch_shapes=[
            pltpu.VMEM((rows, width), BF16),
            pltpu.VMEM((width, slots), BF16),
            pltpu.VMEM((slots, rows), BF16),
            pltpu.VMEM((slots, LANES), F32),
            pltpu.VMEM((slots, rows), BF16),
            pltpu.VMEM((slots, LANES), F32),
            pltpu.SemaphoreType.DMA((2, pieces)),
        ],
        compiler_params=pltpu.CompilerParams(vmem_limit_bytes=28 << 20),
    )(place, tokens, slot_keys)


def merge_kernel(kept_ref, came_ref, *outs):
    width = kept_ref.shape[1] - LANES
    kept_top, kept_total = unpack(kept_ref[:, width:])
    came_top, came_total = unpack(came_ref[:, width:])
    top = jnp.maximum(kept_top, came_top)
    kept_scale, came_scale = jnp.exp(kept_top - top), jnp.exp(came_top - top)
    total = kept_total * kept_scale + came_total * came_scale
    sums = kept_ref[:, :width].astype(F32) * kept_scale + came_ref[:, :width].astype(F32) * came_scale
    if len(outs) == 1:
        outs[0][...] = (sums / total).astype(BF16)
        return
    sums = sums.astype(BF16)
    stats = pack(top, total)
    half = kept_ref.shape[0] // 2
    for index, out_ref in enumerate(outs):
        out_ref[:, :width] = sums[index * half : (index + 1) * half, :]
        out_ref[:, width:] = stats[index * half : (index + 1) * half, :]


def merge(kept, came, last):
    rows, columns = kept.shape
    if last:
        shape, specs = jax.ShapeDtypeStruct((rows, columns - LANES), BF16), VMEM
    else:
        shape, specs = (jax.ShapeDtypeStruct((rows // 2, columns), BF16),) * 2, (VMEM, VMEM)
    return pl.pallas_call(
        merge_kernel,
        out_shape=shape,
        in_specs=[VMEM, VMEM],
        out_specs=specs,
        compiler_params=pltpu.CompilerParams(vmem_limit_bytes=12 << 20),
    )(kept, came)


def experts_kernel(count, *refs):
    rows_refs, (in_a, in_b, back_a, back_b, proj_ref), outs = refs[:count], refs[count : count + 5], refs[count + 5 :]
    rows = jnp.concatenate([ref[...] for ref in rows_refs], axis=0)
    total = None
    for first_ref, second_ref in ((in_a, back_a), (in_b, back_b)):
        hidden = jax.nn.gelu(jnp.dot(rows, first_ref[...], preferred_element_type=F32)).astype(BF16)
        part = jnp.dot(hidden, second_ref[...], preferred_element_type=F32)
        total = part if total is None else total + part
    result = jnp.dot(total.astype(BF16), proj_ref[...], preferred_element_type=F32).astype(BF16)
    step = rows_refs[0].shape[0]
    for index, out_ref in enumerate(outs):
        out_ref[...] = result[index * step : (index + 1) * step, :]


def experts(slot_rows, first, first_other, second, second_other, w_proj):
    count = len(slot_rows)
    rows = slot_rows[0].shape[0]
    return pl.pallas_call(
        lambda *refs: experts_kernel(count, *refs),
        out_shape=(jax.ShapeDtypeStruct((rows, w_proj.shape[1]), BF16),) * count,
        in_specs=[VMEM] * (count + 5),
        out_specs=(VMEM,) * count,
        compiler_params=pltpu.CompilerParams(vmem_limit_bytes=24 << 20),
    )(*slot_rows, first, first_other, second, second_other, w_proj)


def order_kernel(ranks, first_count, places_ref, *refs):
    pieces, out_ref = refs[:-1], refs[-1]
    halves = (pieces[:first_count], pieces[first_count:])
    total, slots = out_ref.shape
    count = len(ranks[0])
    block = total // count
    capacity = block // count
    column = lax.broadcasted_iota(jnp.int32, (block, block), 1)
    for target in range(count):
        path, inner = divmod(target, count // 2)
        rows = [None] * count
        place = 0
        for ref in halves[path]:
            for index in range(ref.shape[0] // (block // 2)):
                start = index * (block // 2) + inner * capacity
                rows[ranks[path][place]] = ref[start : start + capacity, :]
                place += 1
        chosen = (places_ref[target * block : (target + 1) * block, :] == column).astype(BF16)
        out_ref[target * block : (target + 1) * block, :] = jnp.dot(
            chosen, jnp.concatenate(rows, axis=0), preferred_element_type=F32
        ).astype(BF16)


def put_in_order(places, first, second, ranks):
    total, slots = places.shape[0], first[0].shape[1]
    return pl.pallas_call(
        lambda *refs: order_kernel(ranks, len(first), *refs),
        out_shape=jax.ShapeDtypeStruct((total, slots), BF16),
        in_specs=[VMEM] * (1 + len(first) + len(second)),
        out_specs=VMEM,
        compiler_params=pltpu.CompilerParams(vmem_limit_bytes=24 << 20),
    )(places, *first, *second)


def tail_kernel(
    ranks, first_count, place_ref, combine_ref, filler_ref, w_qkv_ref, w_out_ref, *refs
):
    pieces = refs[:-5]
    out_ref, slot_ref, k_ref, v_ref, a_ref = refs[-5:]
    mine, width = out_ref.shape
    total = combine_ref.shape[0]
    head_dim = width // HEADS
    groups = width // LANES
    in_group = LANES // head_dim
    myself = place_ref[0]
    half = pieces[0].shape[0]
    for path, refs_here in enumerate((pieces[:first_count], pieces[first_count:])):
        place = 0
        for ref in refs_here:
            for index in range(ref.shape[0] // half):
                target = pl.multiple_of((myself ^ ranks[path][place]) * (2 * half) + path * half, half)
                slot_ref[pl.ds(target, half), :] = ref[index * half : (index + 1) * half, :]
                place += 1
    slot_rows = slot_ref[...]
    w_kv = w_qkv_ref[:, width:]

    def positions(block):
        rows = pl.ds(pl.multiple_of(block * mine, mine), mine)
        shown = jnp.dot(combine_ref[rows, :], slot_rows, preferred_element_type=F32).astype(BF16)
        dec_in = shown.astype(F32) + filler_ref[rows, :].astype(F32)
        return rows, dec_in, normalise(dec_in).astype(BF16)

    ones = jnp.ones((mine, LANES), BF16)

    @pl.loop(0, total // mine)
    def _(block):
        rows, _, normed = positions(block)
        kv = jnp.dot(normed, w_kv, preferred_element_type=F32).astype(BF16)
        for group in range(groups):
            k_ref[group, rows, :] = kv[:, group * LANES : (group + 1) * LANES]
            v_ref[group, rows, :LANES] = kv[:, width + group * LANES : width + (group + 1) * LANES]
            v_ref[group, rows, LANES:] = ones

    _, dec_in, normed = positions(myself)
    queries = jnp.dot(normed, w_qkv_ref[:, :width], preferred_element_type=F32).astype(BF16)
    for group in range(groups):
        a_ref[group] = queries[:, group * LANES : (group + 1) * LANES]
    head_of = lax.broadcasted_iota(jnp.int32, (mine, LANES), 1) // head_dim
    factor = math.log2(math.e) / math.sqrt(head_dim)

    @pl.loop(0, groups)
    def _(group):
        q_group = a_ref[group]
        result = jnp.zeros((mine, LANES), F32)
        for head in range(in_group):
            q_head = jnp.where(head_of == head, q_group, jnp.zeros_like(q_group))
            scores = lax.dot_general(
                q_head, k_ref[group], (((1,), (1,)), ((), ())), preferred_element_type=F32
            )
            highest = jnp.max(scores, axis=1, keepdims=True)
            raised = jnp.exp2((scores - highest) * factor).astype(BF16)
            both = jnp.dot(raised, v_ref[group], preferred_element_type=F32)
            result = jnp.where(head_of == head, both[:, :LANES] / both[:, LANES:], result)
        a_ref[group] = result.astype(BF16)

    attended = jnp.concatenate([a_ref[group] for group in range(groups)], axis=1)
    mixed = jnp.dot(attended, w_out_ref[...], preferred_element_type=F32)
    out_ref[...] = (mixed + dec_in).astype(BF16)


def tail(place, combine, filler, w_qkv, w_out, first, second, ranks):
    total, width = filler.shape
    groups = width // LANES
    mine = total // len(ranks[0])
    return pl.pallas_call(
        lambda *refs: tail_kernel(ranks, len(first), *refs),
        out_shape=jax.ShapeDtypeStruct((mine, width), BF16),
        in_specs=[SMEM] + [VMEM] * (4 + len(first) + len(second)),
        out_specs=VMEM,
        scratch_shapes=[
            pltpu.VMEM((combine.shape[1], width), BF16),
            pltpu.VMEM((groups, total, LANES), BF16),
            pltpu.VMEM((groups, total, 2 * LANES), BF16),
            pltpu.VMEM((groups, mine, LANES), BF16),
        ],
        compiler_params=pltpu.CompilerParams(vmem_limit_bytes=36 << 20),
    )(place, combine, filler, w_qkv, w_out, *first, *second)


def sinusoid_table(count, block, width):
    half = width // 2
    speeds = jnp.exp(-math.log(10000.0) * jnp.arange(half).astype(F32) / half)
    far = (jnp.arange(count // block) * block).astype(F32)[:, None] * speeds[None, :]
    near = jnp.arange(block).astype(F32)[:, None] * speeds[None, :]
    far_sin, far_cos = jnp.sin(far)[:, None, :], jnp.cos(far)[:, None, :]
    near_sin, near_cos = jnp.sin(near)[None], jnp.cos(near)[None]
    sines = far_sin * near_cos + far_cos * near_sin
    cosines = far_cos * near_cos - far_sin * near_sin
    return jnp.concatenate([sines, cosines], axis=2).reshape(count, width)


def per_device(tokens, slot_keys, w_in, w_back, w_proj, dec_source, mask_token, w_qkv, w_out):
    vis_dev, width = tokens.shape
    n_tok = lax.axis_size("tok")
    n_clip = lax.axis_size("clip")
    slots = slot_keys.shape[1]
    dec_width = w_proj.shape[1]
    listing = dec_source[0]
    dec_total = listing.shape[0]
    dec_dev = dec_total // n_tok
    vis_all = vis_dev * n_tok
    myself = lax.axis_index("tok").astype(jnp.int32)
    capacity = dec_dev // n_tok
    orders = bit_orders(n_tok)
    back_orders = tuple(order[::-1] for order in orders)
    ranks = tuple(gathered_ranks(order) for order in back_orders)

    blocks = listing.reshape(n_tok, dec_dev)
    owners = blocks // vis_dev
    earlier = jnp.arange(dec_dev)[:, None] > jnp.arange(dec_dev)[None, :]
    same = (owners[:, :, None] == owners[:, None, :]) & earlier[None]
    order_here = jnp.minimum(jnp.sum(same.astype(jnp.int32), axis=2), capacity - 1)
    visible = blocks < vis_all
    matched = (owners[:, None, :] == myself) & (order_here[:, None, :] == jnp.arange(capacity)[None, :, None])
    local = blocks - myself * vis_dev + 1
    source_rows = jnp.sum(jnp.where(matched, local[:, None, :], 0), axis=2) - 1
    picker = (source_rows.reshape(-1)[:, None] == jnp.arange(vis_dev)[None, :]).astype(BF16)
    places = jnp.where(visible, (owners ^ myself) * capacity + order_here, -1).reshape(dec_total, 1)
    filler = jnp.where(
        visible.reshape(-1)[:, None],
        0.0,
        mask_token.astype(F32)[None, :] + sinusoid_table(dec_total, dec_dev, dec_width),
    ).astype(BF16)

    first, first_other = w_in[0], swap(w_in[0], "clip", 1)
    second, second_other = w_back[0], swap(w_back[0], "clip", 1)

    *quarters, combine = front(myself.reshape(1), tokens, slot_keys, orders)
    state = [(quarters[0], quarters[1]), (quarters[2], quarters[3])]
    for step in range(len(orders[0])):
        last = step == len(orders[0]) - 1
        arrived = [swap(state[path][1], "tok", 1 << orders[path][step]) for path in range(2)]
        state = [merge(state[path][0], arrived[path], last) for path in range(2)]
    slot_in = jnp.concatenate(state, axis=0)

    outgoing = jnp.dot(picker, combine, preferred_element_type=F32).astype(BF16)
    cut = outgoing.shape[0] // 2
    spread = [
        gather_bits(outgoing[path * cut : (path + 1) * cut], "tok", back_orders[path]) for path in range(2)
    ]
    ordered = put_in_order(places, spread[0], spread[1], ranks)

    others = [2 * step for step in range(1, n_clip // 2)]
    rows = [slot_in] + [swap(slot_in, "clip", mask) for mask in others]
    results = experts(rows, first, first_other, second, second_other, w_proj)
    slot_proj = results[0].astype(F32)
    for mask, result in zip(others, results[1:]):
        slot_proj = slot_proj + swap(result, "clip", mask).astype(F32)
    slot_proj = slot_proj.astype(BF16)
    cut = slot_proj.shape[0] // 2
    everyone = [
        gather_bits(slot_proj[path * cut : (path + 1) * cut], "tok", back_orders[path]) for path in range(2)
    ]
    return tail(myself.reshape(1), ordered, filler, w_qkv, w_out, everyone[0], everyone[1], ranks)


def solution(mesh):
    placed = (
        P(("clip", "tok"), None),
        P(),
        P("tok", None, "clip"),
        P("tok", "clip", None),
        P(),
        P("clip", None),
        P(),
        P(),
        P(),
    )
    return jax.shard_map(
        per_device, mesh=mesh, in_specs=placed, out_specs=P(("clip", "tok"), None), check_vma=False
    )
```

time: 133 us -> 103 us (0.77)
  waiting for transfers between devices: 43 us -> 22.7 us
  starting transfers between devices: 14.5 us -> 33.5 us
  between operations: 13.6 us -> 0.33 us
  matrix products: 7.62 us -> 0.35 us
  blocking collectives: 7.18 us -> 0 us
  Pallas kernels: 26.5 us -> 32.9 us
  local copies, waits for them, and re-layouts: 9.97 us -> 5.87 us
  other arithmetic: 10.6 us -> 7.11 us
    all_to_all x3 -> x0, waiting for transfers between devices: 42.9 us -> none  [the longest x1 32.4 us: per_device(): lax.all_to_all(partial_sums.reshape(n_tok, slots_e, width + LANES), 'tok'...]
    ppermute x0 -> x22, starting transfers between devices: none -> 33.5 us  [swap(): lax.ppermute(values, axis, [(index, index ^ mask) for index in range(coun...]
    ppermute x0 -> x22, waiting for transfers between devices: none -> 22.7 us  [swap(): lax.ppermute(values, axis, [(index, index ^ mask) for index in range(coun...]
    all_to_all x3 -> x0, starting transfers between devices: 14.5 us -> none  [the longest x1 7.42 us: per_device(): lax.all_to_all(partial_sums.reshape(n_tok, slots_e, width + LANES), 'tok'...]
    all_gather x1 -> x0, blocking collectives: 7.18 us -> none  [per_device(): lax.all_gather(slot_in, 'clip', axis=0, tiled=True)]
    dot_general x3 -> x0, matrix products: 6.56 us -> none  [the longest x1 3.6 us: per_device(): jnp.dot(partial_out, w_proj, preferred_element_type=F32).astype(BF16)]
    pallas_call x2 -> x10, Pallas kernels: 26.5 us -> 32.9 us  [the longest x1 21.7 us: tail(): pl.pallas_call(lambda *refs: tail_kernel(ranks, len(first), *refs), out_s...]
    convert_element_type x1, other arithmetic: 3.43 us -> 0.56 us  [per_device(): filler = jnp.where(visible.reshape(-1)[:, None], 0.0, mask_token.astype(F...]
  transfers between devices with their start and end apart: 4 -> 22, of which waited for: 3 -> 11; matrix products, arithmetic and copies ran while one was open for 17% -> 7% of each run, Pallas kernels for 0% -> 7%
where the time goes in v2:
time: 103 us
  starting transfers between devices  33.5 us (33%)
  Pallas kernels  32.9 us (32%)
  waiting for transfers between devices  22.7 us (22%)
  other arithmetic  7.11 us (7%)
  local copies, waits for them, and re-layouts  5.87 us (6%)
    ppermute x22, starting transfers between devices, swap(): lax.ppermute(values, axis, [(index, index ^ mask) for index in range(coun...  33.5 us
    ppermute x22, waiting for transfers between devices, swap(): lax.ppermute(values, axis, [(index, index ^ mask) for index in range(coun...  22.7 us
    pallas_call x1, Pallas kernels, tail(): pl.pallas_call(lambda *refs: tail_kernel(ranks, len(first), *refs), out_s...  21.7 us
    unnamed x21, local copies, waits for them, and re-layouts  4.39 us
    pallas_call x1, Pallas kernels, front(): pl.pallas_call(lambda *refs: front_kernel(orders, *refs), out_shape=(quar...  3.95 us
    pallas_call x1, Pallas kernels, experts(): pl.pallas_call(lambda *refs: experts_kernel(count, *refs), out_shape=(jax...  3.85 us
    pallas_call x6, Pallas kernels, merge(): pl.pallas_call(merge_kernel, out_shape=shape, in_specs=[VMEM, VMEM], out_...  2.67 us
    select_n x1, other arithmetic, per_device(): jnp.where(visible, (owners ^ myself) * capacity + order_here, -1)  2.29 us
  transfers between devices with their start and end apart: 22, of which 11 were waited for; matrix products, arithmetic and copies ran while one was open for 7% of the time, Pallas kernels for 7%

profile of v2, /device:TPU:0, one launch (start us, length us, event | category | flops | bytes accessed | tf_op | source)
XLA Modules:
  0.0 102.7 jit_solution(15745683139975209371)
XLA Ops:
  0.0 0.5 broadcast.301
  0.6 1.4 %reduce.5 = s32[2048]{0:T(1024)S(1)} reduce(s32[1,2048]{1,0:T(1,128)} %param.14, s32[]{:T(128)} %broadcast.301), dimensions={0}, to_apply=%param.14.reduce_sub_computation.3 | reduce | bytes 16388 | tf_op args[5]
  2.0 0.8 convert_reduce_fusion
  2.8 0.2 select_reduce_fusion
  3.1 0.1 sub.36
  3.2 1.2 %copy-done.4 = bf16[512,1024]{1,0:T(8,128)(2,1)S(1)} copy-done((bf16[512,1024]{1,0:T(8,128)(2,1)S(1)}, bf16[512,1024]{1,0:T(8,128)(2,1)}, u32[]{:S(2)}) %copy-start.4) | copy-done | bytes 1048600
  4.4 1.2 %copy-done.5 = bf16[1024,512]{1,0:T(8,128)(2,1)S(1)} copy-done((bf16[1024,512]{1,0:T(8,128)(2,1)S(1)}, bf16[1024,512]{1,0:T(8,128)(2,1)}, u32[]{:S(2)}) %copy-start.5) | copy-done | bytes 1048600
  5.6 4.0 %shard_map.91 = (bf16[128,1152]{1,0:T(8,128)(2,1)S(1)}, bf16[128,1152]{1,0:T(8,128)(2,1)}, bf16[128,1152]{1,0:T(8,128)(2,1)S(1)}, bf16[128,1152]{1,0:T(8,128)(2,1)}, bf16[512,512]{1,0:T(8,128)(2,1)S(1)}) custom-call(s32[1]{0:T(128)} %bitcast.refs_0_, bf16[512,1024]{1,0:T(8,128)(2,1)S(1)} %copy-done.4, bf16[1024,512]{1,0:T(8,128)(2,1)S(1)} %copy-done.5), custom_call_target="tpu_custom_call" | custom-call | tf_op jit(solution)/shard_map/pallas_call | solution.py:139
  9.6 0.3 convolution_convert_fusion
  10.0 4.1 %collective-permute-start.3 = (bf16[128,512]{1,0:T(8,128)(2,1)S(1)}, bf16[128,512]{1,0:T(8,128)(2,1)S(1)}, u32[]{:S(2)}, u32[]{:S(2)}) collective-permute-start(bf16[128,512]{1,0:T(8,128)(2,1)S(1)} %get-tuple-element.39.refs_5_), channel_id=1, source_target_pairs={{0,4},{1,5},{2,6},{3,7},{4,0},{5,1},{6,2},{7,3},{8,12},{9,13},{10,... | collective-permute-start | bytes 393224 | tf_op jit(solution)/shard_map/ppermute | solution.py:51
  14.0 1.6 %collective-permute-start.6 = (bf16[128,1152]{1,0:T(8,128)(2,1)}, bf16[128,1152]{1,0:T(8,128)(2,1)}, u32[]{:S(2)}, u32[]{:S(2)}) collective-permute-start(bf16[128,1152]{1,0:T(8,128)(2,1)} %get-tuple-element.22), channel_id=1, source_target_pairs={{0,2},{1,3},{2,0},{3,1},{4,6},{5,7},{6,4},{7,5},{8,10},{9,11},{10,... | collective-permute-start | bytes 884744 | tf_op jit(solution)/shard_map/ppermute | solution.py:51
  15.6 1.5 %collective-permute-start.9 = (bf16[128,1152]{1,0:T(8,128)(2,1)}, bf16[128,1152]{1,0:T(8,128)(2,1)S(1)}, u32[]{:S(2)}, u32[]{:S(2)}) collective-permute-start(bf16[128,1152]{1,0:T(8,128)(2,1)} %get-tuple-element.28), channel_id=1, source_target_pairs={{0,1},{1,0},{2,3},{3,2},{4,5},{5,4},{6,7},{7,6},{8,9},{9,8},{10,11... | collective-permute-start | bytes 884744 | tf_op jit(solution)/shard_map/ppermute | solution.py:51
  17.1 0.5 collective-permute-start.14
  17.7 1.4 %copy.23 = s32[1,2048]{0,1:T(8,128)} copy(s32[1,2048]{1,0:T(1,128)S(1)} %bitcast.20) | data formatting | bytes 16384
  19.1 1.4 %copy.16 = s32[2048,1]{1,0:T(8,128)} copy(s32[2048,1]{0,1:T(1,128)S(1)} %bitcast.19) | data formatting | bytes 16384 | tf_op jit(solution)/shard_map/reshape;squeeze | solution.py:364
  20.4 0.1 multiply_sine_fusion.1
  20.6 2.3 %fusion.6.refs_0_ = s32[2048,1]{1,0:T(8,128)S(1)} fusion(s32[1,2048]{0,1:T(8,128)} %copy.23, s32[2048,1]{1,0:T(8,128)} %copy.16, s32[]{:T(128)} %axis_index.12), kind=kLoop, calls=%fused_computation.15 | loop fusion | flops 40960 | bytes 24580 | tf_op jit(solution)/shard_map/jit(_where)/select_n | solution.py:374
  22.9 1.0 multiply_cosine_fusion
  23.9 0.6 collective-permute-done.6.came_ref
  24.5 1.3 %shard_map.93 = (bf16[64,1152]{1,0:T(8,128)(2,1)S(1)}, bf16[64,1152]{1,0:T(8,128)(2,1)S(1)}) custom-call(bf16[128,1152]{1,0:T(8,128)(2,1)S(1)} %get-tuple-element.21.kept_ref, bf16[128,1152]{1,0:T(8,128)(2,1)} %collective-permute-done.6.came_ref), custom_call_target="tpu_custom_call" | custom-call | tf_op jit(solution)/shard_map/pallas_call | solution.py:182
  25.8 1.6 %collective-permute-start.7 = (bf16[64,1152]{1,0:T(8,128)(2,1)S(1)}, bf16[64,1152]{1,0:T(8,128)(2,1)S(1)}, u32[]{:S(2)}, u32[]{:S(2)}) collective-permute-start(bf16[64,1152]{1,0:T(8,128)(2,1)S(1)} %get-tuple-element.24), channel_id=1, source_target_pairs={{0,1},{1,0},{2,3},{3,2},{4,5},{5,4},{6,7},{7,6},{8,9},{9,8},{10,11... | collective-permute-start | bytes 442376 | tf_op jit(solution)/shard_map/ppermute | solution.py:51
  27.4 0.0 collective-permute-done.9.came_ref
  27.4 0.3 shard_map.96
  27.8 1.2 %collective-permute-start.10 = (bf16[64,1152]{1,0:T(8,128)(2,1)S(1)}, bf16[64,1152]{1,0:T(8,128)(2,1)S(1)}, u32[]{:S(2)}, u32[]{:S(2)}) collective-permute-start(bf16[64,1152]{1,0:T(8,128)(2,1)S(1)} %get-tuple-element.30), channel_id=1, source_target_pairs={{0,2},{1,3},{2,0},{3,1},{4,6},{5,7},{6,4},{7,5},{8,10},{9,11},{10,... | collective-permute-start | bytes 442376 | tf_op jit(solution)/shard_map/ppermute | solution.py:51
  29.0 0.4 multiply_add_fusion
  29.5 0.0 copy-start.1
  29.5 1.5 %collective-permute-done.7.came_ref = bf16[64,1152]{1,0:T(8,128)(2,1)S(1)} collective-permute-done((bf16[64,1152]{1,0:T(8,128)(2,1)S(1)}, bf16[64,1152]{1,0:T(8,128)(2,1)S(1)}, u32[]{:S(2)}, u32[]{:S(2)}) %collective-permute-start.7) | collective-permute-done | bytes 147488 | tf_op jit(solution)/shard_map/ppermute | solution.py:51
  31.0 1.2 %collective-permute-start = (bf16[128,512]{1,0:T(8,128)(2,1)S(1)}, bf16[128,512]{1,0:T(8,128)(2,1)S(1)}, u32[]{:S(2)}, u32[]{:S(2)}) collective-permute-start(bf16[128,512]{1,0:T(8,128)(2,1)S(1)} %get-tuple-element.40.refs_1_), channel_id=1, source_target_pairs={{0,4},{1,5},{2,6},{3,7},{4,0},{5,1},{6,2},{7,3},{8,12},{9,13},{10,... | collective-permute-start | bytes 393224 | tf_op jit(solution)/shard_map/ppermute | solution.py:51
  32.2 0.3 shard_map.94
  32.4 1.0 %collective-permute-done.10.came_ref = bf16[64,1152]{1,0:T(8,128)(2,1)S(1)} collective-permute-done((bf16[64,1152]{1,0:T(8,128)(2,1)S(1)}, bf16[64,1152]{1,0:T(8,128)(2,1)S(1)}, u32[]{:S(2)}, u32[]{:S(2)}) %collective-permute-start.10) | collective-permute-done | bytes 147488 | tf_op jit(solution)/shard_map/ppermute | solution.py:51
  33.5 1.2 %collective-permute-start.8 = (bf16[32,1152]{1,0:T(8,128)(2,1)S(1)}, bf16[32,1152]{1,0:T(8,128)(2,1)S(1)}, u32[]{:S(2)}, u32[]{:S(2)}) collective-permute-start(bf16[32,1152]{1,0:T(8,128)(2,1)S(1)} %get-tuple-element.26), channel_id=1, source_target_pairs={{0,4},{1,5},{2,6},{3,7},{4,0},{5,1},{6,2},{7,3},{8,12},{9,13},{10,... | collective-permute-start | bytes 221192 | tf_op jit(solution)/shard_map/ppermute | solution.py:51
  34.7 0.3 shard_map.97
  34.9 0.0 collective-permute-done.3.refs_6_
  34.9 1.8 %collective-permute-start.11 = (bf16[32,1152]{1,0:T(8,128)(2,1)S(1)}, bf16[32,1152]{1,0:T(8,128)(2,1)S(1)}, u32[]{:S(2)}, u32[]{:S(2)}) collective-permute-start(bf16[32,1152]{1,0:T(8,128)(2,1)S(1)} %get-tuple-element.32), channel_id=1, source_target_pairs={{0,4},{1,5},{2,6},{3,7},{4,0},{5,1},{6,2},{7,3},{8,12},{9,13},{10,... | collective-permute-start | bytes 221192 | tf_op jit(solution)/shard_map/ppermute | solution.py:51
  36.8 7.1 %collective-permute-done.8.came_ref = bf16[32,1152]{1,0:T(8,128)(2,1)S(1)} collective-permute-done((bf16[32,1152]{1,0:T(8,128)(2,1)S(1)}, bf16[32,1152]{1,0:T(8,128)(2,1)S(1)}, u32[]{:S(2)}, u32[]{:S(2)}) %collective-permute-start.8) | collective-permute-done | bytes 73760 | tf_op jit(solution)/shard_map/ppermute | solution.py:51
  43.9 0.2 shard_map.95
  44.1 0.5 collective-permute-done.11.came_ref
  44.7 0.2 shard_map.98
  44.9 1.6 %collective-permute-start.12 = (bf16[64,1024]{1,0:T(8,128)(2,1)S(1)}, bf16[64,1024]{1,0:T(8,128)(2,1)S(1)}, u32[]{:S(2)}, u32[]{:S(2)}) collective-permute-start(bf16[64,1024]{1,0:T(8,128)(2,1)S(1)} %pad_maximum_fusion.4.refs_0_), channel_id=1, source_target_pairs={{0,16},{8,24},{16,0},{24,8},{1,17},{9,25},{17,1},{25,9},{2,18},{10... | collective-permute-start | bytes 393224 | tf_op jit(solution)/shard_map/ppermute | solution.py:51
  46.6 0.0 collective-permute-done.refs_2_
  46.6 1.0 collective-permute-start.1
  47.6 2.4 %collective-permute-done.12.refs_1_ = bf16[64,1024]{1,0:T(8,128)(2,1)S(1)} collective-permute-done((bf16[64,1024]{1,0:T(8,128)(2,1)S(1)}, bf16[64,1024]{1,0:T(8,128)(2,1)S(1)}, u32[]{:S(2)}, u32[]{:S(2)}) %collective-permute-start.12) | collective-permute-done | bytes 131104 | tf_op jit(solution)/shard_map/ppermute | solution.py:51
  50.0 3.8 %shard_map.99 = (bf16[64,512]{1,0:T(8,128)(2,1)S(1)}, bf16[64,512]{1,0:T(8,128)(2,1)S(1)}) custom-call(bf16[64,1024]{1,0:T(8,128)(2,1)S(1)} %pad_maximum_fusion.4.refs_0_, bf16[64,1024]{1,0:T(8,128)(2,1)S(1)} %collective-permute-done.12.refs_1_, bf16[1024,1024]{1,0:T(8,128)(2,1)S(1)} %bitcast.14, bf16[1024,1024]{1,0:T(8,128)(2,1)} %collective-permute-done.13.refs_3_, ...), custom_call_target="tpu_custom_call" | custom-call | tf_op jit(solution)/shard_map/pallas_call | solution.py:208
  53.9 1.6 %collective-permute-start.15 = (bf16[64,512]{1,0:T(8,128)(2,1)S(1)}, bf16[64,512]{1,0:T(8,128)(2,1)S(1)}, u32[]{:S(2)}, u32[]{:S(2)}) collective-permute-start(bf16[64,512]{1,0:T(8,128)(2,1)S(1)} %get-tuple-element.34), channel_id=1, source_target_pairs={{0,16},{8,24},{16,0},{24,8},{1,17},{9,25},{17,1},{25,9},{2,18},{10... | collective-permute-start | bytes 196616 | tf_op jit(solution)/shard_map/ppermute | solution.py:51
  55.4 0.0 collective-permute-done.4.refs_7_
  55.5 1.0 collective-permute-start.5
  56.4 1.8 %collective-permute-done.15 = bf16[64,512]{1,0:T(8,128)(2,1)S(1)} collective-permute-done((bf16[64,512]{1,0:T(8,128)(2,1)S(1)}, bf16[64,512]{1,0:T(8,128)(2,1)S(1)}, u32[]{:S(2)}, u32[]{:S(2)}) %collective-permute-start.15) | collective-permute-done | bytes 65568 | tf_op jit(solution)/shard_map/ppermute | solution.py:51
  58.2 1.9 %collective-permute-start.19 = (bf16[32,512]{1,0:T(8,128)(2,1)S(1)}, bf16[32,512]{1,0:T(8,128)(2,1)S(1)}, u32[]{:S(2)}, u32[]{:S(2)}) collective-permute-start(bf16[32,512]{1,0:T(8,128)(2,1)S(1)} %get-tuple-element.41.refs_9_), channel_id=1, source_target_pairs={{0,4},{1,5},{2,6},{3,7},{4,0},{5,1},{6,2},{7,3},{8,12},{9,13},{10,... | collective-permute-start | bytes 98312 | tf_op jit(solution)/shard_map/ppermute | solution.py:51
  60.1 0.0 collective-permute-done.1.refs_3_
  60.2 0.6 collective-permute-start.2
  60.8 2.0 %collective-permute-start.16 = (bf16[32,512]{1,0:T(8,128)(2,1)S(1)}, bf16[32,512]{1,0:T(8,128)(2,1)S(1)}, u32[]{:S(2)}, u32[]{:S(2)}) collective-permute-start(bf16[32,512]{1,0:T(8,128)(2,1)S(1)} %get-tuple-element.42.refs_5_), channel_id=1, source_target_pairs={{0,4},{1,5},{2,6},{3,7},{4,0},{5,1},{6,2},{7,3},{8,12},{9,13},{10,... | collective-permute-start | bytes 98312 | tf_op jit(solution)/shard_map/ppermute | solution.py:51
  62.8 0.4 collective-permute-done.19.refs_10_
  63.2 1.8 %collective-permute-start.20 = (bf16[64,512]{1,0:T(8,128)(2,1)S(1)}, bf16[64,512]{1,0:T(8,128)(2,1)S(1)}, u32[]{:S(2)}, u32[]{:S(2)}) collective-permute-start(bf16[64,512]{1,0:T(8,128)(2,1)S(1)} %pad_maximum_fusion.8), channel_id=1, source_target_pairs={{0,2},{1,3},{2,0},{3,1},{4,6},{5,7},{6,4},{7,5},{8,10},{9,11},{10,... | collective-permute-start | bytes 196616 | tf_op jit(solution)/shard_map/ppermute | solution.py:51
  65.0 5.2 %collective-permute-done.16.refs_6_ = bf16[32,512]{1,0:T(8,128)(2,1)S(1)} collective-permute-done((bf16[32,512]{1,0:T(8,128)(2,1)S(1)}, bf16[32,512]{1,0:T(8,128)(2,1)S(1)}, u32[]{:S(2)}, u32[]{:S(2)}) %collective-permute-start.16) | collective-permute-done | bytes 32800 | tf_op jit(solution)/shard_map/ppermute | solution.py:51
  70.3 2.0 %collective-permute-start.17 = (bf16[64,512]{1,0:T(8,128)(2,1)S(1)}, bf16[64,512]{1,0:T(8,128)(2,1)S(1)}, u32[]{:S(2)}, u32[]{:S(2)}) collective-permute-start(bf16[64,512]{1,0:T(8,128)(2,1)S(1)} %pad_maximum_fusion.7), channel_id=1, source_target_pairs={{0,1},{1,0},{2,3},{3,2},{4,5},{5,4},{6,7},{7,6},{8,9},{9,8},{10,11... | collective-permute-start | bytes 196616 | tf_op jit(solution)/shard_map/ppermute | solution.py:51
  72.3 1.7 %collective-permute-start.21 = (bf16[128,512]{1,0:T(8,128)(2,1)S(1)}, bf16[128,512]{1,0:T(8,128)(2,1)S(1)}, u32[]{:S(2)}, u32[]{:S(2)}) collective-permute-start(bf16[128,512]{1,0:T(8,128)(2,1)S(1)} %pad_maximum_fusion.6), channel_id=1, source_target_pairs={{0,1},{1,0},{2,3},{3,2},{4,5},{5,4},{6,7},{7,6},{8,9},{9,8},{10,11... | collective-permute-start | bytes 393224 | tf_op jit(solution)/shard_map/ppermute | solution.py:51
  74.0 0.5 collective-permute-done.17.refs_7_
  74.6 3.6 %collective-permute-start.18 = (bf16[128,512]{1,0:T(8,128)(2,1)S(1)}, bf16[128,512]{1,0:T(8,128)(2,1)S(1)}, u32[]{:S(2)}, u32[]{:S(2)}) collective-permute-start(bf16[128,512]{1,0:T(8,128)(2,1)S(1)} %pad_maximum_fusion.5), channel_id=1, source_target_pairs={{0,2},{1,3},{2,0},{3,1},{4,6},{5,7},{6,4},{7,5},{8,10},{9,11},{10,... | collective-permute-start | bytes 393224 | tf_op jit(solution)/shard_map/ppermute | solution.py:51
  78.1 0.6 fusion.1.refs_2_
  78.7 0.0 copy-start.2
  78.7 0.0 copy-start.6
  78.7 0.8 shard_map.92.refs_1_
  79.5 1.6 %collective-permute-done.18.refs_8_ = bf16[128,512]{1,0:T(8,128)(2,1)S(1)} collective-permute-done((bf16[128,512]{1,0:T(8,128)(2,1)S(1)}, bf16[128,512]{1,0:T(8,128)(2,1)S(1)}, u32[]{:S(2)}, u32[]{:S(2)}) %collective-permute-start.18) | collective-permute-done | bytes 131104 | tf_op jit(solution)/shard_map/ppermute | solution.py:51
  81.1 21.7 %shard_map.100 = bf16[256,512]{1,0:T(8,128)(2,1)} custom-call(s32[1]{0:T(128)} %bitcast.refs_0_, bf16[2048,512]{1,0:T(8,128)(2,1)S(1)} %shard_map.92.refs_1_, bf16[2048,512]{1,0:T(8,128)(2,1)S(1)} %fusion.1.refs_2_, bf16[512,1536]{1,0:T(8,128)(2,1)S(1)} %copy-done.2, bf16[512,512]{1,0:T(8,128)(2,1)S(1)} %copy-done.6, ...), custom_call_target="tpu_custom_call" | custom-call | tf_op jit(solution)/shard_map/pallas_call | solution.py:321
  (45 shorter events, 0.4 us)
Async XLA Ops:
  0.0 17.1 %copy-start = (bf16[1,1024,1024]{2,1,0:T(8,128)(2,1)S(1)}, bf16[1,1024,1024]{2,1,0:T(8,128)(2,1)}, u32[]{:S(2)}) copy-start(bf16[1,1024,1024]{2,1,0:T(8,128)(2,1)} %param.11) | copy-start | bytes 6291460
  3.2 1.2 %copy-start.4 = (bf16[512,1024]{1,0:T(8,128)(2,1)S(1)}, bf16[512,1024]{1,0:T(8,128)(2,1)}, u32[]{:S(2)}) copy-start(bf16[512,1024]{1,0:T(8,128)(2,1)} %refs_1_.1) | copy-start | bytes 3145732
  4.4 1.2 %copy-start.5 = (bf16[1024,512]{1,0:T(8,128)(2,1)S(1)}, bf16[1024,512]{1,0:T(8,128)(2,1)}, u32[]{:S(2)}) copy-start(bf16[1024,512]{1,0:T(8,128)(2,1)} %refs_2_.1) | copy-start | bytes 3145732
  5.6 13.5 %copy-start.7 = (s32[1,2048]{1,0:T(1,128)S(1)}, s32[1,2048]{1,0:T(1,128)}, u32[]{:S(2)}) copy-start(s32[1,2048]{1,0:T(1,128)} %param.14) | copy-start | bytes 24580
  10.0 25.0 %collective-permute-start.3 = (bf16[128,512]{1,0:T(8,128)(2,1)S(1)}, bf16[128,512]{1,0:T(8,128)(2,1)S(1)}, u32[]{:S(2)}, u32[]{:S(2)}) collective-permute-start(bf16[128,512]{1,0:T(8,128)(2,1)S(1)} %get-tuple-element.39.refs_5_), channel_id=1, source_target_pairs={{0,4},{1,5},{2,6},{3,7},{4,0},{5,1},{6,2},{7,3},{8,12},{9,13},{10,... | collective-permute-start | bytes 393224 | tf_op jit(solution)/shard_map/ppermute | solution.py:51
  14.0 10.4 %collective-permute-start.6 = (bf16[128,1152]{1,0:T(8,128)(2,1)}, bf16[128,1152]{1,0:T(8,128)(2,1)}, u32[]{:S(2)}, u32[]{:S(2)}) collective-permute-start(bf16[128,1152]{1,0:T(8,128)(2,1)} %get-tuple-element.22), channel_id=1, source_target_pairs={{0,2},{1,3},{2,0},{3,1},{4,6},{5,7},{6,4},{7,5},{8,10},{9,11},{10,... | collective-permute-start | bytes 884744 | tf_op jit(solution)/shard_map/ppermute | solution.py:51
  15.6 11.8 %collective-permute-start.9 = (bf16[128,1152]{1,0:T(8,128)(2,1)}, bf16[128,1152]{1,0:T(8,128)(2,1)S(1)}, u32[]{:S(2)}, u32[]{:S(2)}) collective-permute-start(bf16[128,1152]{1,0:T(8,128)(2,1)} %get-tuple-element.28), channel_id=1, source_target_pairs={{0,1},{1,0},{2,3},{3,2},{4,5},{5,4},{6,7},{7,6},{8,9},{9,8},{10,11... | collective-permute-start | bytes 884744 | tf_op jit(solution)/shard_map/ppermute | solution.py:51
  17.1 32.8 %collective-permute-start.13 = (bf16[1024,1024]{1,0:T(8,128)(2,1)S(1)}, bf16[1024,1024]{1,0:T(8,128)(2,1)}, u32[]{:S(2)}, u32[]{:S(2)}) collective-permute-start(bf16[1024,1024]{1,0:T(8,128)(2,1)S(1)} %bitcast.13), channel_id=1, source_target_pairs={{0,8},{8,0},{16,24},{24,16},{1,9},{9,1},{17,25},{25,17},{2,10},{10... | collective-permute-start | bytes 6291464 | tf_op jit(solution)/shard_map/ppermute | solution.py:51
  17.1 32.8 %collective-permute-start.14 = (bf16[1024,1024]{1,0:T(8,128)(2,1)}, bf16[1024,1024]{1,0:T(8,128)(2,1)}, u32[]{:S(2)}, u32[]{:S(2)}) collective-permute-start(bf16[1024,1024]{1,0:T(8,128)(2,1)} %bitcast.15), channel_id=1, source_target_pairs={{0,8},{8,0},{16,24},{24,16},{1,9},{9,1},{17,25},{25,17},{2,10},{10... | collective-permute-start | bytes 6291464 | tf_op jit(solution)/shard_map/ppermute | solution.py:51
  25.8 5.2 %collective-permute-start.7 = (bf16[64,1152]{1,0:T(8,128)(2,1)S(1)}, bf16[64,1152]{1,0:T(8,128)(2,1)S(1)}, u32[]{:S(2)}, u32[]{:S(2)}) collective-permute-start(bf16[64,1152]{1,0:T(8,128)(2,1)S(1)} %get-tuple-element.24), channel_id=1, source_target_pairs={{0,1},{1,0},{2,3},{3,2},{4,5},{5,4},{6,7},{7,6},{8,9},{9,8},{10,11... | collective-permute-start | bytes 442376 | tf_op jit(solution)/shard_map/ppermute | solution.py:51
  27.8 5.7 %collective-permute-start.10 = (bf16[64,1152]{1,0:T(8,128)(2,1)S(1)}, bf16[64,1152]{1,0:T(8,128)(2,1)S(1)}, u32[]{:S(2)}, u32[]{:S(2)}) collective-permute-start(bf16[64,1152]{1,0:T(8,128)(2,1)S(1)} %get-tuple-element.30), channel_id=1, source_target_pairs={{0,2},{1,3},{2,0},{3,1},{4,6},{5,7},{6,4},{7,5},{8,10},{9,11},{10,... | collective-permute-start | bytes 442376 | tf_op jit(solution)/shard_map/ppermute | solution.py:51
  29.0 17.5 %copy-start.8 = (bf16[512]{0:T(512)(128)(2,1)S(1)}, bf16[512]{0:T(512)(128)(2,1)}, u32[]{:S(2)}) copy-start(bf16[512]{0:T(512)(128)(2,1)} %param.15) | copy-start | bytes 3076
  29.0 21.0 %copy-start.3 = (bf16[1024,512]{1,0:T(8,128)(2,1)S(1)}, bf16[1024,512]{1,0:T(8,128)(2,1)}, u32[]{:S(2)}) copy-start(bf16[1024,512]{1,0:T(8,128)(2,1)} %refs_6_.1) | copy-start | bytes 3145732
  29.5 20.5 %copy-start.1 = (bf16[1,1024,1024]{2,1,0:T(8,128)(2,1)S(1)}, bf16[1,1024,1024]{2,1,0:T(8,128)(2,1)}, u32[]{:S(2)}) copy-start(bf16[1,1024,1024]{2,1,0:T(8,128)(2,1)} %param.12) | copy-start | bytes 6291460
  31.0 15.6 %collective-permute-start = (bf16[128,512]{1,0:T(8,128)(2,1)S(1)}, bf16[128,512]{1,0:T(8,128)(2,1)S(1)}, u32[]{:S(2)}, u32[]{:S(2)}) collective-permute-start(bf16[128,512]{1,0:T(8,128)(2,1)S(1)} %get-tuple-element.40.refs_1_), channel_id=1, source_target_pairs={{0,4},{1,5},{2,6},{3,7},{4,0},{5,1},{6,2},{7,3},{8,12},{9,13},{10,... | collective-permute-start | bytes 393224 | tf_op jit(solution)/shard_map/ppermute | solution.py:51
  33.5 10.4 %collective-permute-start.8 = (bf16[32,1152]{1,0:T(8,128)(2,1)S(1)}, bf16[32,1152]{1,0:T(8,128)(2,1)S(1)}, u32[]{:S(2)}, u32[]{:S(2)}) collective-permute-start(bf16[32,1152]{1,0:T(8,128)(2,1)S(1)} %get-tuple-element.26), channel_id=1, source_target_pairs={{0,4},{1,5},{2,6},{3,7},{4,0},{5,1},{6,2},{7,3},{8,12},{9,13},{10,... | collective-permute-start | bytes 221192 | tf_op jit(solution)/shard_map/ppermute | solution.py:51
  34.9 9.7 %collective-permute-start.11 = (bf16[32,1152]{1,0:T(8,128)(2,1)S(1)}, bf16[32,1152]{1,0:T(8,128)(2,1)S(1)}, u32[]{:S(2)}, u32[]{:S(2)}) collective-permute-start(bf16[32,1152]{1,0:T(8,128)(2,1)S(1)} %get-tuple-element.32), channel_id=1, source_target_pairs={{0,4},{1,5},{2,6},{3,7},{4,0},{5,1},{6,2},{7,3},{8,12},{9,13},{10,... | collective-permute-start | bytes 221192 | tf_op jit(solution)/shard_map/ppermute | solution.py:51
  43.9 11.5 %collective-permute-start.4 = (bf16[256,512]{1,0:T(8,128)(2,1)S(1)}, bf16[256,512]{1,0:T(8,128)(2,1)S(1)}, u32[]{:S(2)}, u32[]{:S(2)}) collective-permute-start(bf16[256,512]{1,0:T(8,128)(2,1)S(1)} %pad_maximum_fusion.3), channel_id=1, source_target_pairs={{0,2},{1,3},{2,0},{3,1},{4,6},{5,7},{6,4},{7,5},{8,10},{9,11},{10,... | collective-permute-start | bytes 786440 | tf_op jit(solution)/shard_map/ppermute | solution.py:51
  44.9 5.0 %collective-permute-start.12 = (bf16[64,1024]{1,0:T(8,128)(2,1)S(1)}, bf16[64,1024]{1,0:T(8,128)(2,1)S(1)}, u32[]{:S(2)}, u32[]{:S(2)}) collective-permute-start(bf16[64,1024]{1,0:T(8,128)(2,1)S(1)} %pad_maximum_fusion.4.refs_0_), channel_id=1, source_target_pairs={{0,16},{8,24},{16,0},{24,8},{1,17},{9,25},{17,1},{25,9},{2,18},{10... | collective-permute-start | bytes 393224 | tf_op jit(solution)/shard_map/ppermute | solution.py:51
  46.6 13.5 %collective-permute-start.1 = (bf16[256,512]{1,0:T(8,128)(2,1)S(1)}, bf16[256,512]{1,0:T(8,128)(2,1)S(1)}, u32[]{:S(2)}, u32[]{:S(2)}) collective-permute-start(bf16[256,512]{1,0:T(8,128)(2,1)S(1)} %pad_maximum_fusion.2), channel_id=1, source_target_pairs={{0,1},{1,0},{2,3},{3,2},{4,5},{5,4},{6,7},{7,6},{8,9},{9,8},{10,11... | collective-permute-start | bytes 786440 | tf_op jit(solution)/shard_map/ppermute | solution.py:51
  53.9 4.3 %collective-permute-start.15 = (bf16[64,512]{1,0:T(8,128)(2,1)S(1)}, bf16[64,512]{1,0:T(8,128)(2,1)S(1)}, u32[]{:S(2)}, u32[]{:S(2)}) collective-permute-start(bf16[64,512]{1,0:T(8,128)(2,1)S(1)} %get-tuple-element.34), channel_id=1, source_target_pairs={{0,16},{8,24},{16,0},{24,8},{1,17},{9,25},{17,1},{25,9},{2,18},{10... | collective-permute-start | bytes 196616 | tf_op jit(solution)/shard_map/ppermute | solution.py:51
  55.5 23.3 %collective-permute-start.5 = (bf16[512,512]{1,0:T(8,128)(2,1)S(1)}, bf16[512,512]{1,0:T(8,128)(2,1)S(1)}, u32[]{:S(2)}, u32[]{:S(2)}) collective-permute-start(bf16[512,512]{1,0:T(8,128)(2,1)S(1)} %pad_maximum_fusion.1), channel_id=1, source_target_pairs={{0,1},{1,0},{2,3},{3,2},{4,5},{5,4},{6,7},{7,6},{8,9},{9,8},{10,11... | collective-permute-start | bytes 1572872 | tf_op jit(solution)/shard_map/ppermute | solution.py:51
  58.2 5.0 %collective-permute-start.19 = (bf16[32,512]{1,0:T(8,128)(2,1)S(1)}, bf16[32,512]{1,0:T(8,128)(2,1)S(1)}, u32[]{:S(2)}, u32[]{:S(2)}) collective-permute-start(bf16[32,512]{1,0:T(8,128)(2,1)S(1)} %get-tuple-element.41.refs_9_), channel_id=1, source_target_pairs={{0,4},{1,5},{2,6},{3,7},{4,0},{5,1},{6,2},{7,3},{8,12},{9,13},{10,... | collective-permute-start | bytes 98312 | tf_op jit(solution)/shard_map/ppermute | solution.py:51
  60.2 18.6 %collective-permute-start.2 = (bf16[512,512]{1,0:T(8,128)(2,1)S(1)}, bf16[512,512]{1,0:T(8,128)(2,1)S(1)}, u32[]{:S(2)}, u32[]{:S(2)}) collective-permute-start(bf16[512,512]{1,0:T(8,128)(2,1)S(1)} %pad_maximum_fusion), channel_id=1, source_target_pairs={{0,2},{1,3},{2,0},{3,1},{4,6},{5,7},{6,4},{7,5},{8,10},{9,11},{10,... | collective-permute-start | bytes 1572872 | tf_op jit(solution)/shard_map/ppermute | solution.py:51
  60.8 9.5 %collective-permute-start.16 = (bf16[32,512]{1,0:T(8,128)(2,1)S(1)}, bf16[32,512]{1,0:T(8,128)(2,1)S(1)}, u32[]{:S(2)}, u32[]{:S(2)}) collective-permute-start(bf16[32,512]{1,0:T(8,128)(2,1)S(1)} %get-tuple-element.42.refs_5_), channel_id=1, source_target_pairs={{0,4},{1,5},{2,6},{3,7},{4,0},{5,1},{6,2},{7,3},{8,12},{9,13},{10,... | collective-permute-start | bytes 98312 | tf_op jit(solution)/shard_map/ppermute | solution.py:51
  63.2 9.1 %collective-permute-start.20 = (bf16[64,512]{1,0:T(8,128)(2,1)S(1)}, bf16[64,512]{1,0:T(8,128)(2,1)S(1)}, u32[]{:S(2)}, u32[]{:S(2)}) collective-permute-start(bf16[64,512]{1,0:T(8,128)(2,1)S(1)} %pad_maximum_fusion.8), channel_id=1, source_target_pairs={{0,2},{1,3},{2,0},{3,1},{4,6},{5,7},{6,4},{7,5},{8,10},{9,11},{10,... | collective-permute-start | bytes 196616 | tf_op jit(solution)/shard_map/ppermute | solution.py:51
  70.3 4.3 %collective-permute-start.17 = (bf16[64,512]{1,0:T(8,128)(2,1)S(1)}, bf16[64,512]{1,0:T(8,128)(2,1)S(1)}, u32[]{:S(2)}, u32[]{:S(2)}) collective-permute-start(bf16[64,512]{1,0:T(8,128)(2,1)S(1)} %pad_maximum_fusion.7), channel_id=1, source_target_pairs={{0,1},{1,0},{2,3},{3,2},{4,5},{5,4},{6,7},{7,6},{8,9},{9,8},{10,11... | collective-permute-start | bytes 196616 | tf_op jit(solution)/shard_map/ppermute | solution.py:51
  72.3 7.2 %collective-permute-start.21 = (bf16[128,512]{1,0:T(8,128)(2,1)S(1)}, bf16[128,512]{1,0:T(8,128)(2,1)S(1)}, u32[]{:S(2)}, u32[]{:S(2)}) collective-permute-start(bf16[128,512]{1,0:T(8,128)(2,1)S(1)} %pad_maximum_fusion.6), channel_id=1, source_target_pairs={{0,1},{1,0},{2,3},{3,2},{4,5},{5,4},{6,7},{7,6},{8,9},{9,8},{10,11... | collective-permute-start | bytes 393224 | tf_op jit(solution)/shard_map/ppermute | solution.py:51
  74.6 6.5 %collective-permute-start.18 = (bf16[128,512]{1,0:T(8,128)(2,1)S(1)}, bf16[128,512]{1,0:T(8,128)(2,1)S(1)}, u32[]{:S(2)}, u32[]{:S(2)}) collective-permute-start(bf16[128,512]{1,0:T(8,128)(2,1)S(1)} %pad_maximum_fusion.5), channel_id=1, source_target_pairs={{0,2},{1,3},{2,0},{3,1},{4,6},{5,7},{6,4},{7,5},{8,10},{9,11},{10,... | collective-permute-start | bytes 393224 | tf_op jit(solution)/shard_map/ppermute | solution.py:51
  78.7 2.4 %copy-start.2 = (bf16[512,1536]{1,0:T(8,128)(2,1)S(1)}, bf16[512,1536]{1,0:T(8,128)(2,1)}, u32[]{:S(2)}) copy-start(bf16[512,1536]{1,0:T(8,128)(2,1)} %refs_3_.1) | copy-start | bytes 4718596
  78.7 2.4 %copy-start.6 = (bf16[512,512]{1,0:T(8,128)(2,1)S(1)}, bf16[512,512]{1,0:T(8,128)(2,1)}, u32[]{:S(2)}) copy-start(bf16[512,512]{1,0:T(8,128)(2,1)} %refs_4_.1) | copy-start | bytes 1572868

commit v3 on v2

--- a/solution.py
+++ b/solution.py
@@ -66,12 +66,36 @@
     ]
 
 
-def gather_bits(values, axis, order):
-    pieces = [values]
-    for bit in order:
-        held = pieces[0] if len(pieces) == 1 else jnp.concatenate(pieces, axis=0)
-        pieces.append(swap(held, axis, 1 << bit))
-    return pieces
+def gather_pair(values, axis, orders):
+    rows = values.shape[0]
+    half = rows // 2
+    arrays, steps = [values], []
+    starts = [[(0, 0)], [(0, half)]]
+    for step, (first, second) in enumerate(zip(*orders)):
+        together = orders[0][: step + 1] == orders[1][: step + 1]
+        if together:
+            held = arrays[0] if len(arrays) == 1 else jnp.concatenate(arrays, axis=0)
+            count = held.shape[0] // rows
+            arrays.append(swap(held, axis, 1 << first))
+            for path in range(2):
+                starts[path] = starts[path] + [(len(arrays) - 1, index * rows + path * half) for index in range(count)]
+            steps.append([arrays[-1]])
+            continue
+        fresh = []
+        for path, bit in enumerate((first, second)):
+            held = jnp.concatenate([arrays[index][row : row + half] for index, row in starts[path]], axis=0)
+            fresh.append(swap(held, axis, 1 << bit))
+        for path in range(2):
+            index = len(arrays) + path
+            starts[path] = starts[path] + [(index, place * half) for place in range(len(starts[path]))]
+        arrays = arrays + fresh
+        steps.append(fresh)
+    return arrays, starts, steps
+
+
+def tie(values, others):
+    kept = lax.optimization_barrier((tuple(values), tuple(others)))
+    return kept[0]
 
 
 def gathered_ranks(order):
@@ -210,46 +234,88 @@
         out_shape=(jax.ShapeDtypeStruct((rows, w_proj.shape[1]), BF16),) * count,
         in_specs=[VMEM] * (count + 5),
         out_specs=(VMEM,) * count,
-        compiler_params=pltpu.CompilerParams(vmem_limit_bytes=24 << 20),
+        compiler_params=pltpu.CompilerParams(vmem_limit_bytes=16 << 20),
     )(*slot_rows, first, first_other, second, second_other, w_proj)
 
 
-def order_kernel(ranks, first_count, places_ref, *refs):
-    pieces, out_ref = refs[:-1], refs[-1]
-    halves = (pieces[:first_count], pieces[first_count:])
+def slots_of(listing, vis_dev, count, capacity):
+    block = listing.shape[1]
+    owners = listing // vis_dev
+    across = jnp.broadcast_to(owners, (block, block))
+    before = lax.broadcasted_iota(jnp.int32, (block, block), 0) < lax.broadcasted_iota(jnp.int32, (block, block), 1)
+    same = (across == across.T) & before
+    ranks = jnp.sum(same.astype(F32), axis=0, keepdims=True).astype(jnp.int32)
+    return owners, jnp.minimum(ranks, capacity - 1)
+
+
+def pick_kernel(count, place_ref, listing_ref, combine_ref, out_ref):
+    vis_dev = combine_ref.shape[0]
+    block = listing_ref.shape[1] // count
+    capacity = block // count
+    myself = place_ref[0]
+    row = lax.broadcasted_iota(jnp.int32, (capacity, block), 0)
+    token = lax.broadcasted_iota(jnp.int32, (capacity, vis_dev), 1)
+    picks = []
+    for target in range(count):
+        listing = listing_ref[:, target * block : (target + 1) * block]
+        owners, ranks = slots_of(listing, vis_dev, count, capacity)
+        mine = jnp.where(owners == myself, ranks, -1)
+        local = jnp.broadcast_to(listing - myself * vis_dev + 1, (capacity, block))
+        source = jnp.sum(jnp.where(mine == row, local, 0).astype(F32), axis=1, keepdims=True).astype(jnp.int32) - 1
+        picks.append((source == token).astype(BF16))
+    picker = jnp.concatenate(picks, axis=0)
+    out_ref[...] = jnp.dot(picker, combine_ref[...], preferred_element_type=F32).astype(BF16)
+
+
+def pick(place, listing, combine, count):
+    return pl.pallas_call(
+        lambda *refs: pick_kernel(count, *refs),
+        out_shape=jax.ShapeDtypeStruct((listing.shape[1] // count, combine.shape[1]), BF16),
+        in_specs=[SMEM, VMEM, VMEM],
+        out_specs=VMEM,
+        compiler_params=pltpu.CompilerParams(vmem_limit_bytes=12 << 20),
+    )(place, listing, combine)
+
+
+def order_kernel(ranks, starts, vis_dev, place_ref, listing_ref, filler_ref, *refs):
+    pieces, out_ref, masked_ref = refs[:-2], refs[-2], refs[-1]
     total, slots = out_ref.shape
     count = len(ranks[0])
     block = total // count
     capacity = block // count
-    column = lax.broadcasted_iota(jnp.int32, (block, block), 1)
+    myself = place_ref[0]
+    slot = lax.broadcasted_iota(jnp.int32, (block, block), 0)
     for target in range(count):
         path, inner = divmod(target, count // 2)
         rows = [None] * count
-        place = 0
-        for ref in halves[path]:
-            for index in range(ref.shape[0] // (block // 2)):
-                start = index * (block // 2) + inner * capacity
-                rows[ranks[path][place]] = ref[start : start + capacity, :]
-                place += 1
-        chosen = (places_ref[target * block : (target + 1) * block, :] == column).astype(BF16)
-        out_ref[target * block : (target + 1) * block, :] = jnp.dot(
-            chosen, jnp.concatenate(rows, axis=0), preferred_element_type=F32
-        ).astype(BF16)
-
-
-def put_in_order(places, first, second, ranks):
-    total, slots = places.shape[0], first[0].shape[1]
-    return pl.pallas_call(
-        lambda *refs: order_kernel(ranks, len(first), *refs),
-        out_shape=jax.ShapeDtypeStruct((total, slots), BF16),
-        in_specs=[VMEM] * (1 + len(first) + len(second)),
-        out_specs=VMEM,
-        compiler_params=pltpu.CompilerParams(vmem_limit_bytes=24 << 20),
-    )(places, *first, *second)
+        for relative, (index, start) in zip(ranks[path], starts[path]):
+            first = start + inner * capacity
+            rows[relative] = pieces[index][first : first + capacity, :]
+        listing = listing_ref[:, target * block : (target + 1) * block]
+        owners, order = slots_of(listing, vis_dev, count, capacity)
+        visible = listing < count * vis_dev
+        places = jnp.where(visible, (owners ^ myself) * capacity + order, -1)
+        chosen = (places == slot).astype(F32).T.astype(BF16)
+        here = pl.ds(target * block, block)
+        out_ref[here, :] = jnp.dot(chosen, jnp.concatenate(rows, axis=0), preferred_element_type=F32).astype(BF16)
+        shown = jnp.broadcast_to(visible.astype(F32), (LANES, block)).T[:, 0:1]
+        masked_ref[here, :] = jnp.where(shown > 0.5, jnp.zeros((), F32), filler_ref[here, :].astype(F32)).astype(BF16)
+
+
+def put_in_order(place, listing, filler, arrays, starts, ranks, vis_dev):
+    total, width = filler.shape
+    slots = arrays[0].shape[1]
+    return pl.pallas_call(
+        lambda *refs: order_kernel(ranks, starts, vis_dev, *refs),
+        out_shape=(jax.ShapeDtypeStruct((total, slots), BF16), jax.ShapeDtypeStruct((total, width), BF16)),
+        in_specs=[SMEM] + [VMEM] * (2 + len(arrays)),
+        out_specs=(VMEM, VMEM),
+        compiler_params=pltpu.CompilerParams(vmem_limit_bytes=20 << 20),
+    )(place, listing, filler, *arrays)
 
 
 def tail_kernel(
-    ranks, first_count, place_ref, combine_ref, filler_ref, w_qkv_ref, w_out_ref, *refs
+    ranks, starts, place_ref, combine_ref, filler_ref, w_qkv_ref, w_out_ref, *refs
 ):
     pieces = refs[:-5]
     out_ref, slot_ref, k_ref, v_ref, a_ref = refs[-5:]
@@ -259,44 +325,35 @@
     groups = width // LANES
     in_group = LANES // head_dim
     myself = place_ref[0]
-    half = pieces[0].shape[0]
-    for path, refs_here in enumerate((pieces[:first_count], pieces[first_count:])):
-        place = 0
-        for ref in refs_here:
-            for index in range(ref.shape[0] // half):
-                target = pl.multiple_of((myself ^ ranks[path][place]) * (2 * half) + path * half, half)
-                slot_ref[pl.ds(target, half), :] = ref[index * half : (index + 1) * half, :]
-                place += 1
+    half = pieces[0].shape[0] // 2
+    for path in range(2):
+        for relative, (index, start) in zip(ranks[path], starts[path]):
+            target = pl.multiple_of((myself ^ relative) * (2 * half) + path * half, half)
+            slot_ref[pl.ds(target, half), :] = pieces[index][start : start + half, :]
     slot_rows = slot_ref[...]
     w_kv = w_qkv_ref[:, width:]
 
-    def positions(block):
-        rows = pl.ds(pl.multiple_of(block * mine, mine), mine)
+    def positions(block, many=1):
+        rows = pl.ds(block * mine * many, mine * many) if isinstance(block, int) else pl.ds(pl.multiple_of(block * mine, mine), mine)
         shown = jnp.dot(combine_ref[rows, :], slot_rows, preferred_element_type=F32).astype(BF16)
         dec_in = shown.astype(F32) + filler_ref[rows, :].astype(F32)
         return rows, dec_in, normalise(dec_in).astype(BF16)
 
-    ones = jnp.ones((mine, LANES), BF16)
-
-    @pl.loop(0, total // mine)
-    def _(block):
-        rows, _, normed = positions(block)
+    v_ref[:, :, LANES:] = jnp.ones((groups, total, LANES), BF16)
+    for block in range(total // mine // 8):
+        rows, _, normed = positions(block, 8)
         kv = jnp.dot(normed, w_kv, preferred_element_type=F32).astype(BF16)
         for group in range(groups):
             k_ref[group, rows, :] = kv[:, group * LANES : (group + 1) * LANES]
             v_ref[group, rows, :LANES] = kv[:, width + group * LANES : width + (group + 1) * LANES]
-            v_ref[group, rows, LANES:] = ones
 
     _, dec_in, normed = positions(myself)
     queries = jnp.dot(normed, w_qkv_ref[:, :width], preferred_element_type=F32).astype(BF16)
-    for group in range(groups):
-        a_ref[group] = queries[:, group * LANES : (group + 1) * LANES]
     head_of = lax.broadcasted_iota(jnp.int32, (mine, LANES), 1) // head_dim
     factor = math.log2(math.e) / math.sqrt(head_dim)
 
-    @pl.loop(0, groups)
-    def _(group):
-        q_group = a_ref[group]
+    for group in range(groups):
+        q_group = queries[:, group * LANES : (group + 1) * LANES]
         result = jnp.zeros((mine, LANES), F32)
         for head in range(in_group):
             q_head = jnp.where(head_of == head, q_group, jnp.zeros_like(q_group))
@@ -314,14 +371,14 @@
     out_ref[...] = (mixed + dec_in).astype(BF16)
 
 
-def tail(place, combine, filler, w_qkv, w_out, first, second, ranks):
+def tail(place, combine, filler, w_qkv, w_out, arrays, starts, ranks):
     total, width = filler.shape
     groups = width // LANES
     mine = total // len(ranks[0])
     return pl.pallas_call(
-        lambda *refs: tail_kernel(ranks, len(first), *refs),
+        lambda *refs: tail_kernel(ranks, starts, *refs),
         out_shape=jax.ShapeDtypeStruct((mine, width), BF16),
-        in_specs=[SMEM] + [VMEM] * (4 + len(first) + len(second)),
+        in_specs=[SMEM] + [VMEM] * (4 + len(arrays)),
         out_specs=VMEM,
         scratch_shapes=[
             pltpu.VMEM((combine.shape[1], width), BF16),
@@ -329,8 +386,8 @@
             pltpu.VMEM((groups, total, 2 * LANES), BF16),
             pltpu.VMEM((groups, mine, LANES), BF16),
         ],
-        compiler_params=pltpu.CompilerParams(vmem_limit_bytes=36 << 20),
-    )(place, combine, filler, w_qkv, w_out, *first, *second)
+        compiler_params=pltpu.CompilerParams(vmem_limit_bytes=32 << 20),
+    )(place, combine, filler, w_qkv, w_out, *arrays)
 
 
 def sinusoid_table(count, block, width):
@@ -351,63 +408,46 @@
     n_clip = lax.axis_size("clip")
     slots = slot_keys.shape[1]
     dec_width = w_proj.shape[1]
-    listing = dec_source[0]
-    dec_total = listing.shape[0]
+    dec_total = dec_source.shape[1]
     dec_dev = dec_total // n_tok
-    vis_all = vis_dev * n_tok
     myself = lax.axis_index("tok").astype(jnp.int32)
-    capacity = dec_dev // n_tok
+    place = myself.reshape(1)
     orders = bit_orders(n_tok)
     back_orders = tuple(order[::-1] for order in orders)
     ranks = tuple(gathered_ranks(order) for order in back_orders)
-
-    blocks = listing.reshape(n_tok, dec_dev)
-    owners = blocks // vis_dev
-    earlier = jnp.arange(dec_dev)[:, None] > jnp.arange(dec_dev)[None, :]
-    same = (owners[:, :, None] == owners[:, None, :]) & earlier[None]
-    order_here = jnp.minimum(jnp.sum(same.astype(jnp.int32), axis=2), capacity - 1)
-    visible = blocks < vis_all
-    matched = (owners[:, None, :] == myself) & (order_here[:, None, :] == jnp.arange(capacity)[None, :, None])
-    local = blocks - myself * vis_dev + 1
-    source_rows = jnp.sum(jnp.where(matched, local[:, None, :], 0), axis=2) - 1
-    picker = (source_rows.reshape(-1)[:, None] == jnp.arange(vis_dev)[None, :]).astype(BF16)
-    places = jnp.where(visible, (owners ^ myself) * capacity + order_here, -1).reshape(dec_total, 1)
-    filler = jnp.where(
-        visible.reshape(-1)[:, None],
-        0.0,
-        mask_token.astype(F32)[None, :] + sinusoid_table(dec_total, dec_dev, dec_width),
-    ).astype(BF16)
+    steps = len(orders[0])
 
     first, first_other = w_in[0], swap(w_in[0], "clip", 1)
     second, second_other = w_back[0], swap(w_back[0], "clip", 1)
 
-    *quarters, combine = front(myself.reshape(1), tokens, slot_keys, orders)
+    *quarters, combine = front(place, tokens, slot_keys, orders)
+
+    outgoing = pick(place, dec_source, combine, n_tok)
+    arrays, starts, brought = gather_pair(outgoing, "tok", back_orders)
+    (late_mask,) = tie([mask_token], [quarters[1]])
+    filler = (late_mask.astype(F32)[None, :] + sinusoid_table(dec_total, dec_dev, dec_width)).astype(BF16)
+    ordered, filler = put_in_order(place, dec_source, filler, arrays, starts, ranks, vis_dev)
+
     state = [(quarters[0], quarters[1]), (quarters[2], quarters[3])]
-    for step in range(len(orders[0])):
-        last = step == len(orders[0]) - 1
-        arrived = [swap(state[path][1], "tok", 1 << orders[path][step]) for path in range(2)]
+    for step in range(steps):
+        last = step == steps - 1
+        sent = [state[path][1] for path in range(2)]
+        if last:
+            sent = tie(sent, brought[0])
+        arrived = [swap(sent[path], "tok", 1 << orders[path][step]) for path in range(2)]
         state = [merge(state[path][0], arrived[path], last) for path in range(2)]
     slot_in = jnp.concatenate(state, axis=0)
 
-    outgoing = jnp.dot(picker, combine, preferred_element_type=F32).astype(BF16)
-    cut = outgoing.shape[0] // 2
-    spread = [
-        gather_bits(outgoing[path * cut : (path + 1) * cut], "tok", back_orders[path]) for path in range(2)
-    ]
-    ordered = put_in_order(places, spread[0], spread[1], ranks)
-
+    (slot_in,) = tie([slot_in], [array for group in brought[1:-1] for array in group])
     others = [2 * step for step in range(1, n_clip // 2)]
     rows = [slot_in] + [swap(slot_in, "clip", mask) for mask in others]
     results = experts(rows, first, first_other, second, second_other, w_proj)
     slot_proj = results[0].astype(F32)
     for mask, result in zip(others, results[1:]):
         slot_proj = slot_proj + swap(result, "clip", mask).astype(F32)
-    slot_proj = slot_proj.astype(BF16)
-    cut = slot_proj.shape[0] // 2
-    everyone = [
-        gather_bits(slot_proj[path * cut : (path + 1) * cut], "tok", back_orders[path]) for path in range(2)
-    ]
-    return tail(myself.reshape(1), ordered, filler, w_qkv, w_out, everyone[0], everyone[1], ranks)
+    (slot_proj,) = tie([slot_proj.astype(BF16)], brought[-1])
+    everyone, their_starts, _ = gather_pair(slot_proj, "tok", back_orders)
+    return tail(place, ordered, filler, w_qkv, w_out, everyone, their_starts, ranks)
 
 
 def solution(mesh):

time: 103 us -> 90.6 us (0.88)
  waiting for transfers between devices: 22.7 us -> 37.2 us
  starting transfers between devices: 33.5 us -> 21.2 us
  Pallas kernels: 32.9 us -> 26.8 us
  other arithmetic: 7.11 us -> 2.13 us
  local copies, waits for them, and re-layouts: 5.87 us -> 2.76 us
    ppermute x22 -> x20, waiting for transfers between devices: 22.7 us -> 37.2 us  [swap(): lax.ppermute(values, axis, [(index, index ^ mask) for index in range(coun...]
    ppermute x22 -> x20, starting transfers between devices: 33.5 us -> 21.2 us  [swap(): lax.ppermute(values, axis, [(index, index ^ mask) for index in range(coun...]
    pallas_call x2 -> x3, Pallas kernels: 22.4 us -> 18.7 us  [the longest x1 15.7 us: tail(): pl.pallas_call(lambda *refs: tail_kernel(ranks, starts, *refs), out_shape...]
    select_n x1 -> x0, other arithmetic: 2.29 us -> none  [per_device(): jnp.where(visible, (owners ^ myself) * capacity + order_here, -1)]
    unnamed x21 -> x18, local copies, waits for them, and re-layouts: 4.39 us -> 2.72 us
    unnamed x1 -> x0, other arithmetic: 1.45 us -> none
    another operation x2 -> x0, local copies, waits for them, and re-layouts: 1.37 us -> none  [per_device(): blocks = listing.reshape(n_tok, dec_dev)]
  transfers between devices with their start and end apart: 22 -> 20, of which waited for: 11 -> 11; matrix products, arithmetic and copies ran while one was open for 7% -> 2% of each run, Pallas kernels for 7% -> 12%
where the time goes in v3:
time: 90.6 us; the launch traced here: 90.4 us
  waiting for transfers between devices  37.2 us (41%)
  Pallas kernels  26.8 us (30%)
  starting transfers between devices  21.2 us (23%)
  local copies, waits for them, and re-layouts  2.76 us (3%)
  other arithmetic  2.13 us (2%)
    ppermute x20, waiting for transfers between devices, swap(): lax.ppermute(values, axis, [(index, index ^ mask) for index in range(coun...  37.2 us
    ppermute x20, starting transfers between devices, swap(): lax.ppermute(values, axis, [(index, index ^ mask) for index in range(coun...  21.2 us
    pallas_call x1, Pallas kernels, tail(): pl.pallas_call(lambda *refs: tail_kernel(ranks, starts, *refs), out_shape...  15.7 us
    pallas_call x1, Pallas kernels, experts(): pl.pallas_call(lambda *refs: experts_kernel(count, *refs), out_shape=(jax...  3.22 us
    pallas_call x1, Pallas kernels, front(): pl.pallas_call(lambda *refs: front_kernel(orders, *refs), out_shape=(quar...  3.17 us
    unnamed x18, local copies, waits for them, and re-layouts  2.72 us
    pallas_call x1, Pallas kernels, put_in_order(): pl.pallas_call(lambda *refs: order_kernel(ranks, starts, vis_dev, *refs),...  2.2 us
  transfers between devices with their start and end apart: 20, of which 11 were waited for; matrix products, arithmetic and copies ran while one was open for 2% of the time, Pallas kernels for 12%

profile of v3, /device:TPU:0, one launch (start us, length us, event | category | flops | bytes accessed | tf_op | source)
XLA Modules:
  0.0 90.4 jit_solution(6466887880356399239)
XLA Ops:
  0.0 0.5 collective-permute-start.12
  0.5 0.1 collective-permute-start.13
  0.5 1.2 %copy-done.4 = bf16[512,1024]{1,0:T(8,128)(2,1)S(1)} copy-done((bf16[512,1024]{1,0:T(8,128)(2,1)S(1)}, bf16[512,1024]{1,0:T(8,128)(2,1)}, u32[]{:S(2)}) %copy-start.4) | copy-done | bytes 1048600
  1.7 1.2 %copy-done.5 = bf16[1024,512]{1,0:T(8,128)(2,1)S(1)} copy-done((bf16[1024,512]{1,0:T(8,128)(2,1)S(1)}, bf16[1024,512]{1,0:T(8,128)(2,1)}, u32[]{:S(2)}) %copy-start.5) | copy-done | bytes 1048600
  3.0 3.2 %shard_map.91 = (bf16[128,1152]{1,0:T(8,128)(2,1)S(1)}, bf16[128,1152]{1,0:T(8,128)(2,1)S(1)}, bf16[128,1152]{1,0:T(8,128)(2,1)S(1)}, bf16[128,1152]{1,0:T(8,128)(2,1)S(1)}, bf16[512,512]{1,0:T(8,128)(2,1)S(1)}) custom-call(s32[1]{0:T(128)} %bitcast.refs_0_, bf16[512,1024]{1,0:T(8,128)(2,1)S(1)} %copy-done.4, bf16[1024,512]{1,0:T(8,128)(2,1)S(1)} %copy-done.5), custom_call_target="tpu_custom_call" | custom-call | tf_op jit(solution)/shard_map/pallas_call | solution.py:163
  6.1 0.0 copy-done.7
  6.2 0.8 shard_map.92.refs_3_
  7.0 4.1 %collective-permute-start = (bf16[256,512]{1,0:T(8,128)(2,1)S(1)}, bf16[256,512]{1,0:T(8,128)(2,1)S(1)}, u32[]{:S(2)}, u32[]{:S(2)}) collective-permute-start(bf16[256,512]{1,0:T(8,128)(2,1)S(1)} %shard_map.92.refs_3_), channel_id=1, source_target_pairs={{0,4},{1,5},{2,6},{3,7},{4,0},{5,1},{6,2},{7,3},{8,12},{9,13},{10,... | collective-permute-start | bytes 786440 | tf_op jit(solution)/shard_map/ppermute | solution.py:51
  11.1 1.5 %collective-permute-start.7 = (bf16[128,1152]{1,0:T(8,128)(2,1)S(1)}, bf16[128,1152]{1,0:T(8,128)(2,1)S(1)}, u32[]{:S(2)}, u32[]{:S(2)}) collective-permute-start(bf16[128,1152]{1,0:T(8,128)(2,1)S(1)} %get-tuple-element.38), channel_id=1, source_target_pairs={{0,1},{1,0},{2,3},{3,2},{4,5},{5,4},{6,7},{7,6},{8,9},{9,8},{10,11... | collective-permute-start | bytes 884744 | tf_op jit(solution)/shard_map/ppermute | solution.py:51
  12.6 1.6 %collective-permute-start.5 = (bf16[128,1152]{1,0:T(8,128)(2,1)S(1)}, bf16[128,1152]{1,0:T(8,128)(2,1)S(1)}, u32[]{:S(2)}, u32[]{:S(2)}) collective-permute-start(bf16[128,1152]{1,0:T(8,128)(2,1)S(1)} %get-tuple-element.27), channel_id=1, source_target_pairs={{0,2},{1,3},{2,0},{3,1},{4,6},{5,7},{6,4},{7,5},{8,10},{9,11},{10,... | collective-permute-start | bytes 884744 | tf_op jit(solution)/shard_map/ppermute | solution.py:51
  14.2 1.0 %multiply_cosine_fusion = (f32[256,256]{1,0:T(8,128)S(1)}, f32[256,256]{1,0:T(8,128)S(1)}) fusion(f32[256]{0:T(256)S(1)} %multiply_exponential_fusion, f32[256]{0:T(256)S(1)} %iota_convert_fusion), kind=kLoop, calls=%fused_computation.7 | loop fusion | flops 65536 | bytes 526336 | tf_op jit(solution)/shard_map/cos | solution.py:399
  15.2 4.6 %collective-permute-done.7.came_ref = bf16[128,1152]{1,0:T(8,128)(2,1)S(1)} collective-permute-done((bf16[128,1152]{1,0:T(8,128)(2,1)S(1)}, bf16[128,1152]{1,0:T(8,128)(2,1)S(1)}, u32[]{:S(2)}, u32[]{:S(2)}) %collective-permute-start.7) | collective-permute-done | bytes 294944 | tf_op jit(solution)/shard_map/ppermute | solution.py:51
  19.8 0.3 shard_map.96
  20.1 1.6 %collective-permute-start.8 = (bf16[64,1152]{1,0:T(8,128)(2,1)S(1)}, bf16[64,1152]{1,0:T(8,128)(2,1)S(1)}, u32[]{:S(2)}, u32[]{:S(2)}) collective-permute-start(bf16[64,1152]{1,0:T(8,128)(2,1)S(1)} %get-tuple-element.40), channel_id=1, source_target_pairs={{0,2},{1,3},{2,0},{3,1},{4,6},{5,7},{6,4},{7,5},{8,10},{9,11},{10,... | collective-permute-start | bytes 442376 | tf_op jit(solution)/shard_map/ppermute | solution.py:51
  21.8 5.2 %collective-permute-done.5.came_ref = bf16[128,1152]{1,0:T(8,128)(2,1)S(1)} collective-permute-done((bf16[128,1152]{1,0:T(8,128)(2,1)S(1)}, bf16[128,1152]{1,0:T(8,128)(2,1)S(1)}, u32[]{:S(2)}, u32[]{:S(2)}) %collective-permute-start.5) | collective-permute-done | bytes 294944 | tf_op jit(solution)/shard_map/ppermute | solution.py:51
  27.0 0.3 shard_map.94
  27.3 0.2 collective-permute-start.6
  27.5 0.0 collective-permute-done.refs_4_
  27.5 0.0 copy-start.1
  27.6 0.0 copy-start
  27.6 2.0 %collective-permute-start.1 = (bf16[256,512]{1,0:T(8,128)(2,1)S(1)}, bf16[256,512]{1,0:T(8,128)(2,1)S(1)}, u32[]{:S(2)}, u32[]{:S(2)}) collective-permute-start(bf16[256,512]{1,0:T(8,128)(2,1)S(1)} %pad_maximum_fusion.2), channel_id=1, source_target_pairs={{0,1},{1,0},{2,3},{3,2},{4,5},{5,4},{6,7},{7,6},{8,9},{9,8},{10,11... | collective-permute-start | bytes 786440 | tf_op jit(solution)/shard_map/ppermute | solution.py:51
  29.6 0.0 collective-permute-done.8.came_ref
  29.6 0.3 shard_map.97
  29.8 3.2 %collective-permute-done.6.came_ref = bf16[64,1152]{1,0:T(8,128)(2,1)S(1)} collective-permute-done((bf16[64,1152]{1,0:T(8,128)(2,1)S(1)}, bf16[64,1152]{1,0:T(8,128)(2,1)S(1)}, u32[]{:S(2)}, u32[]{:S(2)}) %collective-permute-start.6) | collective-permute-done | bytes 147488 | tf_op jit(solution)/shard_map/ppermute | solution.py:51
  33.0 0.3 shard_map.95
  33.3 0.8 collective-permute-start.9
  34.1 1.4 %collective-permute-start.2 = (bf16[256,512]{1,0:T(8,128)(2,1)S(1)}, bf16[256,512]{1,0:T(8,128)(2,1)S(1)}, u32[]{:S(2)}, u32[]{:S(2)}) collective-permute-start(bf16[256,512]{1,0:T(8,128)(2,1)S(1)} %pad_maximum_fusion.3), channel_id=1, source_target_pairs={{0,2},{1,3},{2,0},{3,1},{4,6},{5,7},{6,4},{7,5},{8,10},{9,11},{10,... | collective-permute-start | bytes 786440 | tf_op jit(solution)/shard_map/ppermute | solution.py:51
  35.5 4.5 %collective-permute-done.9.came_ref = bf16[32,1152]{1,0:T(8,128)(2,1)S(1)} collective-permute-done((bf16[32,1152]{1,0:T(8,128)(2,1)S(1)}, bf16[32,1152]{1,0:T(8,128)(2,1)S(1)}, u32[]{:S(2)}, u32[]{:S(2)}) %collective-permute-start.9) | collective-permute-done | bytes 73760 | tf_op jit(solution)/shard_map/ppermute | solution.py:51
  40.1 0.0 collective-permute-start.10
  40.1 0.1 multiply_sine_fusion.1
  40.2 0.2 shard_map.98
  40.4 5.0 %collective-permute-done.10.came_ref = bf16[32,1152]{1,0:T(8,128)(2,1)S(1)} collective-permute-done((bf16[32,1152]{1,0:T(8,128)(2,1)S(1)}, bf16[32,1152]{1,0:T(8,128)(2,1)S(1)}, u32[]{:S(2)}, u32[]{:S(2)}) %collective-permute-start.10) | collective-permute-done | bytes 73760 | tf_op jit(solution)/shard_map/ppermute | solution.py:51
  45.4 0.2 shard_map.99
  45.7 0.0 collective-permute-done.1.refs_5_
  45.7 0.0 collective-permute-done.2.refs_6_
  45.7 1.6 %collective-permute-start.11 = (bf16[64,1024]{1,0:T(8,128)(2,1)S(1)}, bf16[64,1024]{1,0:T(8,128)(2,1)S(1)}, u32[]{:S(2)}, u32[]{:S(2)}) collective-permute-start(bf16[64,1024]{1,0:T(8,128)(2,1)S(1)} %pad_maximum_fusion.4.refs_0_), channel_id=1, source_target_pairs={{0,16},{8,24},{16,0},{24,8},{1,17},{9,25},{17,1},{25,9},{2,18},{10... | collective-permute-start | bytes 393224 | tf_op jit(solution)/shard_map/ppermute | solution.py:51
  47.3 1.1 %collective-permute-start.4 = (bf16[512,512]{1,0:T(8,128)(2,1)S(1)}, bf16[512,512]{1,0:T(8,128)(2,1)S(1)}, u32[]{:S(2)}, u32[]{:S(2)}) collective-permute-start(bf16[512,512]{1,0:T(8,128)(2,1)S(1)} %pad_maximum_fusion.1), channel_id=1, source_target_pairs={{0,1},{1,0},{2,3},{3,2},{4,5},{5,4},{6,7},{7,6},{8,9},{9,8},{10,11... | collective-permute-start | bytes 1572872 | tf_op jit(solution)/shard_map/ppermute | solution.py:51
  48.4 0.1 collective-permute-start.3
  48.5 2.9 %collective-permute-done.11.refs_1_ = bf16[64,1024]{1,0:T(8,128)(2,1)S(1)} collective-permute-done((bf16[64,1024]{1,0:T(8,128)(2,1)S(1)}, bf16[64,1024]{1,0:T(8,128)(2,1)S(1)}, u32[]{:S(2)}, u32[]{:S(2)}) %collective-permute-start.11) | collective-permute-done | bytes 131104 | tf_op jit(solution)/shard_map/ppermute | solution.py:51
  51.4 0.0 collective-permute-done.12.refs_3_
  51.4 0.0 collective-permute-done.13.refs_5_
  51.4 0.0 copy-done.3
  51.5 3.2 %shard_map.100 = (bf16[64,512]{1,0:T(8,128)(2,1)S(1)}, bf16[64,512]{1,0:T(8,128)(2,1)S(1)}) custom-call(bf16[64,1024]{1,0:T(8,128)(2,1)S(1)} %pad_maximum_fusion.4.refs_0_, bf16[64,1024]{1,0:T(8,128)(2,1)S(1)} %collective-permute-done.11.refs_1_, bf16[1024,1024]{1,0:T(8,128)(2,1)S(1)} %bitcast.6, bf16[1024,1024]{1,0:T(8,128)(2,1)S(1)} %collective-permute-done.12.refs_3_, ...), custom_call_target="tpu_custom_call" | custom-call | tf_op jit(solution)/shard_map/pallas_call | solution.py:232
  54.7 1.6 %collective-permute-start.14 = (bf16[64,512]{1,0:T(8,128)(2,1)S(1)}, bf16[64,512]{1,0:T(8,128)(2,1)S(1)}, u32[]{:S(2)}, u32[]{:S(2)}) collective-permute-start(bf16[64,512]{1,0:T(8,128)(2,1)S(1)} %get-tuple-element.47), channel_id=1, source_target_pairs={{0,16},{8,24},{16,0},{24,8},{1,17},{9,25},{17,1},{25,9},{2,18},{10... | collective-permute-start | bytes 196616 | tf_op jit(solution)/shard_map/ppermute | solution.py:51
  56.3 0.4 multiply_add_fusion
  56.7 0.2 copy-done.8
  57.0 2.1 %collective-permute-done.14 = bf16[64,512]{1,0:T(8,128)(2,1)S(1)} collective-permute-done((bf16[64,512]{1,0:T(8,128)(2,1)S(1)}, bf16[64,512]{1,0:T(8,128)(2,1)S(1)}, u32[]{:S(2)}, u32[]{:S(2)}) %collective-permute-start.14) | collective-permute-done | bytes 65568 | tf_op jit(solution)/shard_map/ppermute | solution.py:51
  59.1 0.0 collective-permute-done.4.refs_8_
  59.1 0.0 collective-permute-done.3.refs_7_
  59.1 0.2 collective-permute-start.15
  59.3 5.2 %collective-permute-done.15.refs_6_ = bf16[64,512]{1,0:T(8,128)(2,1)S(1)} collective-permute-done((bf16[64,512]{1,0:T(8,128)(2,1)S(1)}, bf16[64,512]{1,0:T(8,128)(2,1)S(1)}, u32[]{:S(2)}, u32[]{:S(2)}) %collective-permute-start.15) | collective-permute-done | bytes 65568 | tf_op jit(solution)/shard_map/ppermute | solution.py:51
  64.4 0.1 collective-permute-start.17
  64.5 0.8 collective-permute-start.16
  65.4 3.4 %collective-permute-done.17.refs_8_ = bf16[64,512]{1,0:T(8,128)(2,1)S(1)} collective-permute-done((bf16[64,512]{1,0:T(8,128)(2,1)S(1)}, bf16[64,512]{1,0:T(8,128)(2,1)S(1)}, u32[]{:S(2)}, u32[]{:S(2)}) %collective-permute-start.17) | collective-permute-done | bytes 65568 | tf_op jit(solution)/shard_map/ppermute | solution.py:51
  68.8 0.8 collective-permute-start.19
  69.6 0.0 collective-permute-done.16.refs_7_
  69.6 1.2 %collective-permute-start.18 = (bf16[128,512]{1,0:T(8,128)(2,1)S(1)}, bf16[128,512]{1,0:T(8,128)(2,1)S(1)}, u32[]{:S(2)}, u32[]{:S(2)}) collective-permute-start(bf16[128,512]{1,0:T(8,128)(2,1)S(1)} %pad_maximum_fusion.5), channel_id=1, source_target_pairs={{0,2},{1,3},{2,0},{3,1},{4,6},{5,7},{6,4},{7,5},{8,10},{9,11},{10,... | collective-permute-start | bytes 393224 | tf_op jit(solution)/shard_map/ppermute | solution.py:51
  70.9 0.4 fusion.refs_2_
  71.3 0.0 copy-start.2
  71.3 0.0 copy-start.6
  71.3 2.2 %shard_map.93 = (bf16[2048,512]{1,0:T(8,128)(2,1)S(1)}, bf16[2048,512]{1,0:T(8,128)(2,1)S(1)}) custom-call(s32[1]{0:T(128)} %bitcast.refs_0_, s32[1,2048]{1,0:T(1,128)S(1)} %copy-done.7, bf16[2048,512]{1,0:T(8,128)(2,1)S(1)} %fusion.refs_2_, bf16[256,512]{1,0:T(8,128)(2,1)S(1)} %shard_map.92.refs_3_, bf16[256,512]{1,0:T(8,128)(2,1)S(1)} %collective-permute-done.refs_4_, ...), custom_call_target="tpu_custom_call" | custom-call | tf_op jit(solution)/shard_map/pallas_call | solution.py:308
  73.5 0.3 collective-permute-done.19.refs_10_
  73.8 0.9 collective-permute-done.18.refs_9_
  74.7 15.7 %shard_map.101 = bf16[256,512]{1,0:T(8,128)(2,1)} custom-call(s32[1]{0:T(128)} %bitcast.refs_0_, bf16[2048,512]{1,0:T(8,128)(2,1)S(1)} %get-tuple-element.30.refs_1_, bf16[2048,512]{1,0:T(8,128)(2,1)S(1)} %get-tuple-element.31.refs_2_, bf16[512,1536]{1,0:T(8,128)(2,1)S(1)} %copy-done.2, bf16[512,512]{1,0:T(8,128)(2,1)S(1)} %copy-done.6, ...), custom_call_target="tpu_custom_call" | custom-call | tf_op jit(solution)/shard_map/pallas_call | solution.py:378
  (27 shorter events, 0.2 us)
Async XLA Ops:
  0.0 6.2 %copy-start.7 = (s32[1,2048]{1,0:T(1,128)S(1)}, s32[1,2048]{1,0:T(1,128)}, u32[]{:S(2)}) copy-start(s32[1,2048]{1,0:T(1,128)} %refs_1_.5) | copy-start | bytes 24580
  0.0 51.4 %collective-permute-start.12 = (bf16[1024,1024]{1,0:T(8,128)(2,1)}, bf16[1024,1024]{1,0:T(8,128)(2,1)S(1)}, u32[]{:S(2)}, u32[]{:S(2)}) collective-permute-start(bf16[1024,1024]{1,0:T(8,128)(2,1)} %bitcast.5), channel_id=1, source_target_pairs={{0,8},{8,0},{16,24},{24,16},{1,9},{9,1},{17,25},{25,17},{2,10},{10... | collective-permute-start | bytes 6291464 | tf_op jit(solution)/shard_map/ppermute | solution.py:51
  0.5 51.0 %collective-permute-start.13 = (bf16[1024,1024]{1,0:T(8,128)(2,1)}, bf16[1024,1024]{1,0:T(8,128)(2,1)}, u32[]{:S(2)}, u32[]{:S(2)}) collective-permute-start(bf16[1024,1024]{1,0:T(8,128)(2,1)} %bitcast.7), channel_id=1, source_target_pairs={{0,8},{8,0},{16,24},{24,16},{1,9},{9,1},{17,25},{25,17},{2,10},{10... | collective-permute-start | bytes 6291464 | tf_op jit(solution)/shard_map/ppermute | solution.py:51
  0.5 1.2 %copy-start.4 = (bf16[512,1024]{1,0:T(8,128)(2,1)S(1)}, bf16[512,1024]{1,0:T(8,128)(2,1)}, u32[]{:S(2)}) copy-start(bf16[512,1024]{1,0:T(8,128)(2,1)} %refs_1_.3) | copy-start | bytes 3145732
  1.7 1.2 %copy-start.5 = (bf16[1024,512]{1,0:T(8,128)(2,1)S(1)}, bf16[1024,512]{1,0:T(8,128)(2,1)}, u32[]{:S(2)}) copy-start(bf16[1024,512]{1,0:T(8,128)(2,1)} %refs_2_.1) | copy-start | bytes 3145732
  7.0 20.5 %collective-permute-start = (bf16[256,512]{1,0:T(8,128)(2,1)S(1)}, bf16[256,512]{1,0:T(8,128)(2,1)S(1)}, u32[]{:S(2)}, u32[]{:S(2)}) collective-permute-start(bf16[256,512]{1,0:T(8,128)(2,1)S(1)} %shard_map.92.refs_3_), channel_id=1, source_target_pairs={{0,4},{1,5},{2,6},{3,7},{4,0},{5,1},{6,2},{7,3},{8,12},{9,13},{10,... | collective-permute-start | bytes 786440 | tf_op jit(solution)/shard_map/ppermute | solution.py:51
  11.1 8.7 %collective-permute-start.7 = (bf16[128,1152]{1,0:T(8,128)(2,1)S(1)}, bf16[128,1152]{1,0:T(8,128)(2,1)S(1)}, u32[]{:S(2)}, u32[]{:S(2)}) collective-permute-start(bf16[128,1152]{1,0:T(8,128)(2,1)S(1)} %get-tuple-element.38), channel_id=1, source_target_pairs={{0,1},{1,0},{2,3},{3,2},{4,5},{5,4},{6,7},{7,6},{8,9},{9,8},{10,11... | collective-permute-start | bytes 884744 | tf_op jit(solution)/shard_map/ppermute | solution.py:51
  12.6 14.4 %collective-permute-start.5 = (bf16[128,1152]{1,0:T(8,128)(2,1)S(1)}, bf16[128,1152]{1,0:T(8,128)(2,1)S(1)}, u32[]{:S(2)}, u32[]{:S(2)}) collective-permute-start(bf16[128,1152]{1,0:T(8,128)(2,1)S(1)} %get-tuple-element.27), channel_id=1, source_target_pairs={{0,2},{1,3},{2,0},{3,1},{4,6},{5,7},{6,4},{7,5},{8,10},{9,11},{10,... | collective-permute-start | bytes 884744 | tf_op jit(solution)/shard_map/ppermute | solution.py:51
  20.1 9.5 %collective-permute-start.8 = (bf16[64,1152]{1,0:T(8,128)(2,1)S(1)}, bf16[64,1152]{1,0:T(8,128)(2,1)S(1)}, u32[]{:S(2)}, u32[]{:S(2)}) collective-permute-start(bf16[64,1152]{1,0:T(8,128)(2,1)S(1)} %get-tuple-element.40), channel_id=1, source_target_pairs={{0,2},{1,3},{2,0},{3,1},{4,6},{5,7},{6,4},{7,5},{8,10},{9,11},{10,... | collective-permute-start | bytes 442376 | tf_op jit(solution)/shard_map/ppermute | solution.py:51
  27.0 24.5 %copy-start.3 = (bf16[1024,512]{1,0:T(8,128)(2,1)S(1)}, bf16[1024,512]{1,0:T(8,128)(2,1)}, u32[]{:S(2)}) copy-start(bf16[1024,512]{1,0:T(8,128)(2,1)} %refs_6_.1) | copy-start | bytes 3145732
  27.3 5.7 %collective-permute-start.6 = (bf16[64,1152]{1,0:T(8,128)(2,1)S(1)}, bf16[64,1152]{1,0:T(8,128)(2,1)S(1)}, u32[]{:S(2)}, u32[]{:S(2)}) collective-permute-start(bf16[64,1152]{1,0:T(8,128)(2,1)S(1)} %get-tuple-element.34), channel_id=1, source_target_pairs={{0,1},{1,0},{2,3},{3,2},{4,5},{5,4},{6,7},{7,6},{8,9},{9,8},{10,11... | collective-permute-start | bytes 442376 | tf_op jit(solution)/shard_map/ppermute | solution.py:51
  27.5 23.9 %copy-start.1 = (bf16[1,1024,1024]{2,1,0:T(8,128)(2,1)S(1)}, bf16[1,1024,1024]{2,1,0:T(8,128)(2,1)}, u32[]{:S(2)}) copy-start(bf16[1,1024,1024]{2,1,0:T(8,128)(2,1)} %param.12) | copy-start | bytes 6291460
  27.6 23.9 %copy-start = (bf16[1,1024,1024]{2,1,0:T(8,128)(2,1)S(1)}, bf16[1,1024,1024]{2,1,0:T(8,128)(2,1)}, u32[]{:S(2)}) copy-start(bf16[1,1024,1024]{2,1,0:T(8,128)(2,1)} %param.11) | copy-start | bytes 6291460
  27.6 18.1 %collective-permute-start.1 = (bf16[256,512]{1,0:T(8,128)(2,1)S(1)}, bf16[256,512]{1,0:T(8,128)(2,1)S(1)}, u32[]{:S(2)}, u32[]{:S(2)}) collective-permute-start(bf16[256,512]{1,0:T(8,128)(2,1)S(1)} %pad_maximum_fusion.2), channel_id=1, source_target_pairs={{0,1},{1,0},{2,3},{3,2},{4,5},{5,4},{6,7},{7,6},{8,9},{9,8},{10,11... | collective-permute-start | bytes 786440 | tf_op jit(solution)/shard_map/ppermute | solution.py:51
  33.3 6.8 %collective-permute-start.9 = (bf16[32,1152]{1,0:T(8,128)(2,1)S(1)}, bf16[32,1152]{1,0:T(8,128)(2,1)S(1)}, u32[]{:S(2)}, u32[]{:S(2)}) collective-permute-start(bf16[32,1152]{1,0:T(8,128)(2,1)S(1)} %get-tuple-element.42), channel_id=1, source_target_pairs={{0,4},{1,5},{2,6},{3,7},{4,0},{5,1},{6,2},{7,3},{8,12},{9,13},{10,... | collective-permute-start | bytes 221192 | tf_op jit(solution)/shard_map/ppermute | solution.py:51
  34.1 11.6 %collective-permute-start.2 = (bf16[256,512]{1,0:T(8,128)(2,1)S(1)}, bf16[256,512]{1,0:T(8,128)(2,1)S(1)}, u32[]{:S(2)}, u32[]{:S(2)}) collective-permute-start(bf16[256,512]{1,0:T(8,128)(2,1)S(1)} %pad_maximum_fusion.3), channel_id=1, source_target_pairs={{0,2},{1,3},{2,0},{3,1},{4,6},{5,7},{6,4},{7,5},{8,10},{9,11},{10,... | collective-permute-start | bytes 786440 | tf_op jit(solution)/shard_map/ppermute | solution.py:51
  40.1 5.4 %collective-permute-start.10 = (bf16[32,1152]{1,0:T(8,128)(2,1)S(1)}, bf16[32,1152]{1,0:T(8,128)(2,1)S(1)}, u32[]{:S(2)}, u32[]{:S(2)}) collective-permute-start(bf16[32,1152]{1,0:T(8,128)(2,1)S(1)} %get-tuple-element.44), channel_id=1, source_target_pairs={{0,4},{1,5},{2,6},{3,7},{4,0},{5,1},{6,2},{7,3},{8,12},{9,13},{10,... | collective-permute-start | bytes 221192 | tf_op jit(solution)/shard_map/ppermute | solution.py:51
  45.7 5.7 %collective-permute-start.11 = (bf16[64,1024]{1,0:T(8,128)(2,1)S(1)}, bf16[64,1024]{1,0:T(8,128)(2,1)S(1)}, u32[]{:S(2)}, u32[]{:S(2)}) collective-permute-start(bf16[64,1024]{1,0:T(8,128)(2,1)S(1)} %pad_maximum_fusion.4.refs_0_), channel_id=1, source_target_pairs={{0,16},{8,24},{16,0},{24,8},{1,17},{9,25},{17,1},{25,9},{2,18},{10... | collective-permute-start | bytes 393224 | tf_op jit(solution)/shard_map/ppermute | solution.py:51
  47.3 11.7 %collective-permute-start.4 = (bf16[512,512]{1,0:T(8,128)(2,1)S(1)}, bf16[512,512]{1,0:T(8,128)(2,1)S(1)}, u32[]{:S(2)}, u32[]{:S(2)}) collective-permute-start(bf16[512,512]{1,0:T(8,128)(2,1)S(1)} %pad_maximum_fusion.1), channel_id=1, source_target_pairs={{0,1},{1,0},{2,3},{3,2},{4,5},{5,4},{6,7},{7,6},{8,9},{9,8},{10,11... | collective-permute-start | bytes 1572872 | tf_op jit(solution)/shard_map/ppermute | solution.py:51
  48.4 10.6 %collective-permute-start.3 = (bf16[512,512]{1,0:T(8,128)(2,1)S(1)}, bf16[512,512]{1,0:T(8,128)(2,1)S(1)}, u32[]{:S(2)}, u32[]{:S(2)}) collective-permute-start(bf16[512,512]{1,0:T(8,128)(2,1)S(1)} %pad_maximum_fusion), channel_id=1, source_target_pairs={{0,2},{1,3},{2,0},{3,1},{4,6},{5,7},{6,4},{7,5},{8,10},{9,11},{10,... | collective-permute-start | bytes 1572872 | tf_op jit(solution)/shard_map/ppermute | solution.py:51
  54.7 4.3 %collective-permute-start.14 = (bf16[64,512]{1,0:T(8,128)(2,1)S(1)}, bf16[64,512]{1,0:T(8,128)(2,1)S(1)}, u32[]{:S(2)}, u32[]{:S(2)}) collective-permute-start(bf16[64,512]{1,0:T(8,128)(2,1)S(1)} %get-tuple-element.47), channel_id=1, source_target_pairs={{0,16},{8,24},{16,0},{24,8},{1,17},{9,25},{17,1},{25,9},{2,18},{10... | collective-permute-start | bytes 196616 | tf_op jit(solution)/shard_map/ppermute | solution.py:51
  56.3 0.7 copy-start.8
  59.1 5.3 %collective-permute-start.15 = (bf16[64,512]{1,0:T(8,128)(2,1)S(1)}, bf16[64,512]{1,0:T(8,128)(2,1)S(1)}, u32[]{:S(2)}, u32[]{:S(2)}) collective-permute-start(bf16[64,512]{1,0:T(8,128)(2,1)S(1)} %add_convert_fusion.refs_5_), channel_id=1, source_target_pairs={{0,4},{1,5},{2,6},{3,7},{4,0},{5,1},{6,2},{7,3},{8,12},{9,13},{10,... | collective-permute-start | bytes 196616 | tf_op jit(solution)/shard_map/ppermute | solution.py:51
  64.4 4.3 %collective-permute-start.17 = (bf16[64,512]{1,0:T(8,128)(2,1)S(1)}, bf16[64,512]{1,0:T(8,128)(2,1)S(1)}, u32[]{:S(2)}, u32[]{:S(2)}) collective-permute-start(bf16[64,512]{1,0:T(8,128)(2,1)S(1)} %pad_maximum_fusion.8), channel_id=1, source_target_pairs={{0,2},{1,3},{2,0},{3,1},{4,6},{5,7},{6,4},{7,5},{8,10},{9,11},{10,... | collective-permute-start | bytes 196616 | tf_op jit(solution)/shard_map/ppermute | solution.py:51
  64.5 5.1 %collective-permute-start.16 = (bf16[64,512]{1,0:T(8,128)(2,1)S(1)}, bf16[64,512]{1,0:T(8,128)(2,1)S(1)}, u32[]{:S(2)}, u32[]{:S(2)}) collective-permute-start(bf16[64,512]{1,0:T(8,128)(2,1)S(1)} %pad_maximum_fusion.7), channel_id=1, source_target_pairs={{0,1},{1,0},{2,3},{3,2},{4,5},{5,4},{6,7},{7,6},{8,9},{9,8},{10,11... | collective-permute-start | bytes 196616 | tf_op jit(solution)/shard_map/ppermute | solution.py:51
  68.8 5.0 %collective-permute-start.19 = (bf16[128,512]{1,0:T(8,128)(2,1)S(1)}, bf16[128,512]{1,0:T(8,128)(2,1)S(1)}, u32[]{:S(2)}, u32[]{:S(2)}) collective-permute-start(bf16[128,512]{1,0:T(8,128)(2,1)S(1)} %pad_maximum_fusion.6), channel_id=1, source_target_pairs={{0,1},{1,0},{2,3},{3,2},{4,5},{5,4},{6,7},{7,6},{8,9},{9,8},{10,11... | collective-permute-start | bytes 393224 | tf_op jit(solution)/shard_map/ppermute | solution.py:51
  69.6 5.0 %collective-permute-start.18 = (bf16[128,512]{1,0:T(8,128)(2,1)S(1)}, bf16[128,512]{1,0:T(8,128)(2,1)S(1)}, u32[]{:S(2)}, u32[]{:S(2)}) collective-permute-start(bf16[128,512]{1,0:T(8,128)(2,1)S(1)} %pad_maximum_fusion.5), channel_id=1, source_target_pairs={{0,2},{1,3},{2,0},{3,1},{4,6},{5,7},{6,4},{7,5},{8,10},{9,11},{10,... | collective-permute-start | bytes 393224 | tf_op jit(solution)/shard_map/ppermute | solution.py:51
  71.3 3.4 %copy-start.2 = (bf16[512,1536]{1,0:T(8,128)(2,1)S(1)}, bf16[512,1536]{1,0:T(8,128)(2,1)}, u32[]{:S(2)}) copy-start(bf16[512,1536]{1,0:T(8,128)(2,1)} %refs_3_.1) | copy-start | bytes 4718596
  71.3 3.4 %copy-start.6 = (bf16[512,512]{1,0:T(8,128)(2,1)S(1)}, bf16[512,512]{1,0:T(8,128)(2,1)}, u32[]{:S(2)}) copy-start(bf16[512,512]{1,0:T(8,128)(2,1)} %refs_4_.1) | copy-start | bytes 1572868

commit v4 on v3

--- a/solution.py
+++ b/solution.py
@@ -175,7 +175,7 @@
             pltpu.SemaphoreType.DMA((2, pieces)),
         ],
         compiler_params=pltpu.CompilerParams(vmem_limit_bytes=28 << 20),
-    )(place, tokens, slot_keys)
+    )(place, *(pltpu.with_memory_space_constraint(array, pltpu.HBM) for array in (tokens, slot_keys)))
 
 
 def merge_kernel(kept_ref, came_ref, *outs):
@@ -213,13 +213,24 @@
 
 
 def experts_kernel(count, *refs):
-    rows_refs, (in_a, in_b, back_a, back_b, proj_ref), outs = refs[:count], refs[count : count + 5], refs[count + 5 :]
+    rows_refs, (in_a, in_b, back_a, back_b, proj_ref), refs = refs[:count], refs[count : count + 5], refs[count + 5 :]
+    outs, (in_ref, back_ref, sems) = refs[:count], refs[count:]
+    copies = [
+        pltpu.make_async_copy(source, target, sems.at[index])
+        for index, (source, target) in enumerate(((in_b, in_ref), (back_b, back_ref)))
+    ]
+    for copy in copies:
+        copy.start()
     rows = jnp.concatenate([ref[...] for ref in rows_refs], axis=0)
-    total = None
-    for first_ref, second_ref in ((in_a, back_a), (in_b, back_b)):
-        hidden = jax.nn.gelu(jnp.dot(rows, first_ref[...], preferred_element_type=F32)).astype(BF16)
-        part = jnp.dot(hidden, second_ref[...], preferred_element_type=F32)
-        total = part if total is None else total + part
+
+    def hidden(weights):
+        return jax.nn.gelu(jnp.dot(rows, weights, preferred_element_type=F32)).astype(BF16)
+
+    total = jnp.dot(hidden(in_a[...]), back_a[...], preferred_element_type=F32)
+    copies[0].wait()
+    other = hidden(in_ref[...])
+    copies[1].wait()
+    total = total + jnp.dot(other, back_ref[...], preferred_element_type=F32)
     result = jnp.dot(total.astype(BF16), proj_ref[...], preferred_element_type=F32).astype(BF16)
     step = rows_refs[0].shape[0]
     for index, out_ref in enumerate(outs):
@@ -232,9 +243,14 @@
     return pl.pallas_call(
         lambda *refs: experts_kernel(count, *refs),
         out_shape=(jax.ShapeDtypeStruct((rows, w_proj.shape[1]), BF16),) * count,
-        in_specs=[VMEM] * (count + 5),
+        in_specs=[VMEM] * count + [VMEM, HBM, VMEM, HBM, VMEM],
         out_specs=(VMEM,) * count,
-        compiler_params=pltpu.CompilerParams(vmem_limit_bytes=16 << 20),
+        scratch_shapes=[
+            pltpu.VMEM(first.shape, BF16),
+            pltpu.VMEM(second.shape, BF16),
+            pltpu.SemaphoreType.DMA((2,)),
+        ],
+        compiler_params=pltpu.CompilerParams(vmem_limit_bytes=20 << 20),
     )(*slot_rows, first, first_other, second, second_other, w_proj)
 
 
@@ -424,18 +440,16 @@
 
     outgoing = pick(place, dec_source, combine, n_tok)
     arrays, starts, brought = gather_pair(outgoing, "tok", back_orders)
-    (late_mask,) = tie([mask_token], [quarters[1]])
-    filler = (late_mask.astype(F32)[None, :] + sinusoid_table(dec_total, dec_dev, dec_width)).astype(BF16)
+    filler = (mask_token.astype(F32)[None, :] + sinusoid_table(dec_total, dec_dev, dec_width)).astype(BF16)
     ordered, filler = put_in_order(place, dec_source, filler, arrays, starts, ranks, vis_dev)
 
     state = [(quarters[0], quarters[1]), (quarters[2], quarters[3])]
     for step in range(steps):
-        last = step == steps - 1
         sent = [state[path][1] for path in range(2)]
-        if last:
+        if step == 1:
             sent = tie(sent, brought[0])
         arrived = [swap(sent[path], "tok", 1 << orders[path][step]) for path in range(2)]
-        state = [merge(state[path][0], arrived[path], last) for path in range(2)]
+        state = [merge(state[path][0], arrived[path], step == steps - 1) for path in range(2)]
     slot_in = jnp.concatenate(state, axis=0)
 
     (slot_in,) = tie([slot_in], [array for group in brought[1:-1] for array in group])

time: 90.6 us -> 88.9 us (0.981)
  starting transfers between devices: 21.2 us -> 25.7 us
  waiting for transfers between devices: 37.2 us -> 32.7 us
  local copies, waits for them, and re-layouts: 2.76 us -> 0.32 us
    ppermute x20, waiting for transfers between devices: 37.2 us -> 32.7 us  [swap(): lax.ppermute(values, axis, [(index, index ^ mask) for index in range(coun...]
    ppermute x20, starting transfers between devices: 21.2 us -> 25.7 us  [swap(): lax.ppermute(values, axis, [(index, index ^ mask) for index in range(coun...]
    unnamed x18 -> x14, local copies, waits for them, and re-layouts: 2.72 us -> 0.27 us
  transfers between devices with their start and end apart: 20 -> 20, of which waited for: 11 -> 11; matrix products, arithmetic and copies ran while one was open for 2% -> 2% of each run, Pallas kernels for 12% -> 13%
where the time goes in v4:
time: 88.9 us; the launch traced here: 88.7 us
  waiting for transfers between devices  32.7 us (37%)
  Pallas kernels  27.6 us (31%)
  starting transfers between devices  25.7 us (29%)
  other arithmetic  2.12 us (2%)
    ppermute x20, waiting for transfers between devices, swap(): lax.ppermute(values, axis, [(index, index ^ mask) for index in range(coun...  32.7 us
    ppermute x20, starting transfers between devices, swap(): lax.ppermute(values, axis, [(index, index ^ mask) for index in range(coun...  25.7 us
    pallas_call x1, Pallas kernels, tail(): pl.pallas_call(lambda *refs: tail_kernel(ranks, starts, *refs), out_shape...  15.8 us
    pallas_call x1, Pallas kernels, front(): pl.pallas_call(lambda *refs: front_kernel(orders, *refs), out_shape=(quar...  3.98 us
    pallas_call x1, Pallas kernels, experts(): pl.pallas_call(lambda *refs: experts_kernel(count, *refs), out_shape=(jax...  3.09 us
    pallas_call x1, Pallas kernels, put_in_order(): pl.pallas_call(lambda *refs: order_kernel(ranks, starts, vis_dev, *refs),...  2.2 us
  transfers between devices with their start and end apart: 20, of which 11 were waited for; matrix products, arithmetic and copies ran while one was open for 2% of the time, Pallas kernels for 13%

profile of v4, /device:TPU:0, one launch (start us, length us, event | category | flops | bytes accessed | tf_op | source)
XLA Modules:
  0.0 88.7 jit_solution(7773390321136075608)
XLA Ops:
  0.0 0.5 collective-permute-start.12
  0.5 0.1 collective-permute-start.13
  0.5 4.0 %shard_map.91 = (bf16[128,1152]{1,0:T(8,128)(2,1)S(1)}, bf16[128,1152]{1,0:T(8,128)(2,1)S(1)}, bf16[128,1152]{1,0:T(8,128)(2,1)S(1)}, bf16[128,1152]{1,0:T(8,128)(2,1)S(1)}, bf16[512,512]{1,0:T(8,128)(2,1)S(1)}) custom-call(s32[1]{0:T(128)} %bitcast.refs_0_, bf16[512,1024]{1,0:T(8,128)(2,1)} %refs_1_.3, bf16[1024,512]{1,0:T(8,128)(2,1)} %refs_2_.1), custom_call_target="tpu_custom_call" | custom-call | tf_op jit(solution)/shard_map/pallas_call | solution.py:163
  4.5 0.0 copy-done.5
  4.5 0.8 shard_map.92.refs_3_
  5.3 4.1 %collective-permute-start = (bf16[256,512]{1,0:T(8,128)(2,1)S(1)}, bf16[256,512]{1,0:T(8,128)(2,1)S(1)}, u32[]{:S(2)}, u32[]{:S(2)}) collective-permute-start(bf16[256,512]{1,0:T(8,128)(2,1)S(1)} %shard_map.92.refs_3_), channel_id=1, source_target_pairs={{0,4},{1,5},{2,6},{3,7},{4,0},{5,1},{6,2},{7,3},{8,12},{9,13},{10,... | collective-permute-start | bytes 786440 | tf_op jit(solution)/shard_map/ppermute | solution.py:51
  9.4 1.6 %collective-permute-start.5 = (bf16[128,1152]{1,0:T(8,128)(2,1)S(1)}, bf16[128,1152]{1,0:T(8,128)(2,1)S(1)}, u32[]{:S(2)}, u32[]{:S(2)}) collective-permute-start(bf16[128,1152]{1,0:T(8,128)(2,1)S(1)} %get-tuple-element.30), channel_id=1, source_target_pairs={{0,2},{1,3},{2,0},{3,1},{4,6},{5,7},{6,4},{7,5},{8,10},{9,11},{10,... | collective-permute-start | bytes 884744 | tf_op jit(solution)/shard_map/ppermute | solution.py:51
  11.0 1.5 %collective-permute-start.6 = (bf16[128,1152]{1,0:T(8,128)(2,1)S(1)}, bf16[128,1152]{1,0:T(8,128)(2,1)S(1)}, u32[]{:S(2)}, u32[]{:S(2)}) collective-permute-start(bf16[128,1152]{1,0:T(8,128)(2,1)S(1)} %get-tuple-element.34), channel_id=1, source_target_pairs={{0,1},{1,0},{2,3},{3,2},{4,5},{5,4},{6,7},{7,6},{8,9},{9,8},{10,11... | collective-permute-start | bytes 884744 | tf_op jit(solution)/shard_map/ppermute | solution.py:51
  12.6 1.0 %multiply_cosine_fusion = (f32[256,256]{1,0:T(8,128)S(1)}, f32[256,256]{1,0:T(8,128)S(1)}) fusion(f32[256]{0:T(256)S(1)} %multiply_exponential_fusion, f32[256]{0:T(256)S(1)} %iota_convert_fusion), kind=kLoop, calls=%fused_computation.7 | loop fusion | flops 65536 | bytes 526336 | tf_op jit(solution)/shard_map/cos | solution.py:415
  13.6 9.0 %collective-permute-done.5.came_ref = bf16[128,1152]{1,0:T(8,128)(2,1)S(1)} collective-permute-done((bf16[128,1152]{1,0:T(8,128)(2,1)S(1)}, bf16[128,1152]{1,0:T(8,128)(2,1)S(1)}, u32[]{:S(2)}, u32[]{:S(2)}) %collective-permute-start.5) | collective-permute-done | bytes 294944 | tf_op jit(solution)/shard_map/ppermute | solution.py:51
  22.6 0.3 shard_map.94
  22.9 0.0 collective-permute-done.6.came_ref
  22.9 0.0 copy-start.3
  22.9 0.3 shard_map.95
  23.3 0.0 collective-permute-done.refs_4_
  23.3 1.6 %collective-permute-start.7 = (bf16[64,1152]{1,0:T(8,128)(2,1)S(1)}, bf16[64,1152]{1,0:T(8,128)(2,1)S(1)}, u32[]{:S(2)}, u32[]{:S(2)}) collective-permute-start(bf16[64,1152]{1,0:T(8,128)(2,1)S(1)} %get-tuple-element.36), channel_id=1, source_target_pairs={{0,1},{1,0},{2,3},{3,2},{4,5},{5,4},{6,7},{7,6},{8,9},{9,8},{10,11... | collective-permute-start | bytes 442376 | tf_op jit(solution)/shard_map/ppermute | solution.py:51
  25.0 1.5 %collective-permute-start.9 = (bf16[64,1152]{1,0:T(8,128)(2,1)S(1)}, bf16[64,1152]{1,0:T(8,128)(2,1)S(1)}, u32[]{:S(2)}, u32[]{:S(2)}) collective-permute-start(bf16[64,1152]{1,0:T(8,128)(2,1)S(1)} %get-tuple-element.40), channel_id=1, source_target_pairs={{0,2},{1,3},{2,0},{3,1},{4,6},{5,7},{6,4},{7,5},{8,10},{9,11},{10,... | collective-permute-start | bytes 442376 | tf_op jit(solution)/shard_map/ppermute | solution.py:51
  26.5 0.0 copy-start
  26.5 0.6 collective-permute-start.1
  27.1 2.1 %collective-permute-done.7.came_ref = bf16[64,1152]{1,0:T(8,128)(2,1)S(1)} collective-permute-done((bf16[64,1152]{1,0:T(8,128)(2,1)S(1)}, bf16[64,1152]{1,0:T(8,128)(2,1)S(1)}, u32[]{:S(2)}, u32[]{:S(2)}) %collective-permute-start.7) | collective-permute-done | bytes 147488 | tf_op jit(solution)/shard_map/ppermute | solution.py:51
  29.2 0.3 shard_map.96
  29.5 1.2 %collective-permute-start.8 = (bf16[32,1152]{1,0:T(8,128)(2,1)S(1)}, bf16[32,1152]{1,0:T(8,128)(2,1)S(1)}, u32[]{:S(2)}, u32[]{:S(2)}) collective-permute-start(bf16[32,1152]{1,0:T(8,128)(2,1)S(1)} %get-tuple-element.38), channel_id=1, source_target_pairs={{0,4},{1,5},{2,6},{3,7},{4,0},{5,1},{6,2},{7,3},{8,12},{9,13},{10,... | collective-permute-start | bytes 221192 | tf_op jit(solution)/shard_map/ppermute | solution.py:51
  30.7 0.2 collective-permute-done.9.came_ref
  31.0 1.8 %collective-permute-start.2 = (bf16[256,512]{1,0:T(8,128)(2,1)S(1)}, bf16[256,512]{1,0:T(8,128)(2,1)S(1)}, u32[]{:S(2)}, u32[]{:S(2)}) collective-permute-start(bf16[256,512]{1,0:T(8,128)(2,1)S(1)} %pad_maximum_fusion.3), channel_id=1, source_target_pairs={{0,2},{1,3},{2,0},{3,1},{4,6},{5,7},{6,4},{7,5},{8,10},{9,11},{10,... | collective-permute-start | bytes 786440 | tf_op jit(solution)/shard_map/ppermute | solution.py:51
  32.8 0.3 shard_map.98
  33.1 2.3 %collective-permute-done.8.came_ref = bf16[32,1152]{1,0:T(8,128)(2,1)S(1)} collective-permute-done((bf16[32,1152]{1,0:T(8,128)(2,1)S(1)}, bf16[32,1152]{1,0:T(8,128)(2,1)S(1)}, u32[]{:S(2)}, u32[]{:S(2)}) %collective-permute-start.8) | collective-permute-done | bytes 73760 | tf_op jit(solution)/shard_map/ppermute | solution.py:51
  35.3 1.4 %collective-permute-start.10 = (bf16[32,1152]{1,0:T(8,128)(2,1)S(1)}, bf16[32,1152]{1,0:T(8,128)(2,1)S(1)}, u32[]{:S(2)}, u32[]{:S(2)}) collective-permute-start(bf16[32,1152]{1,0:T(8,128)(2,1)S(1)} %get-tuple-element.42), channel_id=1, source_target_pairs={{0,4},{1,5},{2,6},{3,7},{4,0},{5,1},{6,2},{7,3},{8,12},{9,13},{10,... | collective-permute-start | bytes 221192 | tf_op jit(solution)/shard_map/ppermute | solution.py:51
  36.7 0.1 multiply_sine_fusion.1
  36.8 0.2 shard_map.97
  37.1 3.5 %collective-permute-done.10.came_ref = bf16[32,1152]{1,0:T(8,128)(2,1)S(1)} collective-permute-done((bf16[32,1152]{1,0:T(8,128)(2,1)S(1)}, bf16[32,1152]{1,0:T(8,128)(2,1)S(1)}, u32[]{:S(2)}, u32[]{:S(2)}) %collective-permute-start.10) | collective-permute-done | bytes 73760 | tf_op jit(solution)/shard_map/ppermute | solution.py:51
  40.6 0.2 shard_map.99
  40.9 0.0 collective-permute-done.1.refs_5_
  40.9 0.0 collective-permute-done.2.refs_6_
  40.9 1.9 %collective-permute-start.11 = (bf16[64,1024]{1,0:T(8,128)(2,1)S(1)}, bf16[64,1024]{1,0:T(8,128)(2,1)S(1)}, u32[]{:S(2)}, u32[]{:S(2)}) collective-permute-start(bf16[64,1024]{1,0:T(8,128)(2,1)S(1)} %pad_maximum_fusion.4.refs_0_), channel_id=1, source_target_pairs={{0,16},{8,24},{16,0},{24,8},{1,17},{9,25},{17,1},{25,9},{2,18},{10... | collective-permute-start | bytes 393224 | tf_op jit(solution)/shard_map/ppermute | solution.py:51
  42.8 4.0 %collective-permute-start.4 = (bf16[512,512]{1,0:T(8,128)(2,1)S(1)}, bf16[512,512]{1,0:T(8,128)(2,1)S(1)}, u32[]{:S(2)}, u32[]{:S(2)}) collective-permute-start(bf16[512,512]{1,0:T(8,128)(2,1)S(1)} %pad_maximum_fusion.1), channel_id=1, source_target_pairs={{0,1},{1,0},{2,3},{3,2},{4,5},{5,4},{6,7},{7,6},{8,9},{9,8},{10,11... | collective-permute-start | bytes 1572872 | tf_op jit(solution)/shard_map/ppermute | solution.py:51
  46.8 0.1 collective-permute-start.3
  46.9 0.0 collective-permute-done.11.refs_1_
  46.9 0.0 collective-permute-done.12.refs_3_
  46.9 0.0 collective-permute-done.13.refs_5_
  46.9 0.0 copy-done.3
  46.9 0.0 copy-done.1
  46.9 0.0 copy-done
  46.9 3.1 %shard_map.100 = (bf16[64,512]{1,0:T(8,128)(2,1)S(1)}, bf16[64,512]{1,0:T(8,128)(2,1)S(1)}) custom-call(bf16[64,1024]{1,0:T(8,128)(2,1)S(1)} %pad_maximum_fusion.4.refs_0_, bf16[64,1024]{1,0:T(8,128)(2,1)S(1)} %collective-permute-done.11.refs_1_, bf16[1024,1024]{1,0:T(8,128)(2,1)S(1)} %bitcast.6, bf16[1024,1024]{1,0:T(8,128)(2,1)S(1)} %collective-permute-done.12.refs_3_, ...), custom_call_target="tpu_custom_call" | custom-call | tf_op jit(solution)/shard_map/pallas_call | solution.py:243
  50.0 0.9 %collective-permute-start.14 = (bf16[64,512]{1,0:T(8,128)(2,1)S(1)}, bf16[64,512]{1,0:T(8,128)(2,1)S(1)}, u32[]{:S(2)}, u32[]{:S(2)}) collective-permute-start(bf16[64,512]{1,0:T(8,128)(2,1)S(1)} %get-tuple-element.45), channel_id=1, source_target_pairs={{0,16},{8,24},{16,0},{24,8},{1,17},{9,25},{17,1},{25,9},{2,18},{10... | collective-permute-start | bytes 196616 | tf_op jit(solution)/shard_map/ppermute | solution.py:51
  50.9 0.4 multiply_add_fusion
  51.4 0.2 copy-done.6
  51.6 2.8 %collective-permute-done.14 = bf16[64,512]{1,0:T(8,128)(2,1)S(1)} collective-permute-done((bf16[64,512]{1,0:T(8,128)(2,1)S(1)}, bf16[64,512]{1,0:T(8,128)(2,1)S(1)}, u32[]{:S(2)}, u32[]{:S(2)}) %collective-permute-start.14) | collective-permute-done | bytes 65568 | tf_op jit(solution)/shard_map/ppermute | solution.py:51
  54.4 0.0 collective-permute-done.4.refs_8_
  54.4 3.0 %collective-permute-done.3.refs_7_ = bf16[512,512]{1,0:T(8,128)(2,1)S(1)} collective-permute-done((bf16[512,512]{1,0:T(8,128)(2,1)S(1)}, bf16[512,512]{1,0:T(8,128)(2,1)S(1)}, u32[]{:S(2)}, u32[]{:S(2)}) %collective-permute-start.3) | collective-permute-done | bytes 524320 | tf_op jit(solution)/shard_map/ppermute | solution.py:51
  57.4 0.0 collective-permute-start.15
  57.5 5.2 %collective-permute-done.15.refs_6_ = bf16[64,512]{1,0:T(8,128)(2,1)S(1)} collective-permute-done((bf16[64,512]{1,0:T(8,128)(2,1)S(1)}, bf16[64,512]{1,0:T(8,128)(2,1)S(1)}, u32[]{:S(2)}, u32[]{:S(2)}) %collective-permute-start.15) | collective-permute-done | bytes 65568 | tf_op jit(solution)/shard_map/ppermute | solution.py:51
  62.6 0.1 collective-permute-start.17
  62.7 0.9 collective-permute-start.16
  63.6 3.4 %collective-permute-done.17.refs_8_ = bf16[64,512]{1,0:T(8,128)(2,1)S(1)} collective-permute-done((bf16[64,512]{1,0:T(8,128)(2,1)S(1)}, bf16[64,512]{1,0:T(8,128)(2,1)S(1)}, u32[]{:S(2)}, u32[]{:S(2)}) %collective-permute-start.17) | collective-permute-done | bytes 65568 | tf_op jit(solution)/shard_map/ppermute | solution.py:51
  67.0 0.9 collective-permute-start.19
  67.8 0.0 collective-permute-done.16.refs_7_
  67.9 1.2 %collective-permute-start.18 = (bf16[128,512]{1,0:T(8,128)(2,1)S(1)}, bf16[128,512]{1,0:T(8,128)(2,1)S(1)}, u32[]{:S(2)}, u32[]{:S(2)}) collective-permute-start(bf16[128,512]{1,0:T(8,128)(2,1)S(1)} %pad_maximum_fusion.5), channel_id=1, source_target_pairs={{0,2},{1,3},{2,0},{3,1},{4,6},{5,7},{6,4},{7,5},{8,10},{9,11},{10,... | collective-permute-start | bytes 393224 | tf_op jit(solution)/shard_map/ppermute | solution.py:51
  69.1 0.4 fusion.refs_2_
  69.5 0.0 copy-start.2
  69.5 0.0 copy-start.4
  69.5 2.2 %shard_map.93 = (bf16[2048,512]{1,0:T(8,128)(2,1)S(1)}, bf16[2048,512]{1,0:T(8,128)(2,1)S(1)}) custom-call(s32[1]{0:T(128)} %bitcast.refs_0_, s32[1,2048]{1,0:T(1,128)S(1)} %copy-done.5, bf16[2048,512]{1,0:T(8,128)(2,1)S(1)} %fusion.refs_2_, bf16[256,512]{1,0:T(8,128)(2,1)S(1)} %shard_map.92.refs_3_, bf16[256,512]{1,0:T(8,128)(2,1)S(1)} %collective-permute-done.refs_4_, ...), custom_call_target="tpu_custom_call" | custom-call | tf_op jit(solution)/shard_map/pallas_call | solution.py:324
  71.7 0.3 collective-permute-done.19.refs_10_
  72.0 0.9 %collective-permute-done.18.refs_9_ = bf16[128,512]{1,0:T(8,128)(2,1)S(1)} collective-permute-done((bf16[128,512]{1,0:T(8,128)(2,1)S(1)}, bf16[128,512]{1,0:T(8,128)(2,1)S(1)}, u32[]{:S(2)}, u32[]{:S(2)}) %collective-permute-start.18) | collective-permute-done | bytes 131104 | tf_op jit(solution)/shard_map/ppermute | solution.py:51
  72.9 15.8 %shard_map.101 = bf16[256,512]{1,0:T(8,128)(2,1)} custom-call(s32[1]{0:T(128)} %bitcast.refs_0_, bf16[2048,512]{1,0:T(8,128)(2,1)S(1)} %get-tuple-element.27.refs_1_, bf16[2048,512]{1,0:T(8,128)(2,1)S(1)} %get-tuple-element.28.refs_2_, bf16[512,1536]{1,0:T(8,128)(2,1)S(1)} %copy-done.2, bf16[512,512]{1,0:T(8,128)(2,1)S(1)} %copy-done.4, ...), custom_call_target="tpu_custom_call" | custom-call | tf_op jit(solution)/shard_map/pallas_call | solution.py:394
  (23 shorter events, 0.2 us)
Async XLA Ops:
  0.0 4.5 %copy-start.5 = (s32[1,2048]{1,0:T(1,128)S(1)}, s32[1,2048]{1,0:T(1,128)}, u32[]{:S(2)}) copy-start(s32[1,2048]{1,0:T(1,128)} %refs_1_.5) | copy-start | bytes 24580
  0.0 46.9 %collective-permute-start.12 = (bf16[1024,1024]{1,0:T(8,128)(2,1)}, bf16[1024,1024]{1,0:T(8,128)(2,1)S(1)}, u32[]{:S(2)}, u32[]{:S(2)}) collective-permute-start(bf16[1024,1024]{1,0:T(8,128)(2,1)} %bitcast.5), channel_id=1, source_target_pairs={{0,8},{8,0},{16,24},{24,16},{1,9},{9,1},{17,25},{25,17},{2,10},{10... | collective-permute-start | bytes 6291464 | tf_op jit(solution)/shard_map/ppermute | solution.py:51
  0.5 46.4 %collective-permute-start.13 = (bf16[1024,1024]{1,0:T(8,128)(2,1)}, bf16[1024,1024]{1,0:T(8,128)(2,1)}, u32[]{:S(2)}, u32[]{:S(2)}) collective-permute-start(bf16[1024,1024]{1,0:T(8,128)(2,1)} %bitcast.7), channel_id=1, source_target_pairs={{0,8},{8,0},{16,24},{24,16},{1,9},{9,1},{17,25},{25,17},{2,10},{10... | collective-permute-start | bytes 6291464 | tf_op jit(solution)/shard_map/ppermute | solution.py:51
  5.3 18.0 %collective-permute-start = (bf16[256,512]{1,0:T(8,128)(2,1)S(1)}, bf16[256,512]{1,0:T(8,128)(2,1)S(1)}, u32[]{:S(2)}, u32[]{:S(2)}) collective-permute-start(bf16[256,512]{1,0:T(8,128)(2,1)S(1)} %shard_map.92.refs_3_), channel_id=1, source_target_pairs={{0,4},{1,5},{2,6},{3,7},{4,0},{5,1},{6,2},{7,3},{8,12},{9,13},{10,... | collective-permute-start | bytes 786440 | tf_op jit(solution)/shard_map/ppermute | solution.py:51
  9.4 13.1 %collective-permute-start.5 = (bf16[128,1152]{1,0:T(8,128)(2,1)S(1)}, bf16[128,1152]{1,0:T(8,128)(2,1)S(1)}, u32[]{:S(2)}, u32[]{:S(2)}) collective-permute-start(bf16[128,1152]{1,0:T(8,128)(2,1)S(1)} %get-tuple-element.30), channel_id=1, source_target_pairs={{0,2},{1,3},{2,0},{3,1},{4,6},{5,7},{6,4},{7,5},{8,10},{9,11},{10,... | collective-permute-start | bytes 884744 | tf_op jit(solution)/shard_map/ppermute | solution.py:51
  11.0 11.9 %collective-permute-start.6 = (bf16[128,1152]{1,0:T(8,128)(2,1)S(1)}, bf16[128,1152]{1,0:T(8,128)(2,1)S(1)}, u32[]{:S(2)}, u32[]{:S(2)}) collective-permute-start(bf16[128,1152]{1,0:T(8,128)(2,1)S(1)} %get-tuple-element.34), channel_id=1, source_target_pairs={{0,1},{1,0},{2,3},{3,2},{4,5},{5,4},{6,7},{7,6},{8,9},{9,8},{10,11... | collective-permute-start | bytes 884744 | tf_op jit(solution)/shard_map/ppermute | solution.py:51
  22.9 24.0 %copy-start.3 = (bf16[1024,512]{1,0:T(8,128)(2,1)S(1)}, bf16[1024,512]{1,0:T(8,128)(2,1)}, u32[]{:S(2)}) copy-start(bf16[1024,512]{1,0:T(8,128)(2,1)} %refs_6_.1) | copy-start | bytes 3145732
  23.3 5.9 %collective-permute-start.7 = (bf16[64,1152]{1,0:T(8,128)(2,1)S(1)}, bf16[64,1152]{1,0:T(8,128)(2,1)S(1)}, u32[]{:S(2)}, u32[]{:S(2)}) collective-permute-start(bf16[64,1152]{1,0:T(8,128)(2,1)S(1)} %get-tuple-element.36), channel_id=1, source_target_pairs={{0,1},{1,0},{2,3},{3,2},{4,5},{5,4},{6,7},{7,6},{8,9},{9,8},{10,11... | collective-permute-start | bytes 442376 | tf_op jit(solution)/shard_map/ppermute | solution.py:51
  25.0 6.0 %collective-permute-start.9 = (bf16[64,1152]{1,0:T(8,128)(2,1)S(1)}, bf16[64,1152]{1,0:T(8,128)(2,1)S(1)}, u32[]{:S(2)}, u32[]{:S(2)}) collective-permute-start(bf16[64,1152]{1,0:T(8,128)(2,1)S(1)} %get-tuple-element.40), channel_id=1, source_target_pairs={{0,2},{1,3},{2,0},{3,1},{4,6},{5,7},{6,4},{7,5},{8,10},{9,11},{10,... | collective-permute-start | bytes 442376 | tf_op jit(solution)/shard_map/ppermute | solution.py:51
  26.5 20.4 %copy-start.1 = (bf16[1,1024,1024]{2,1,0:T(8,128)(2,1)S(1)}, bf16[1,1024,1024]{2,1,0:T(8,128)(2,1)}, u32[]{:S(2)}) copy-start(bf16[1,1024,1024]{2,1,0:T(8,128)(2,1)} %param.12) | copy-start | bytes 6291460
  26.5 20.4 %copy-start = (bf16[1,1024,1024]{2,1,0:T(8,128)(2,1)S(1)}, bf16[1,1024,1024]{2,1,0:T(8,128)(2,1)}, u32[]{:S(2)}) copy-start(bf16[1,1024,1024]{2,1,0:T(8,128)(2,1)} %param.11) | copy-start | bytes 6291460
  26.5 14.4 %collective-permute-start.1 = (bf16[256,512]{1,0:T(8,128)(2,1)S(1)}, bf16[256,512]{1,0:T(8,128)(2,1)S(1)}, u32[]{:S(2)}, u32[]{:S(2)}) collective-permute-start(bf16[256,512]{1,0:T(8,128)(2,1)S(1)} %pad_maximum_fusion.2), channel_id=1, source_target_pairs={{0,1},{1,0},{2,3},{3,2},{4,5},{5,4},{6,7},{7,6},{8,9},{9,8},{10,11... | collective-permute-start | bytes 786440 | tf_op jit(solution)/shard_map/ppermute | solution.py:51
  29.5 5.9 %collective-permute-start.8 = (bf16[32,1152]{1,0:T(8,128)(2,1)S(1)}, bf16[32,1152]{1,0:T(8,128)(2,1)S(1)}, u32[]{:S(2)}, u32[]{:S(2)}) collective-permute-start(bf16[32,1152]{1,0:T(8,128)(2,1)S(1)} %get-tuple-element.38), channel_id=1, source_target_pairs={{0,4},{1,5},{2,6},{3,7},{4,0},{5,1},{6,2},{7,3},{8,12},{9,13},{10,... | collective-permute-start | bytes 221192 | tf_op jit(solution)/shard_map/ppermute | solution.py:51
  31.0 9.9 %collective-permute-start.2 = (bf16[256,512]{1,0:T(8,128)(2,1)S(1)}, bf16[256,512]{1,0:T(8,128)(2,1)S(1)}, u32[]{:S(2)}, u32[]{:S(2)}) collective-permute-start(bf16[256,512]{1,0:T(8,128)(2,1)S(1)} %pad_maximum_fusion.3), channel_id=1, source_target_pairs={{0,2},{1,3},{2,0},{3,1},{4,6},{5,7},{6,4},{7,5},{8,10},{9,11},{10,... | collective-permute-start | bytes 786440 | tf_op jit(solution)/shard_map/ppermute | solution.py:51
  35.3 5.3 %collective-permute-start.10 = (bf16[32,1152]{1,0:T(8,128)(2,1)S(1)}, bf16[32,1152]{1,0:T(8,128)(2,1)S(1)}, u32[]{:S(2)}, u32[]{:S(2)}) collective-permute-start(bf16[32,1152]{1,0:T(8,128)(2,1)S(1)} %get-tuple-element.42), channel_id=1, source_target_pairs={{0,4},{1,5},{2,6},{3,7},{4,0},{5,1},{6,2},{7,3},{8,12},{9,13},{10,... | collective-permute-start | bytes 221192 | tf_op jit(solution)/shard_map/ppermute | solution.py:51
  40.9 6.0 %collective-permute-start.11 = (bf16[64,1024]{1,0:T(8,128)(2,1)S(1)}, bf16[64,1024]{1,0:T(8,128)(2,1)S(1)}, u32[]{:S(2)}, u32[]{:S(2)}) collective-permute-start(bf16[64,1024]{1,0:T(8,128)(2,1)S(1)} %pad_maximum_fusion.4.refs_0_), channel_id=1, source_target_pairs={{0,16},{8,24},{16,0},{24,8},{1,17},{9,25},{17,1},{25,9},{2,18},{10... | collective-permute-start | bytes 393224 | tf_op jit(solution)/shard_map/ppermute | solution.py:51
  42.8 11.6 %collective-permute-start.4 = (bf16[512,512]{1,0:T(8,128)(2,1)S(1)}, bf16[512,512]{1,0:T(8,128)(2,1)S(1)}, u32[]{:S(2)}, u32[]{:S(2)}) collective-permute-start(bf16[512,512]{1,0:T(8,128)(2,1)S(1)} %pad_maximum_fusion.1), channel_id=1, source_target_pairs={{0,1},{1,0},{2,3},{3,2},{4,5},{5,4},{6,7},{7,6},{8,9},{9,8},{10,11... | collective-permute-start | bytes 1572872 | tf_op jit(solution)/shard_map/ppermute | solution.py:51
  46.8 10.7 %collective-permute-start.3 = (bf16[512,512]{1,0:T(8,128)(2,1)S(1)}, bf16[512,512]{1,0:T(8,128)(2,1)S(1)}, u32[]{:S(2)}, u32[]{:S(2)}) collective-permute-start(bf16[512,512]{1,0:T(8,128)(2,1)S(1)} %pad_maximum_fusion), channel_id=1, source_target_pairs={{0,2},{1,3},{2,0},{3,1},{4,6},{5,7},{6,4},{7,5},{8,10},{9,11},{10,... | collective-permute-start | bytes 1572872 | tf_op jit(solution)/shard_map/ppermute | solution.py:51
  50.0 4.3 %collective-permute-start.14 = (bf16[64,512]{1,0:T(8,128)(2,1)S(1)}, bf16[64,512]{1,0:T(8,128)(2,1)S(1)}, u32[]{:S(2)}, u32[]{:S(2)}) collective-permute-start(bf16[64,512]{1,0:T(8,128)(2,1)S(1)} %get-tuple-element.45), channel_id=1, source_target_pairs={{0,16},{8,24},{16,0},{24,8},{1,17},{9,25},{17,1},{25,9},{2,18},{10... | collective-permute-start | bytes 196616 | tf_op jit(solution)/shard_map/ppermute | solution.py:51
  50.9 0.7 copy-start.6
  57.4 5.2 %collective-permute-start.15 = (bf16[64,512]{1,0:T(8,128)(2,1)S(1)}, bf16[64,512]{1,0:T(8,128)(2,1)S(1)}, u32[]{:S(2)}, u32[]{:S(2)}) collective-permute-start(bf16[64,512]{1,0:T(8,128)(2,1)S(1)} %add_convert_fusion.refs_5_), channel_id=1, source_target_pairs={{0,4},{1,5},{2,6},{3,7},{4,0},{5,1},{6,2},{7,3},{8,12},{9,13},{10,... | collective-permute-start | bytes 196616 | tf_op jit(solution)/shard_map/ppermute | solution.py:51
  62.6 4.3 %collective-permute-start.17 = (bf16[64,512]{1,0:T(8,128)(2,1)S(1)}, bf16[64,512]{1,0:T(8,128)(2,1)S(1)}, u32[]{:S(2)}, u32[]{:S(2)}) collective-permute-start(bf16[64,512]{1,0:T(8,128)(2,1)S(1)} %pad_maximum_fusion.8), channel_id=1, source_target_pairs={{0,2},{1,3},{2,0},{3,1},{4,6},{5,7},{6,4},{7,5},{8,10},{9,11},{10,... | collective-permute-start | bytes 196616 | tf_op jit(solution)/shard_map/ppermute | solution.py:51
  62.7 5.1 %collective-permute-start.16 = (bf16[64,512]{1,0:T(8,128)(2,1)S(1)}, bf16[64,512]{1,0:T(8,128)(2,1)S(1)}, u32[]{:S(2)}, u32[]{:S(2)}) collective-permute-start(bf16[64,512]{1,0:T(8,128)(2,1)S(1)} %pad_maximum_fusion.7), channel_id=1, source_target_pairs={{0,1},{1,0},{2,3},{3,2},{4,5},{5,4},{6,7},{7,6},{8,9},{9,8},{10,11... | collective-permute-start | bytes 196616 | tf_op jit(solution)/shard_map/ppermute | solution.py:51
  67.0 5.0 %collective-permute-start.19 = (bf16[128,512]{1,0:T(8,128)(2,1)S(1)}, bf16[128,512]{1,0:T(8,128)(2,1)S(1)}, u32[]{:S(2)}, u32[]{:S(2)}) collective-permute-start(bf16[128,512]{1,0:T(8,128)(2,1)S(1)} %pad_maximum_fusion.6), channel_id=1, source_target_pairs={{0,1},{1,0},{2,3},{3,2},{4,5},{5,4},{6,7},{7,6},{8,9},{9,8},{10,11... | collective-permute-start | bytes 393224 | tf_op jit(solution)/shard_map/ppermute | solution.py:51
  67.9 5.0 %collective-permute-start.18 = (bf16[128,512]{1,0:T(8,128)(2,1)S(1)}, bf16[128,512]{1,0:T(8,128)(2,1)S(1)}, u32[]{:S(2)}, u32[]{:S(2)}) collective-permute-start(bf16[128,512]{1,0:T(8,128)(2,1)S(1)} %pad_maximum_fusion.5), channel_id=1, source_target_pairs={{0,2},{1,3},{2,0},{3,1},{4,6},{5,7},{6,4},{7,5},{8,10},{9,11},{10,... | collective-permute-start | bytes 393224 | tf_op jit(solution)/shard_map/ppermute | solution.py:51
  69.5 3.4 %copy-start.2 = (bf16[512,1536]{1,0:T(8,128)(2,1)S(1)}, bf16[512,1536]{1,0:T(8,128)(2,1)}, u32[]{:S(2)}) copy-start(bf16[512,1536]{1,0:T(8,128)(2,1)} %refs_3_.1) | copy-start | bytes 4718596
  69.5 3.4 %copy-start.4 = (bf16[512,512]{1,0:T(8,128)(2,1)S(1)}, bf16[512,512]{1,0:T(8,128)(2,1)}, u32[]{:S(2)}) copy-start(bf16[512,512]{1,0:T(8,128)(2,1)} %refs_4_.1) | copy-start | bytes 1572868

commit v5 on v4

--- a/solution.py
+++ b/solution.py
@@ -93,6 +93,21 @@
     return arrays, starts, steps
 
 
+def gather_direct(values, axis):
+    count = lax.axis_size(axis)
+    bits = count.bit_length() - 1
+    low = 1 << (bits // 2)
+    rows = values.shape[0]
+    near = [values] + [swap(values, axis, step) for step in range(1, low)]
+    held = jnp.concatenate(near, axis=0)
+    arrays = [held] + [swap(held, axis, step * low) for step in range(1, count // low)]
+    ranks = [step * low + inner for step in range(count // low) for inner in range(low)]
+    starts = [
+        [(step, inner * rows + half) for step in range(count // low) for inner in range(low)] for half in (0, rows // 2)
+    ]
+    return arrays, starts, (ranks, ranks)
+
+
 def tie(values, others):
     kept = lax.optimization_barrier((tuple(values), tuple(others)))
     return kept[0]
@@ -105,11 +120,35 @@
     return held
 
 
-def front_kernel(orders, place_ref, tokens_hbm, keys_hbm, *refs):
-    outs, combine_ref = refs[:4], refs[4]
-    tokens_ref, keys_ref, turned_ref, tops_ref, picked_ref, picked_tops_ref, sems = refs[5:]
+def slots_of(listing, vis_dev, count, capacity):
+    block = listing.shape[1]
+    owners = listing // vis_dev
+    across = jnp.broadcast_to(owners, (block, block))
+    before = lax.broadcasted_iota(jnp.int32, (block, block), 0) < lax.broadcasted_iota(jnp.int32, (block, block), 1)
+    same = (across == across.T) & before
+    ranks = jnp.sum(same.astype(F32), axis=0, keepdims=True).astype(jnp.int32)
+    return owners, jnp.minimum(ranks, capacity - 1)
+
+
+def picker_of(myself, listing_ref, vis_dev, count):
+    block = listing_ref.shape[1] // count
+    capacity = block // count
+    row = lax.broadcasted_iota(jnp.int32, (capacity, block), 0)
+    token = lax.broadcasted_iota(jnp.int32, (capacity, vis_dev), 1)
+    picks = []
+    for target in range(count):
+        listing = listing_ref[:, target * block : (target + 1) * block]
+        owners, ranks = slots_of(listing, vis_dev, count, capacity)
+        mine = jnp.where(owners == myself, ranks, -1)
+        local = jnp.broadcast_to(listing - myself * vis_dev + 1, (capacity, block))
+        source = jnp.sum(jnp.where(mine == row, local, 0).astype(F32), axis=1, keepdims=True).astype(jnp.int32) - 1
+        picks.append((source == token).astype(BF16))
+    return jnp.concatenate(picks, axis=0)
+
+
+def rows_kernel(count, place_ref, listing_ref, tokens_hbm, keys_hbm, picked_ref, normed_ref, logits_ref, *refs):
+    tokens_ref, keys_ref, sems = refs
     rows, width = tokens_ref.shape
-    slots = keys_ref.shape[1]
     pieces = sems.shape[1]
     token_step, key_step = rows // pieces, width // pieces
     copies = []
@@ -121,15 +160,50 @@
         copies.append(pltpu.make_async_copy(keys_hbm.at[part], keys_ref.at[part], sems.at[1, piece]))
     for copy in copies:
         copy.start()
+    picker = picker_of(place_ref[0], listing_ref, rows, count)
     parts = []
     for piece in range(pieces):
         copies[piece].wait()
         part = tokens_ref[piece * token_step : (piece + 1) * token_step, :].astype(F32)
         parts.append(normalise(part).astype(BF16))
     normed = jnp.concatenate(parts, axis=0)
+    normed_ref[...] = normed
     for copy in copies[pieces:]:
         copy.wait()
     logits = jnp.dot(normed, keys_ref[...], preferred_element_type=F32)
+    logits_ref[...] = logits
+    raised = jnp.exp(logits - jnp.max(logits, axis=1, keepdims=True))
+    combine = (raised / jnp.sum(raised, axis=1, keepdims=True)).astype(BF16)
+    picked_ref[...] = jnp.dot(picker, combine, preferred_element_type=F32).astype(BF16)
+
+
+def rows_and_picks(place, listing, tokens, slot_keys, count):
+    rows, width = tokens.shape
+    slots = slot_keys.shape[1]
+    pieces = 4
+    return pl.pallas_call(
+        lambda *refs: rows_kernel(count, *refs),
+        out_shape=(
+            jax.ShapeDtypeStruct((listing.shape[1] // count, slots), BF16),
+            jax.ShapeDtypeStruct((rows, width), BF16),
+            jax.ShapeDtypeStruct((rows, slots), F32),
+        ),
+        in_specs=[SMEM, VMEM, HBM, HBM],
+        out_specs=(VMEM,) * 3,
+        scratch_shapes=[
+            pltpu.VMEM((rows, width), BF16),
+            pltpu.VMEM((width, slots), BF16),
+            pltpu.SemaphoreType.DMA((2, pieces)),
+        ],
+        compiler_params=pltpu.CompilerParams(vmem_limit_bytes=24 << 20),
+    )(place, listing, *(pltpu.with_memory_space_constraint(array, pltpu.HBM) for array in (tokens, slot_keys)))
+
+
+def sums_kernel(orders, place_ref, normed_ref, logits_ref, *refs):
+    outs, (turned_ref, tops_ref, picked_ref, picked_tops_ref) = refs[:4], refs[4:]
+    rows, width = normed_ref.shape
+    slots = logits_ref.shape[1]
+    logits = logits_ref[...]
     top = jnp.max(logits, axis=0, keepdims=True)
     turned_ref[...] = jnp.exp(logits - top).astype(BF16).T
     tops_ref[...] = jnp.broadcast_to(top, (LANES, slots)).T
@@ -144,38 +218,31 @@
             picked_ref[target, :] = turned_ref[source, :]
             picked_tops_ref[target, :] = tops_ref[source, :]
     picked = picked_ref[...]
-    sums = jnp.dot(picked, normed, preferred_element_type=F32).astype(BF16)
+    sums = jnp.dot(picked, normed_ref[...], preferred_element_type=F32).astype(BF16)
     totals = jnp.dot(picked, jnp.ones((rows, LANES), BF16), preferred_element_type=F32)
     stats = pack(picked_tops_ref[...], totals)
     quarter = slots // 4
     for index, out_ref in enumerate(outs):
         out_ref[:, :width] = sums[index * quarter : (index + 1) * quarter, :]
         out_ref[:, width:] = stats[index * quarter : (index + 1) * quarter, :]
-    raised = jnp.exp(logits - jnp.max(logits, axis=1, keepdims=True))
-    combine_ref[...] = (raised / jnp.sum(raised, axis=1, keepdims=True)).astype(BF16)
-
-
-def front(place, tokens, slot_keys, orders):
-    rows, width = tokens.shape
-    slots = slot_keys.shape[1]
-    quarter = jax.ShapeDtypeStruct((slots // 4, width + LANES), BF16)
-    pieces = 4
+
+
+def own_sums(place, normed, logits, orders):
+    rows, width = normed.shape
+    slots = logits.shape[1]
     return pl.pallas_call(
-        lambda *refs: front_kernel(orders, *refs),
-        out_shape=(quarter,) * 4 + (jax.ShapeDtypeStruct((rows, slots), BF16),),
-        in_specs=[SMEM, HBM, HBM],
-        out_specs=(VMEM,) * 5,
+        lambda *refs: sums_kernel(orders, *refs),
+        out_shape=(jax.ShapeDtypeStruct((slots // 4, width + LANES), BF16),) * 4,
+        in_specs=[SMEM, VMEM, VMEM],
+        out_specs=(VMEM,) * 4,
         scratch_shapes=[
-            pltpu.VMEM((rows, width), BF16),
-            pltpu.VMEM((width, slots), BF16),
             pltpu.VMEM((slots, rows), BF16),
             pltpu.VMEM((slots, LANES), F32),
             pltpu.VMEM((slots, rows), BF16),
             pltpu.VMEM((slots, LANES), F32),
-            pltpu.SemaphoreType.DMA((2, pieces)),
         ],
-        compiler_params=pltpu.CompilerParams(vmem_limit_bytes=28 << 20),
-    )(place, *(pltpu.with_memory_space_constraint(array, pltpu.HBM) for array in (tokens, slot_keys)))
+        compiler_params=pltpu.CompilerParams(vmem_limit_bytes=24 << 20),
+    )(place, normed, logits)
 
 
 def merge_kernel(kept_ref, came_ref, *outs):
@@ -252,45 +319,6 @@
         ],
         compiler_params=pltpu.CompilerParams(vmem_limit_bytes=20 << 20),
     )(*slot_rows, first, first_other, second, second_other, w_proj)
-
-
-def slots_of(listing, vis_dev, count, capacity):
-    block = listing.shape[1]
-    owners = listing // vis_dev
-    across = jnp.broadcast_to(owners, (block, block))
-    before = lax.broadcasted_iota(jnp.int32, (block, block), 0) < lax.broadcasted_iota(jnp.int32, (block, block), 1)
-    same = (across == across.T) & before
-    ranks = jnp.sum(same.astype(F32), axis=0, keepdims=True).astype(jnp.int32)
-    return owners, jnp.minimum(ranks, capacity - 1)
-
-
-def pick_kernel(count, place_ref, listing_ref, combine_ref, out_ref):
-    vis_dev = combine_ref.shape[0]
-    block = listing_ref.shape[1] // count
-    capacity = block // count
-    myself = place_ref[0]
-    row = lax.broadcasted_iota(jnp.int32, (capacity, block), 0)
-    token = lax.broadcasted_iota(jnp.int32, (capacity, vis_dev), 1)
-    picks = []
-    for target in range(count):
-        listing = listing_ref[:, target * block : (target + 1) * block]
-        owners, ranks = slots_of(listing, vis_dev, count, capacity)
-        mine = jnp.where(owners == myself, ranks, -1)
-        local = jnp.broadcast_to(listing - myself * vis_dev + 1, (capacity, block))
-        source = jnp.sum(jnp.where(mine == row, local, 0).astype(F32), axis=1, keepdims=True).astype(jnp.int32) - 1
-        picks.append((source == token).astype(BF16))
-    picker = jnp.concatenate(picks, axis=0)
-    out_ref[...] = jnp.dot(picker, combine_ref[...], preferred_element_type=F32).astype(BF16)
-
-
-def pick(place, listing, combine, count):
-    return pl.pallas_call(
-        lambda *refs: pick_kernel(count, *refs),
-        out_shape=jax.ShapeDtypeStruct((listing.shape[1] // count, combine.shape[1]), BF16),
-        in_specs=[SMEM, VMEM, VMEM],
-        out_specs=VMEM,
-        compiler_params=pltpu.CompilerParams(vmem_limit_bytes=12 << 20),
-    )(place, listing, combine)
 
 
 def order_kernel(ranks, starts, vis_dev, place_ref, listing_ref, filler_ref, *refs):
@@ -331,7 +359,7 @@
 
 
 def tail_kernel(
-    ranks, starts, place_ref, combine_ref, filler_ref, w_qkv_ref, w_out_ref, *refs
+    ranks, starts, half, place_ref, combine_ref, filler_ref, w_qkv_ref, w_out_ref, *refs
 ):
     pieces = refs[:-5]
     out_ref, slot_ref, k_ref, v_ref, a_ref = refs[-5:]
@@ -341,7 +369,6 @@
     groups = width // LANES
     in_group = LANES // head_dim
     myself = place_ref[0]
-    half = pieces[0].shape[0] // 2
     for path in range(2):
         for relative, (index, start) in zip(ranks[path], starts[path]):
             target = pl.multiple_of((myself ^ relative) * (2 * half) + path * half, half)
@@ -387,12 +414,12 @@
     out_ref[...] = (mixed + dec_in).astype(BF16)
 
 
-def tail(place, combine, filler, w_qkv, w_out, arrays, starts, ranks):
+def tail(place, combine, filler, w_qkv, w_out, arrays, starts, ranks, half):
     total, width = filler.shape
     groups = width // LANES
     mine = total // len(ranks[0])
     return pl.pallas_call(
-        lambda *refs: tail_kernel(ranks, starts, *refs),
+        lambda *refs: tail_kernel(ranks, starts, half, *refs),
         out_shape=jax.ShapeDtypeStruct((mine, width), BF16),
         in_specs=[SMEM] + [VMEM] * (4 + len(arrays)),
         out_specs=VMEM,
@@ -436,18 +463,15 @@
     first, first_other = w_in[0], swap(w_in[0], "clip", 1)
     second, second_other = w_back[0], swap(w_back[0], "clip", 1)
 
-    *quarters, combine = front(place, tokens, slot_keys, orders)
-
-    outgoing = pick(place, dec_source, combine, n_tok)
+    outgoing, normed, logits = rows_and_picks(place, dec_source, tokens, slot_keys, n_tok)
     arrays, starts, brought = gather_pair(outgoing, "tok", back_orders)
     filler = (mask_token.astype(F32)[None, :] + sinusoid_table(dec_total, dec_dev, dec_width)).astype(BF16)
     ordered, filler = put_in_order(place, dec_source, filler, arrays, starts, ranks, vis_dev)
 
+    quarters = own_sums(place, normed, logits, orders)
     state = [(quarters[0], quarters[1]), (quarters[2], quarters[3])]
     for step in range(steps):
         sent = [state[path][1] for path in range(2)]
-        if step == 1:
-            sent = tie(sent, brought[0])
         arrived = [swap(sent[path], "tok", 1 << orders[path][step]) for path in range(2)]
         state = [merge(state[path][0], arrived[path], step == steps - 1) for path in range(2)]
     slot_in = jnp.concatenate(state, axis=0)
@@ -460,8 +484,8 @@
     for mask, result in zip(others, results[1:]):
         slot_proj = slot_proj + swap(result, "clip", mask).astype(F32)
     (slot_proj,) = tie([slot_proj.astype(BF16)], brought[-1])
-    everyone, their_starts, _ = gather_pair(slot_proj, "tok", back_orders)
-    return tail(place, ordered, filler, w_qkv, w_out, everyone, their_starts, ranks)
+    everyone, their_starts, their_ranks = gather_direct(slot_proj, "tok")
+    return tail(place, ordered, filler, w_qkv, w_out, everyone, their_starts, their_ranks, slot_proj.shape[0] // 2)
 
 
 def solution(mesh):

time: 88.9 us -> 86.7 us (0.975)
  starting transfers between devices: 25.7 us -> 23.6 us
  waiting for transfers between devices: 32.7 us -> 31.7 us
  local copies, waits for them, and re-layouts: 0.32 us -> 1.3 us
    ppermute x20 -> x19, starting transfers between devices: 25.7 us -> 23.6 us  [swap(): lax.ppermute(values, axis, [(index, index ^ mask) for index in range(coun...]
    ppermute x20 -> x19, waiting for transfers between devices: 32.7 us -> 31.7 us  [swap(): lax.ppermute(values, axis, [(index, index ^ mask) for index in range(coun...]
    unnamed x14 -> x17, local copies, waits for them, and re-layouts: 0.27 us -> 1.26 us
  transfers between devices with their start and end apart: 20 -> 19, of which waited for: 11 -> 9; matrix products, arithmetic and copies ran while one was open for 2% -> 2% of each run, Pallas kernels for 13% -> 14%
where the time goes in v5:
time: 86.7 us; the launch traced here: 86.4 us
  waiting for transfers between devices  31.7 us (37%)
  Pallas kernels  27.5 us (32%)
  starting transfers between devices  23.6 us (27%)
  other arithmetic  2.1 us (2%)
  local copies, waits for them, and re-layouts  1.3 us (1%)
    ppermute x19, waiting for transfers between devices, swap(): lax.ppermute(values, axis, [(index, index ^ mask) for index in range(coun...  31.7 us
    ppermute x19, starting transfers between devices, swap(): lax.ppermute(values, axis, [(index, index ^ mask) for index in range(coun...  23.6 us
    pallas_call x1, Pallas kernels, tail(): pl.pallas_call(lambda *refs: tail_kernel(ranks, starts, half, *refs), out...  15.8 us
    pallas_call x1, Pallas kernels, rows_and_picks(): pl.pallas_call(lambda *refs: rows_kernel(count, *refs), out_shape=(jax.Sh...  3.58 us
    pallas_call x1, Pallas kernels, experts(): pl.pallas_call(lambda *refs: experts_kernel(count, *refs), out_shape=(jax...  3.09 us
    pallas_call x1, Pallas kernels, put_in_order(): pl.pallas_call(lambda *refs: order_kernel(ranks, starts, vis_dev, *refs),...  2.19 us
  transfers between devices with their start and end apart: 19, of which 9 were waited for; matrix products, arithmetic and copies ran while one was open for 2% of the time, Pallas kernels for 14%

profile of v5, /device:TPU:0, one launch (start us, length us, event | category | flops | bytes accessed | tf_op | source)
XLA Modules:
  0.0 86.4 jit_solution(14815835160728581833)
XLA Ops:
  0.0 0.5 collective-permute-start.12
  0.5 0.1 collective-permute-start.13
  0.5 0.0 copy-start.5
  0.5 0.7 copy-done.5
  1.2 3.6 %shard_map.91 = (bf16[256,512]{1,0:T(8,128)(2,1)S(1)}, bf16[512,1024]{1,0:T(8,128)(2,1)S(1)}, f32[512,512]{1,0:T(8,128)S(1)}) custom-call(s32[1]{0:T(128)} %bitcast.refs_0_, s32[1,2048]{1,0:T(1,128)S(1)} %copy-done.5, bf16[512,1024]{1,0:T(8,128)(2,1)} %refs_2_.1, bf16[1024,512]{1,0:T(8,128)(2,1)} %refs_3_.2), custom_call_target="tpu_custom_call" | custom-call | tf_op jit(solution)/shard_map/pallas_call | solution.py:184
  4.8 4.1 %collective-permute-start = (bf16[256,512]{1,0:T(8,128)(2,1)S(1)}, bf16[256,512]{1,0:T(8,128)(2,1)S(1)}, u32[]{:S(2)}, u32[]{:S(2)}) collective-permute-start(bf16[256,512]{1,0:T(8,128)(2,1)S(1)} %get-tuple-element.26.refs_3_), channel_id=1, source_target_pairs={{0,4},{1,5},{2,6},{3,7},{4,0},{5,1},{6,2},{7,3},{8,12},{9,13},{10,... | collective-permute-start | bytes 786440 | tf_op jit(solution)/shard_map/ppermute | solution.py:51
  8.9 1.1 %shard_map.93 = (bf16[128,1152]{1,0:T(8,128)(2,1)S(1)}, bf16[128,1152]{1,0:T(8,128)(2,1)S(1)}, bf16[128,1152]{1,0:T(8,128)(2,1)S(1)}, bf16[128,1152]{1,0:T(8,128)(2,1)S(1)}) custom-call(s32[1]{0:T(128)} %bitcast.refs_0_, bf16[512,1024]{1,0:T(8,128)(2,1)S(1)} %get-tuple-element.29.refs_1_, f32[512,512]{1,0:T(8,128)S(1)} %get-tuple-element.30.refs_2_), custom_call_target="tpu_custom_call" | custom-call | tf_op jit(solution)/shard_map/pallas_call | solution.py:233
  10.0 1.6 %collective-permute-start.5 = (bf16[128,1152]{1,0:T(8,128)(2,1)S(1)}, bf16[128,1152]{1,0:T(8,128)(2,1)S(1)}, u32[]{:S(2)}, u32[]{:S(2)}) collective-permute-start(bf16[128,1152]{1,0:T(8,128)(2,1)S(1)} %get-tuple-element.32), channel_id=1, source_target_pairs={{0,2},{1,3},{2,0},{3,1},{4,6},{5,7},{6,4},{7,5},{8,10},{9,11},{10,... | collective-permute-start | bytes 884744 | tf_op jit(solution)/shard_map/ppermute | solution.py:51
  11.7 1.5 %collective-permute-start.8 = (bf16[128,1152]{1,0:T(8,128)(2,1)S(1)}, bf16[128,1152]{1,0:T(8,128)(2,1)S(1)}, u32[]{:S(2)}, u32[]{:S(2)}) collective-permute-start(bf16[128,1152]{1,0:T(8,128)(2,1)S(1)} %get-tuple-element.38), channel_id=1, source_target_pairs={{0,1},{1,0},{2,3},{3,2},{4,5},{5,4},{6,7},{7,6},{8,9},{9,8},{10,11... | collective-permute-start | bytes 884744 | tf_op jit(solution)/shard_map/ppermute | solution.py:51
  13.2 1.0 %multiply_cosine_fusion = (f32[256,256]{1,0:T(8,128)S(1)}, f32[256,256]{1,0:T(8,128)S(1)}) fusion(f32[256]{0:T(256)S(1)} %multiply_exponential_fusion, f32[256]{0:T(256)S(1)} %iota_convert_fusion), kind=kLoop, calls=%fused_computation.7 | loop fusion | flops 65536 | bytes 526336 | tf_op jit(solution)/shard_map/cos | solution.py:442
  14.2 9.0 %collective-permute-done.5.came_ref = bf16[128,1152]{1,0:T(8,128)(2,1)S(1)} collective-permute-done((bf16[128,1152]{1,0:T(8,128)(2,1)S(1)}, bf16[128,1152]{1,0:T(8,128)(2,1)S(1)}, u32[]{:S(2)}, u32[]{:S(2)}) %collective-permute-start.5) | collective-permute-done | bytes 294944 | tf_op jit(solution)/shard_map/ppermute | solution.py:51
  23.2 0.3 shard_map.94
  23.5 1.6 %collective-permute-start.6 = (bf16[64,1152]{1,0:T(8,128)(2,1)S(1)}, bf16[64,1152]{1,0:T(8,128)(2,1)S(1)}, u32[]{:S(2)}, u32[]{:S(2)}) collective-permute-start(bf16[64,1152]{1,0:T(8,128)(2,1)S(1)} %get-tuple-element.34), channel_id=1, source_target_pairs={{0,1},{1,0},{2,3},{3,2},{4,5},{5,4},{6,7},{7,6},{8,9},{9,8},{10,11... | collective-permute-start | bytes 442376 | tf_op jit(solution)/shard_map/ppermute | solution.py:51
  25.2 0.0 collective-permute-done.refs_4_
  25.2 0.0 copy-start.3
  25.2 0.0 collective-permute-done.8.came_ref
  25.2 0.3 shard_map.97
  25.6 0.3 collective-permute-start.9
  25.9 0.0 copy-start
  25.9 0.6 collective-permute-start.1
  26.5 3.9 %collective-permute-done.6.came_ref = bf16[64,1152]{1,0:T(8,128)(2,1)S(1)} collective-permute-done((bf16[64,1152]{1,0:T(8,128)(2,1)S(1)}, bf16[64,1152]{1,0:T(8,128)(2,1)S(1)}, u32[]{:S(2)}, u32[]{:S(2)}) %collective-permute-start.6) | collective-permute-done | bytes 147488 | tf_op jit(solution)/shard_map/ppermute | solution.py:51
  30.3 0.3 shard_map.95
  30.6 0.3 collective-permute-start.7
  30.9 0.4 collective-permute-done.9.came_ref
  31.3 2.5 %collective-permute-start.2 = (bf16[256,512]{1,0:T(8,128)(2,1)S(1)}, bf16[256,512]{1,0:T(8,128)(2,1)S(1)}, u32[]{:S(2)}, u32[]{:S(2)}) collective-permute-start(bf16[256,512]{1,0:T(8,128)(2,1)S(1)} %pad_maximum_fusion.3), channel_id=1, source_target_pairs={{0,2},{1,3},{2,0},{3,1},{4,6},{5,7},{6,4},{7,5},{8,10},{9,11},{10,... | collective-permute-start | bytes 786440 | tf_op jit(solution)/shard_map/ppermute | solution.py:51
  33.8 0.3 shard_map.98
  34.1 4.0 %collective-permute-done.7.came_ref = bf16[32,1152]{1,0:T(8,128)(2,1)S(1)} collective-permute-done((bf16[32,1152]{1,0:T(8,128)(2,1)S(1)}, bf16[32,1152]{1,0:T(8,128)(2,1)S(1)}, u32[]{:S(2)}, u32[]{:S(2)}) %collective-permute-start.7) | collective-permute-done | bytes 73760 | tf_op jit(solution)/shard_map/ppermute | solution.py:51
  38.0 0.0 collective-permute-start.10
  38.0 0.1 multiply_sine_fusion.1
  38.2 0.2 shard_map.96
  38.4 4.9 %collective-permute-done.10.came_ref = bf16[32,1152]{1,0:T(8,128)(2,1)S(1)} collective-permute-done((bf16[32,1152]{1,0:T(8,128)(2,1)S(1)}, bf16[32,1152]{1,0:T(8,128)(2,1)S(1)}, u32[]{:S(2)}, u32[]{:S(2)}) %collective-permute-start.10) | collective-permute-done | bytes 73760 | tf_op jit(solution)/shard_map/ppermute | solution.py:51
  43.3 0.2 shard_map.99
  43.6 0.0 collective-permute-done.1.refs_5_
  43.6 0.0 collective-permute-done.2.refs_6_
  43.6 1.7 %collective-permute-start.11 = (bf16[64,1024]{1,0:T(8,128)(2,1)S(1)}, bf16[64,1024]{1,0:T(8,128)(2,1)S(1)}, u32[]{:S(2)}, u32[]{:S(2)}) collective-permute-start(bf16[64,1024]{1,0:T(8,128)(2,1)S(1)} %pad_maximum_fusion.4.refs_0_), channel_id=1, source_target_pairs={{0,16},{8,24},{16,0},{24,8},{1,17},{9,25},{17,1},{25,9},{2,18},{10... | collective-permute-start | bytes 393224 | tf_op jit(solution)/shard_map/ppermute | solution.py:51
  45.3 1.3 %collective-permute-start.4 = (bf16[512,512]{1,0:T(8,128)(2,1)S(1)}, bf16[512,512]{1,0:T(8,128)(2,1)S(1)}, u32[]{:S(2)}, u32[]{:S(2)}) collective-permute-start(bf16[512,512]{1,0:T(8,128)(2,1)S(1)} %pad_maximum_fusion.1), channel_id=1, source_target_pairs={{0,1},{1,0},{2,3},{3,2},{4,5},{5,4},{6,7},{7,6},{8,9},{9,8},{10,11... | collective-permute-start | bytes 1572872 | tf_op jit(solution)/shard_map/ppermute | solution.py:51
  46.6 0.1 collective-permute-start.3
  46.7 2.5 %collective-permute-done.11.refs_1_ = bf16[64,1024]{1,0:T(8,128)(2,1)S(1)} collective-permute-done((bf16[64,1024]{1,0:T(8,128)(2,1)S(1)}, bf16[64,1024]{1,0:T(8,128)(2,1)S(1)}, u32[]{:S(2)}, u32[]{:S(2)}) %collective-permute-start.11) | collective-permute-done | bytes 131104 | tf_op jit(solution)/shard_map/ppermute | solution.py:51
  49.2 0.0 collective-permute-done.12.refs_3_
  49.2 0.0 collective-permute-done.13.refs_5_
  49.2 0.0 copy-done.3
  49.2 0.0 copy-done.1
  49.2 0.0 copy-done
  49.2 3.1 %shard_map.100 = (bf16[64,512]{1,0:T(8,128)(2,1)S(1)}, bf16[64,512]{1,0:T(8,128)(2,1)S(1)}) custom-call(bf16[64,1024]{1,0:T(8,128)(2,1)S(1)} %pad_maximum_fusion.4.refs_0_, bf16[64,1024]{1,0:T(8,128)(2,1)S(1)} %collective-permute-done.11.refs_1_, bf16[1024,1024]{1,0:T(8,128)(2,1)S(1)} %bitcast.6, bf16[1024,1024]{1,0:T(8,128)(2,1)S(1)} %collective-permute-done.12.refs_3_, ...), custom_call_target="tpu_custom_call" | custom-call | tf_op jit(solution)/shard_map/pallas_call | solution.py:310
  52.3 1.8 %collective-permute-start.14 = (bf16[64,512]{1,0:T(8,128)(2,1)S(1)}, bf16[64,512]{1,0:T(8,128)(2,1)S(1)}, u32[]{:S(2)}, u32[]{:S(2)}) collective-permute-start(bf16[64,512]{1,0:T(8,128)(2,1)S(1)} %get-tuple-element.45), channel_id=1, source_target_pairs={{0,16},{8,24},{16,0},{24,8},{1,17},{9,25},{17,1},{25,9},{2,18},{10... | collective-permute-start | bytes 196616 | tf_op jit(solution)/shard_map/ppermute | solution.py:51
  54.1 0.4 multiply_add_fusion
  54.6 0.2 copy-done.7
  54.8 1.8 %collective-permute-done.14 = bf16[64,512]{1,0:T(8,128)(2,1)S(1)} collective-permute-done((bf16[64,512]{1,0:T(8,128)(2,1)S(1)}, bf16[64,512]{1,0:T(8,128)(2,1)S(1)}, u32[]{:S(2)}, u32[]{:S(2)}) %collective-permute-start.14) | collective-permute-done | bytes 65568 | tf_op jit(solution)/shard_map/ppermute | solution.py:51
  56.7 0.0 collective-permute-done.4.refs_8_
  56.7 0.0 collective-permute-done.3.refs_7_
  56.7 1.4 %collective-permute-start.15 = (bf16[64,512]{1,0:T(8,128)(2,1)S(1)}, bf16[64,512]{1,0:T(8,128)(2,1)S(1)}, u32[]{:S(2)}, u32[]{:S(2)}) collective-permute-start(bf16[64,512]{1,0:T(8,128)(2,1)S(1)} %add_convert_fusion), channel_id=1, source_target_pairs={{0,1},{1,0},{2,3},{3,2},{4,5},{5,4},{6,7},{7,6},{8,9},{9,8},{10,11... | collective-permute-start | bytes 196616 | tf_op jit(solution)/shard_map/ppermute | solution.py:51
  58.1 3.0 %collective-permute-done.15 = bf16[64,512]{1,0:T(8,128)(2,1)S(1)} collective-permute-done((bf16[64,512]{1,0:T(8,128)(2,1)S(1)}, bf16[64,512]{1,0:T(8,128)(2,1)S(1)}, u32[]{:S(2)}, u32[]{:S(2)}) %collective-permute-start.15) | collective-permute-done | bytes 65568 | tf_op jit(solution)/shard_map/ppermute | solution.py:51
  61.0 1.2 %collective-permute-start.18 = (bf16[128,512]{1,0:T(8,128)(2,1)S(1)}, bf16[128,512]{1,0:T(8,128)(2,1)S(1)}, u32[]{:S(2)}, u32[]{:S(2)}) collective-permute-start(bf16[128,512]{1,0:T(8,128)(2,1)S(1)} %constant_dynamic-update-slice_fusion.refs_5_), channel_id=1, source_target_pairs={{0,6},{1,7},{2,4},{3,5},{4,2},{5,3},{6,0},{7,1},{8,14},{9,15},{10,... | collective-permute-start | bytes 393224 | tf_op jit(solution)/shard_map/ppermute | solution.py:51
  62.2 0.0 collective-permute-start.17
  62.2 3.2 %collective-permute-start.16 = (bf16[128,512]{1,0:T(8,128)(2,1)S(1)}, bf16[128,512]{1,0:T(8,128)(2,1)S(1)}, u32[]{:S(2)}, u32[]{:S(2)}) collective-permute-start(bf16[128,512]{1,0:T(8,128)(2,1)S(1)} %constant_dynamic-update-slice_fusion.refs_5_), channel_id=1, source_target_pairs={{0,2},{1,3},{2,0},{3,1},{4,6},{5,7},{6,4},{7,5},{8,10},{9,11},{10,... | collective-permute-start | bytes 393224 | tf_op jit(solution)/shard_map/ppermute | solution.py:51
  65.4 0.4 fusion.refs_2_
  65.8 0.3 copy-done.6
  66.1 2.2 %shard_map.92 = (bf16[2048,512]{1,0:T(8,128)(2,1)S(1)}, bf16[2048,512]{1,0:T(8,128)(2,1)S(1)}) custom-call(s32[1]{0:T(128)} %bitcast.refs_0_, s32[1,2048]{1,0:T(1,128)S(1)} %copy-done.6, bf16[2048,512]{1,0:T(8,128)(2,1)S(1)} %fusion.refs_2_, bf16[256,512]{1,0:T(8,128)(2,1)S(1)} %get-tuple-element.26.refs_3_, ...), custom_call_target="tpu_custom_call" | custom-call | tf_op jit(solution)/shard_map/pallas_call | solution.py:352
  68.3 0.0 collective-permute-done.18.refs_8_
  68.3 2.3 %collective-permute-done.17.refs_7_ = bf16[128,512]{1,0:T(8,128)(2,1)S(1)} collective-permute-done((bf16[128,512]{1,0:T(8,128)(2,1)S(1)}, bf16[128,512]{1,0:T(8,128)(2,1)S(1)}, u32[]{:S(2)}, u32[]{:S(2)}) %collective-permute-start.17) | collective-permute-done | bytes 131104 | tf_op jit(solution)/shard_map/ppermute | solution.py:51
  70.6 0.0 collective-permute-done.16.refs_6_
  70.6 0.0 copy-done.2
  70.6 0.0 copy-done.4
  70.6 15.8 %shard_map.101 = bf16[256,512]{1,0:T(8,128)(2,1)} custom-call(s32[1]{0:T(128)} %bitcast.refs_0_, bf16[2048,512]{1,0:T(8,128)(2,1)S(1)} %get-tuple-element.27.refs_1_, bf16[2048,512]{1,0:T(8,128)(2,1)S(1)} %get-tuple-element.28.refs_2_, bf16[512,1536]{1,0:T(8,128)(2,1)S(1)} %copy-done.2, bf16[512,512]{1,0:T(8,128)(2,1)S(1)} %copy-done.4, ...), custom_call_target="tpu_custom_call" | custom-call | tf_op jit(solution)/shard_map/pallas_call | solution.py:421
  (19 shorter events, 0.2 us)
Async XLA Ops:
  0.0 49.2 %collective-permute-start.12 = (bf16[1024,1024]{1,0:T(8,128)(2,1)}, bf16[1024,1024]{1,0:T(8,128)(2,1)S(1)}, u32[]{:S(2)}, u32[]{:S(2)}) collective-permute-start(bf16[1024,1024]{1,0:T(8,128)(2,1)} %bitcast.5), channel_id=1, source_target_pairs={{0,8},{8,0},{16,24},{24,16},{1,9},{9,1},{17,25},{25,17},{2,10},{10... | collective-permute-start | bytes 6291464 | tf_op jit(solution)/shard_map/ppermute | solution.py:51
  0.5 48.7 %collective-permute-start.13 = (bf16[1024,1024]{1,0:T(8,128)(2,1)}, bf16[1024,1024]{1,0:T(8,128)(2,1)}, u32[]{:S(2)}, u32[]{:S(2)}) collective-permute-start(bf16[1024,1024]{1,0:T(8,128)(2,1)} %bitcast.7), channel_id=1, source_target_pairs={{0,8},{8,0},{16,24},{24,16},{1,9},{9,1},{17,25},{25,17},{2,10},{10... | collective-permute-start | bytes 6291464 | tf_op jit(solution)/shard_map/ppermute | solution.py:51
  0.5 0.7 copy-start.5
  4.8 20.4 %collective-permute-start = (bf16[256,512]{1,0:T(8,128)(2,1)S(1)}, bf16[256,512]{1,0:T(8,128)(2,1)S(1)}, u32[]{:S(2)}, u32[]{:S(2)}) collective-permute-start(bf16[256,512]{1,0:T(8,128)(2,1)S(1)} %get-tuple-element.26.refs_3_), channel_id=1, source_target_pairs={{0,4},{1,5},{2,6},{3,7},{4,0},{5,1},{6,2},{7,3},{8,12},{9,13},{10,... | collective-permute-start | bytes 786440 | tf_op jit(solution)/shard_map/ppermute | solution.py:51
  10.0 13.2 %collective-permute-start.5 = (bf16[128,1152]{1,0:T(8,128)(2,1)S(1)}, bf16[128,1152]{1,0:T(8,128)(2,1)S(1)}, u32[]{:S(2)}, u32[]{:S(2)}) collective-permute-start(bf16[128,1152]{1,0:T(8,128)(2,1)S(1)} %get-tuple-element.32), channel_id=1, source_target_pairs={{0,2},{1,3},{2,0},{3,1},{4,6},{5,7},{6,4},{7,5},{8,10},{9,11},{10,... | collective-permute-start | bytes 884744 | tf_op jit(solution)/shard_map/ppermute | solution.py:51
  11.7 13.5 %collective-permute-start.8 = (bf16[128,1152]{1,0:T(8,128)(2,1)S(1)}, bf16[128,1152]{1,0:T(8,128)(2,1)S(1)}, u32[]{:S(2)}, u32[]{:S(2)}) collective-permute-start(bf16[128,1152]{1,0:T(8,128)(2,1)S(1)} %get-tuple-element.38), channel_id=1, source_target_pairs={{0,1},{1,0},{2,3},{3,2},{4,5},{5,4},{6,7},{7,6},{8,9},{9,8},{10,11... | collective-permute-start | bytes 884744 | tf_op jit(solution)/shard_map/ppermute | solution.py:51
  23.5 6.8 %collective-permute-start.6 = (bf16[64,1152]{1,0:T(8,128)(2,1)S(1)}, bf16[64,1152]{1,0:T(8,128)(2,1)S(1)}, u32[]{:S(2)}, u32[]{:S(2)}) collective-permute-start(bf16[64,1152]{1,0:T(8,128)(2,1)S(1)} %get-tuple-element.34), channel_id=1, source_target_pairs={{0,1},{1,0},{2,3},{3,2},{4,5},{5,4},{6,7},{7,6},{8,9},{9,8},{10,11... | collective-permute-start | bytes 442376 | tf_op jit(solution)/shard_map/ppermute | solution.py:51
  25.2 24.0 %copy-start.3 = (bf16[1024,512]{1,0:T(8,128)(2,1)S(1)}, bf16[1024,512]{1,0:T(8,128)(2,1)}, u32[]{:S(2)}) copy-start(bf16[1024,512]{1,0:T(8,128)(2,1)} %refs_6_.1) | copy-start | bytes 3145732
  25.6 5.8 %collective-permute-start.9 = (bf16[64,1152]{1,0:T(8,128)(2,1)S(1)}, bf16[64,1152]{1,0:T(8,128)(2,1)S(1)}, u32[]{:S(2)}, u32[]{:S(2)}) collective-permute-start(bf16[64,1152]{1,0:T(8,128)(2,1)S(1)} %get-tuple-element.40), channel_id=1, source_target_pairs={{0,2},{1,3},{2,0},{3,1},{4,6},{5,7},{6,4},{7,5},{8,10},{9,11},{10,... | collective-permute-start | bytes 442376 | tf_op jit(solution)/shard_map/ppermute | solution.py:51
  25.9 23.3 %copy-start.1 = (bf16[1,1024,1024]{2,1,0:T(8,128)(2,1)S(1)}, bf16[1,1024,1024]{2,1,0:T(8,128)(2,1)}, u32[]{:S(2)}) copy-start(bf16[1,1024,1024]{2,1,0:T(8,128)(2,1)} %param.12) | copy-start | bytes 6291460
  25.9 23.3 %copy-start = (bf16[1,1024,1024]{2,1,0:T(8,128)(2,1)S(1)}, bf16[1,1024,1024]{2,1,0:T(8,128)(2,1)}, u32[]{:S(2)}) copy-start(bf16[1,1024,1024]{2,1,0:T(8,128)(2,1)} %param.11) | copy-start | bytes 6291460
  25.9 17.7 %collective-permute-start.1 = (bf16[256,512]{1,0:T(8,128)(2,1)S(1)}, bf16[256,512]{1,0:T(8,128)(2,1)S(1)}, u32[]{:S(2)}, u32[]{:S(2)}) collective-permute-start(bf16[256,512]{1,0:T(8,128)(2,1)S(1)} %pad_maximum_fusion.2), channel_id=1, source_target_pairs={{0,1},{1,0},{2,3},{3,2},{4,5},{5,4},{6,7},{7,6},{8,9},{9,8},{10,11... | collective-permute-start | bytes 786440 | tf_op jit(solution)/shard_map/ppermute | solution.py:51
  30.6 7.4 %collective-permute-start.7 = (bf16[32,1152]{1,0:T(8,128)(2,1)S(1)}, bf16[32,1152]{1,0:T(8,128)(2,1)S(1)}, u32[]{:S(2)}, u32[]{:S(2)}) collective-permute-start(bf16[32,1152]{1,0:T(8,128)(2,1)S(1)} %get-tuple-element.36), channel_id=1, source_target_pairs={{0,4},{1,5},{2,6},{3,7},{4,0},{5,1},{6,2},{7,3},{8,12},{9,13},{10,... | collective-permute-start | bytes 221192 | tf_op jit(solution)/shard_map/ppermute | solution.py:51
  31.3 12.2 %collective-permute-start.2 = (bf16[256,512]{1,0:T(8,128)(2,1)S(1)}, bf16[256,512]{1,0:T(8,128)(2,1)S(1)}, u32[]{:S(2)}, u32[]{:S(2)}) collective-permute-start(bf16[256,512]{1,0:T(8,128)(2,1)S(1)} %pad_maximum_fusion.3), channel_id=1, source_target_pairs={{0,2},{1,3},{2,0},{3,1},{4,6},{5,7},{6,4},{7,5},{8,10},{9,11},{10,... | collective-permute-start | bytes 786440 | tf_op jit(solution)/shard_map/ppermute | solution.py:51
  38.0 5.3 %collective-permute-start.10 = (bf16[32,1152]{1,0:T(8,128)(2,1)S(1)}, bf16[32,1152]{1,0:T(8,128)(2,1)S(1)}, u32[]{:S(2)}, u32[]{:S(2)}) collective-permute-start(bf16[32,1152]{1,0:T(8,128)(2,1)S(1)} %get-tuple-element.42), channel_id=1, source_target_pairs={{0,4},{1,5},{2,6},{3,7},{4,0},{5,1},{6,2},{7,3},{8,12},{9,13},{10,... | collective-permute-start | bytes 221192 | tf_op jit(solution)/shard_map/ppermute | solution.py:51
  43.6 5.6 %collective-permute-start.11 = (bf16[64,1024]{1,0:T(8,128)(2,1)S(1)}, bf16[64,1024]{1,0:T(8,128)(2,1)S(1)}, u32[]{:S(2)}, u32[]{:S(2)}) collective-permute-start(bf16[64,1024]{1,0:T(8,128)(2,1)S(1)} %pad_maximum_fusion.4.refs_0_), channel_id=1, source_target_pairs={{0,16},{8,24},{16,0},{24,8},{1,17},{9,25},{17,1},{25,9},{2,18},{10... | collective-permute-start | bytes 393224 | tf_op jit(solution)/shard_map/ppermute | solution.py:51
  45.3 11.4 %collective-permute-start.4 = (bf16[512,512]{1,0:T(8,128)(2,1)S(1)}, bf16[512,512]{1,0:T(8,128)(2,1)S(1)}, u32[]{:S(2)}, u32[]{:S(2)}) collective-permute-start(bf16[512,512]{1,0:T(8,128)(2,1)S(1)} %pad_maximum_fusion.1), channel_id=1, source_target_pairs={{0,1},{1,0},{2,3},{3,2},{4,5},{5,4},{6,7},{7,6},{8,9},{9,8},{10,11... | collective-permute-start | bytes 1572872 | tf_op jit(solution)/shard_map/ppermute | solution.py:51
  46.6 10.1 %collective-permute-start.3 = (bf16[512,512]{1,0:T(8,128)(2,1)S(1)}, bf16[512,512]{1,0:T(8,128)(2,1)S(1)}, u32[]{:S(2)}, u32[]{:S(2)}) collective-permute-start(bf16[512,512]{1,0:T(8,128)(2,1)S(1)} %pad_maximum_fusion), channel_id=1, source_target_pairs={{0,2},{1,3},{2,0},{3,1},{4,6},{5,7},{6,4},{7,5},{8,10},{9,11},{10,... | collective-permute-start | bytes 1572872 | tf_op jit(solution)/shard_map/ppermute | solution.py:51
  52.3 4.3 %collective-permute-start.14 = (bf16[64,512]{1,0:T(8,128)(2,1)S(1)}, bf16[64,512]{1,0:T(8,128)(2,1)S(1)}, u32[]{:S(2)}, u32[]{:S(2)}) collective-permute-start(bf16[64,512]{1,0:T(8,128)(2,1)S(1)} %get-tuple-element.45), channel_id=1, source_target_pairs={{0,16},{8,24},{16,0},{24,8},{1,17},{9,25},{17,1},{25,9},{2,18},{10... | collective-permute-start | bytes 196616 | tf_op jit(solution)/shard_map/ppermute | solution.py:51
  54.1 0.7 copy-start.7
  56.7 4.3 %collective-permute-start.15 = (bf16[64,512]{1,0:T(8,128)(2,1)S(1)}, bf16[64,512]{1,0:T(8,128)(2,1)S(1)}, u32[]{:S(2)}, u32[]{:S(2)}) collective-permute-start(bf16[64,512]{1,0:T(8,128)(2,1)S(1)} %add_convert_fusion), channel_id=1, source_target_pairs={{0,1},{1,0},{2,3},{3,2},{4,5},{5,4},{6,7},{7,6},{8,9},{9,8},{10,11... | collective-permute-start | bytes 196616 | tf_op jit(solution)/shard_map/ppermute | solution.py:51
  61.0 7.3 %collective-permute-start.18 = (bf16[128,512]{1,0:T(8,128)(2,1)S(1)}, bf16[128,512]{1,0:T(8,128)(2,1)S(1)}, u32[]{:S(2)}, u32[]{:S(2)}) collective-permute-start(bf16[128,512]{1,0:T(8,128)(2,1)S(1)} %constant_dynamic-update-slice_fusion.refs_5_), channel_id=1, source_target_pairs={{0,6},{1,7},{2,4},{3,5},{4,2},{5,3},{6,0},{7,1},{8,14},{9,15},{10,... | collective-permute-start | bytes 393224 | tf_op jit(solution)/shard_map/ppermute | solution.py:51
  62.2 8.4 %collective-permute-start.17 = (bf16[128,512]{1,0:T(8,128)(2,1)S(1)}, bf16[128,512]{1,0:T(8,128)(2,1)S(1)}, u32[]{:S(2)}, u32[]{:S(2)}) collective-permute-start(bf16[128,512]{1,0:T(8,128)(2,1)S(1)} %constant_dynamic-update-slice_fusion.refs_5_), channel_id=1, source_target_pairs={{0,4},{1,5},{2,6},{3,7},{4,0},{5,1},{6,2},{7,3},{8,12},{9,13},{10,... | collective-permute-start | bytes 393224 | tf_op jit(solution)/shard_map/ppermute | solution.py:51
  62.2 8.4 %collective-permute-start.16 = (bf16[128,512]{1,0:T(8,128)(2,1)S(1)}, bf16[128,512]{1,0:T(8,128)(2,1)S(1)}, u32[]{:S(2)}, u32[]{:S(2)}) collective-permute-start(bf16[128,512]{1,0:T(8,128)(2,1)S(1)} %constant_dynamic-update-slice_fusion.refs_5_), channel_id=1, source_target_pairs={{0,2},{1,3},{2,0},{3,1},{4,6},{5,7},{6,4},{7,5},{8,10},{9,11},{10,... | collective-permute-start | bytes 393224 | tf_op jit(solution)/shard_map/ppermute | solution.py:51
  65.4 0.7 copy-start.6
  66.1 4.5 %copy-start.2 = (bf16[512,1536]{1,0:T(8,128)(2,1)S(1)}, bf16[512,1536]{1,0:T(8,128)(2,1)}, u32[]{:S(2)}) copy-start(bf16[512,1536]{1,0:T(8,128)(2,1)} %refs_3_.3) | copy-start | bytes 4718596
  66.1 4.5 %copy-start.4 = (bf16[512,512]{1,0:T(8,128)(2,1)S(1)}, bf16[512,512]{1,0:T(8,128)(2,1)}, u32[]{:S(2)}) copy-start(bf16[512,512]{1,0:T(8,128)(2,1)} %refs_4_.1) | copy-start | bytes 1572868

commit v6 on v5

--- a/solution.py
+++ b/solution.py
@@ -56,6 +56,10 @@
     first = bits[1:2] + bits[0:1] + bits[2:]
     second = bits
     return first, second
+
+
+def path_shares(block):
+    return (block // 4, block - block // 4) if block % 64 == 0 else (block // 2, block // 2)
 
 
 def ranks_of(order):
@@ -146,8 +150,10 @@
     return jnp.concatenate(picks, axis=0)
 
 
-def rows_kernel(count, place_ref, listing_ref, tokens_hbm, keys_hbm, picked_ref, normed_ref, logits_ref, *refs):
-    tokens_ref, keys_ref, sems = refs
+def rows_kernel(count, place_ref, listing_hbm, tokens_hbm, keys_hbm, picked_ref, normed_ref, logits_ref, *refs):
+    listing_ref, tokens_ref, keys_ref, listing_sem, sems = refs
+    listing_copy = pltpu.make_async_copy(listing_hbm, listing_ref, listing_sem)
+    listing_copy.start()
     rows, width = tokens_ref.shape
     pieces = sems.shape[1]
     token_step, key_step = rows // pieces, width // pieces
@@ -160,6 +166,7 @@
         copies.append(pltpu.make_async_copy(keys_hbm.at[part], keys_ref.at[part], sems.at[1, piece]))
     for copy in copies:
         copy.start()
+    listing_copy.wait()
     picker = picker_of(place_ref[0], listing_ref, rows, count)
     parts = []
     for piece in range(pieces):
@@ -188,15 +195,17 @@
             jax.ShapeDtypeStruct((rows, width), BF16),
             jax.ShapeDtypeStruct((rows, slots), F32),
         ),
-        in_specs=[SMEM, VMEM, HBM, HBM],
+        in_specs=[SMEM, HBM, HBM, HBM],
         out_specs=(VMEM,) * 3,
         scratch_shapes=[
+            pltpu.VMEM(listing.shape, jnp.int32),
             pltpu.VMEM((rows, width), BF16),
             pltpu.VMEM((width, slots), BF16),
+            pltpu.SemaphoreType.DMA,
             pltpu.SemaphoreType.DMA((2, pieces)),
         ],
         compiler_params=pltpu.CompilerParams(vmem_limit_bytes=24 << 20),
-    )(place, listing, *(pltpu.with_memory_space_constraint(array, pltpu.HBM) for array in (tokens, slot_keys)))
+    )(place, *(pltpu.with_memory_space_constraint(array, pltpu.HBM) for array in (listing, tokens, slot_keys)))
 
 
 def sums_kernel(orders, place_ref, normed_ref, logits_ref, *refs):
@@ -210,29 +219,38 @@
     myself = place_ref[0]
     count = 1 << len(orders[0])
     block = slots // count
-    half = block // 2
+    shares = path_shares(block)
+    first = 0
     for path, order in enumerate(orders):
+        share = shares[path]
         for place, relative in enumerate(ranks_of(order)):
-            source = pl.ds(pl.multiple_of((myself ^ relative) * block + path * half, half), half)
-            target = pl.ds((path * count + place) * half, half)
+            source = pl.ds(pl.multiple_of((myself ^ relative) * block + path * shares[0], 16), share)
+            target = pl.ds(first + place * share, share)
             picked_ref[target, :] = turned_ref[source, :]
             picked_tops_ref[target, :] = tops_ref[source, :]
+        first = first + count * share
     picked = picked_ref[...]
     sums = jnp.dot(picked, normed_ref[...], preferred_element_type=F32).astype(BF16)
     totals = jnp.dot(picked, jnp.ones((rows, LANES), BF16), preferred_element_type=F32)
     stats = pack(picked_tops_ref[...], totals)
-    quarter = slots // 4
-    for index, out_ref in enumerate(outs):
-        out_ref[:, :width] = sums[index * quarter : (index + 1) * quarter, :]
-        out_ref[:, width:] = stats[index * quarter : (index + 1) * quarter, :]
+    start = 0
+    for out_ref in outs:
+        end = start + out_ref.shape[0]
+        out_ref[:, :width] = sums[start:end, :]
+        out_ref[:, width:] = stats[start:end, :]
+        start = end
 
 
 def own_sums(place, normed, logits, orders):
     rows, width = normed.shape
     slots = logits.shape[1]
+    count = 1 << len(orders[0])
+    shares = path_shares(slots // count)
     return pl.pallas_call(
         lambda *refs: sums_kernel(orders, *refs),
-        out_shape=(jax.ShapeDtypeStruct((slots // 4, width + LANES), BF16),) * 4,
+        out_shape=tuple(
+            jax.ShapeDtypeStruct((share * count // 2, width + LANES), BF16) for share in shares for _ in range(2)
+        ),
         in_specs=[SMEM, VMEM, VMEM],
         out_specs=(VMEM,) * 4,
         scratch_shapes=[
@@ -476,9 +494,9 @@
         state = [merge(state[path][0], arrived[path], step == steps - 1) for path in range(2)]
     slot_in = jnp.concatenate(state, axis=0)
 
-    (slot_in,) = tie([slot_in], [array for group in brought[1:-1] for array in group])
     others = [2 * step for step in range(1, n_clip // 2)]
     rows = [slot_in] + [swap(slot_in, "clip", mask) for mask in others]
+    rows = list(tie(rows, [array for group in brought[1:-1] for array in group]))
     results = experts(rows, first, first_other, second, second_other, w_proj)
     slot_proj = results[0].astype(F32)
     for mask, result in zip(others, results[1:]):

time: 86.7 us -> 84.3 us (0.972)
  waiting for transfers between devices: 31.7 us -> 26.4 us
  starting transfers between devices: 23.6 us -> 26.7 us
    ppermute x19, waiting for transfers between devices: 31.7 us -> 26.4 us  [swap(): lax.ppermute(values, axis, [(index, index ^ mask) for index in range(coun...]
    ppermute x19, starting transfers between devices: 23.6 us -> 26.7 us  [swap(): lax.ppermute(values, axis, [(index, index ^ mask) for index in range(coun...]
  transfers between devices with their start and end apart: 19 -> 19, of which waited for: 9 -> 8; matrix products, arithmetic and copies ran while one was open for 2% -> 3% of each run, Pallas kernels for 14% -> 15%
where the time goes in v6:
time: 84.3 us; the launch traced here: 84.1 us
  Pallas kernels  28.1 us (33%)
  starting transfers between devices  26.7 us (32%)
  waiting for transfers between devices  26.4 us (31%)
  other arithmetic  2.1 us (2%)
    ppermute x19, starting transfers between devices, swap(): lax.ppermute(values, axis, [(index, index ^ mask) for index in range(coun...  26.7 us
    ppermute x19, waiting for transfers between devices, swap(): lax.ppermute(values, axis, [(index, index ^ mask) for index in range(coun...  26.4 us
    pallas_call x1, Pallas kernels, tail(): pl.pallas_call(lambda *refs: tail_kernel(ranks, starts, half, *refs), out...  15.8 us
    pallas_call x1, Pallas kernels, rows_and_picks(): pl.pallas_call(lambda *refs: rows_kernel(count, *refs), out_shape=(jax.Sh...  4.03 us
    pallas_call x1, Pallas kernels, experts(): pl.pallas_call(lambda *refs: experts_kernel(count, *refs), out_shape=(jax...  3.08 us
    pallas_call x1, Pallas kernels, put_in_order(): pl.pallas_call(lambda *refs: order_kernel(ranks, starts, vis_dev, *refs),...  2.19 us
    pallas_call x6, Pallas kernels, merge(): pl.pallas_call(merge_kernel, out_shape=shape, in_specs=[VMEM, VMEM], out_...  1.83 us
  transfers between devices with their start and end apart: 19, of which 8 were waited for; matrix products, arithmetic and copies ran while one was open for 3% of the time, Pallas kernels for 15%

profile of v6, /device:TPU:0, one launch (start us, length us, event | category | flops | bytes accessed | tf_op | source)
XLA Modules:
  0.0 84.1 jit_solution(10285071734953003573)
XLA Ops:
  0.0 0.5 collective-permute-start.12
  0.5 0.1 collective-permute-start.13
  0.5 4.0 %shard_map.91 = (bf16[256,512]{1,0:T(8,128)(2,1)S(1)}, bf16[512,1024]{1,0:T(8,128)(2,1)S(1)}, f32[512,512]{1,0:T(8,128)S(1)}) custom-call(s32[1]{0:T(128)} %bitcast.refs_0_, s32[1,2048]{1,0:T(1,128)} %refs_1_.3, bf16[512,1024]{1,0:T(8,128)(2,1)} %refs_2_.1, bf16[1024,512]{1,0:T(8,128)(2,1)} %refs_3_.2), custom_call_target="tpu_custom_call" | custom-call | tf_op jit(solution)/shard_map/pallas_call | solution.py:191
  4.6 1.1 %shard_map.93 = (bf16[64,1152]{1,0:T(8,128)(2,1)S(1)}, bf16[64,1152]{1,0:T(8,128)(2,1)S(1)}, bf16[192,1152]{1,0:T(8,128)(2,1)S(1)}, bf16[192,1152]{1,0:T(8,128)(2,1)S(1)}) custom-call(s32[1]{0:T(128)} %bitcast.refs_0_, bf16[512,1024]{1,0:T(8,128)(2,1)S(1)} %get-tuple-element.30.refs_1_, f32[512,512]{1,0:T(8,128)S(1)} %get-tuple-element.31.refs_2_), custom_call_target="tpu_custom_call" | custom-call | tf_op jit(solution)/shard_map/pallas_call | solution.py:249
  5.7 3.1 %collective-permute-start.5 = (bf16[64,1152]{1,0:T(8,128)(2,1)S(1)}, bf16[64,1152]{1,0:T(8,128)(2,1)S(1)}, u32[]{:S(2)}, u32[]{:S(2)}) collective-permute-start(bf16[64,1152]{1,0:T(8,128)(2,1)S(1)} %get-tuple-element.33), channel_id=1, source_target_pairs={{0,2},{1,3},{2,0},{3,1},{4,6},{5,7},{6,4},{7,5},{8,10},{9,11},{10,... | collective-permute-start | bytes 442376 | tf_op jit(solution)/shard_map/ppermute | solution.py:51
  8.8 2.6 %collective-permute-start = (bf16[256,512]{1,0:T(8,128)(2,1)S(1)}, bf16[256,512]{1,0:T(8,128)(2,1)S(1)}, u32[]{:S(2)}, u32[]{:S(2)}) collective-permute-start(bf16[256,512]{1,0:T(8,128)(2,1)S(1)} %get-tuple-element.27.refs_3_), channel_id=1, source_target_pairs={{0,4},{1,5},{2,6},{3,7},{4,0},{5,1},{6,2},{7,3},{8,12},{9,13},{10,... | collective-permute-start | bytes 786440 | tf_op jit(solution)/shard_map/ppermute | solution.py:51
  11.4 1.5 %collective-permute-start.8 = (bf16[192,1152]{1,0:T(8,128)(2,1)S(1)}, bf16[192,1152]{1,0:T(8,128)(2,1)S(1)}, u32[]{:S(2)}, u32[]{:S(2)}) collective-permute-start(bf16[192,1152]{1,0:T(8,128)(2,1)S(1)} %get-tuple-element.39), channel_id=1, source_target_pairs={{0,1},{1,0},{2,3},{3,2},{4,5},{5,4},{6,7},{7,6},{8,9},{9,8},{10,11... | collective-permute-start | bytes 1327112 | tf_op jit(solution)/shard_map/ppermute | solution.py:51
  12.9 1.0 %multiply_cosine_fusion = (f32[256,256]{1,0:T(8,128)S(1)}, f32[256,256]{1,0:T(8,128)S(1)}) fusion(f32[256]{0:T(256)S(1)} %multiply_exponential_fusion, f32[256]{0:T(256)S(1)} %iota_convert_fusion), kind=kLoop, calls=%fused_computation.7 | loop fusion | flops 65536 | bytes 526336 | tf_op jit(solution)/shard_map/cos | solution.py:460
  13.9 1.6 %collective-permute-done.5.came_ref = bf16[64,1152]{1,0:T(8,128)(2,1)S(1)} collective-permute-done((bf16[64,1152]{1,0:T(8,128)(2,1)S(1)}, bf16[64,1152]{1,0:T(8,128)(2,1)S(1)}, u32[]{:S(2)}, u32[]{:S(2)}) %collective-permute-start.5) | collective-permute-done | bytes 147488 | tf_op jit(solution)/shard_map/ppermute | solution.py:51
  15.5 0.3 shard_map.94
  15.8 1.9 %collective-permute-start.6 = (bf16[32,1152]{1,0:T(8,128)(2,1)S(1)}, bf16[32,1152]{1,0:T(8,128)(2,1)S(1)}, u32[]{:S(2)}, u32[]{:S(2)}) collective-permute-start(bf16[32,1152]{1,0:T(8,128)(2,1)S(1)} %get-tuple-element.35), channel_id=1, source_target_pairs={{0,1},{1,0},{2,3},{3,2},{4,5},{5,4},{6,7},{7,6},{8,9},{9,8},{10,11... | collective-permute-start | bytes 221192 | tf_op jit(solution)/shard_map/ppermute | solution.py:51
  17.7 6.8 %collective-permute-done.6.came_ref = bf16[32,1152]{1,0:T(8,128)(2,1)S(1)} collective-permute-done((bf16[32,1152]{1,0:T(8,128)(2,1)S(1)}, bf16[32,1152]{1,0:T(8,128)(2,1)S(1)}, u32[]{:S(2)}, u32[]{:S(2)}) %collective-permute-start.6) | collective-permute-done | bytes 73760 | tf_op jit(solution)/shard_map/ppermute | solution.py:51
  24.5 0.3 shard_map.95
  24.7 0.4 collective-permute-start.7
  25.1 0.0 collective-permute-done.refs_4_
  25.1 0.0 copy-start.3
  25.1 0.0 collective-permute-done.8.came_ref
  25.1 0.5 shard_map.97
  25.6 0.5 collective-permute-start.9
  26.1 0.0 copy-start
  26.1 0.0 copy-start.1
  26.1 1.6 %collective-permute-start.1 = (bf16[256,512]{1,0:T(8,128)(2,1)S(1)}, bf16[256,512]{1,0:T(8,128)(2,1)S(1)}, u32[]{:S(2)}, u32[]{:S(2)}) collective-permute-start(bf16[256,512]{1,0:T(8,128)(2,1)S(1)} %pad_maximum_fusion.2), channel_id=1, source_target_pairs={{0,1},{1,0},{2,3},{3,2},{4,5},{5,4},{6,7},{7,6},{8,9},{9,8},{10,11... | collective-permute-start | bytes 786440 | tf_op jit(solution)/shard_map/ppermute | solution.py:51
  27.8 4.3 %collective-permute-done.9.came_ref = bf16[96,1152]{1,0:T(8,128)(2,1)S(1)} collective-permute-done((bf16[96,1152]{1,0:T(8,128)(2,1)S(1)}, bf16[96,1152]{1,0:T(8,128)(2,1)S(1)}, u32[]{:S(2)}, u32[]{:S(2)}) %collective-permute-start.9) | collective-permute-done | bytes 221216 | tf_op jit(solution)/shard_map/ppermute | solution.py:51
  32.1 0.3 collective-permute-start.2
  32.4 0.3 shard_map.98
  32.7 0.0 collective-permute-done.7.came_ref
  32.7 2.4 %collective-permute-start.10 = (bf16[48,1152]{1,0:T(8,128)(2,1)S(1)}, bf16[48,1152]{1,0:T(8,128)(2,1)S(1)}, u32[]{:S(2)}, u32[]{:S(2)}) collective-permute-start(bf16[48,1152]{1,0:T(8,128)(2,1)S(1)} %get-tuple-element.43), channel_id=1, source_target_pairs={{0,4},{1,5},{2,6},{3,7},{4,0},{5,1},{6,2},{7,3},{8,12},{9,13},{10,... | collective-permute-start | bytes 331784 | tf_op jit(solution)/shard_map/ppermute | solution.py:51
  35.1 0.1 multiply_sine_fusion.1
  35.2 0.2 shard_map.96
  35.5 3.6 %collective-permute-done.10.came_ref = bf16[48,1152]{1,0:T(8,128)(2,1)S(1)} collective-permute-done((bf16[48,1152]{1,0:T(8,128)(2,1)S(1)}, bf16[48,1152]{1,0:T(8,128)(2,1)S(1)}, u32[]{:S(2)}, u32[]{:S(2)}) %collective-permute-start.10) | collective-permute-done | bytes 110624 | tf_op jit(solution)/shard_map/ppermute | solution.py:51
  39.1 0.3 shard_map.99
  39.3 1.5 %collective-permute-start.11 = (bf16[64,1024]{1,0:T(8,128)(2,1)S(1)}, bf16[64,1024]{1,0:T(8,128)(2,1)S(1)}, u32[]{:S(2)}, u32[]{:S(2)}) collective-permute-start(bf16[64,1024]{1,0:T(8,128)(2,1)S(1)} %pad_maximum_fusion.4.refs_0_), channel_id=1, source_target_pairs={{0,16},{8,24},{16,0},{24,8},{1,17},{9,25},{17,1},{25,9},{2,18},{10... | collective-permute-start | bytes 393224 | tf_op jit(solution)/shard_map/ppermute | solution.py:51
  40.9 0.0 collective-permute-done.2.refs_6_
  40.9 1.6 %collective-permute-start.4 = (bf16[512,512]{1,0:T(8,128)(2,1)S(1)}, bf16[512,512]{1,0:T(8,128)(2,1)S(1)}, u32[]{:S(2)}, u32[]{:S(2)}) collective-permute-start(bf16[512,512]{1,0:T(8,128)(2,1)S(1)} %pad_maximum_fusion.1), channel_id=1, source_target_pairs={{0,1},{1,0},{2,3},{3,2},{4,5},{5,4},{6,7},{7,6},{8,9},{9,8},{10,11... | collective-permute-start | bytes 1572872 | tf_op jit(solution)/shard_map/ppermute | solution.py:51
  42.5 0.0 collective-permute-done.1.refs_5_
  42.5 3.3 %collective-permute-start.3 = (bf16[512,512]{1,0:T(8,128)(2,1)S(1)}, bf16[512,512]{1,0:T(8,128)(2,1)S(1)}, u32[]{:S(2)}, u32[]{:S(2)}) collective-permute-start(bf16[512,512]{1,0:T(8,128)(2,1)S(1)} %pad_maximum_fusion), channel_id=1, source_target_pairs={{0,2},{1,3},{2,0},{3,1},{4,6},{5,7},{6,4},{7,5},{8,10},{9,11},{10,... | collective-permute-start | bytes 1572872 | tf_op jit(solution)/shard_map/ppermute | solution.py:51
  45.9 0.0 collective-permute-done.11.refs_1_
  45.9 0.0 collective-permute-done.12.refs_3_
  45.9 0.0 collective-permute-done.13.refs_5_
  45.9 0.0 copy-done.3
  45.9 0.0 copy-done
  45.9 0.0 copy-done.1
  45.9 3.1 %shard_map.100 = (bf16[64,512]{1,0:T(8,128)(2,1)S(1)}, bf16[64,512]{1,0:T(8,128)(2,1)S(1)}) custom-call(bf16[64,1024]{1,0:T(8,128)(2,1)S(1)} %pad_maximum_fusion.4.refs_0_, bf16[64,1024]{1,0:T(8,128)(2,1)S(1)} %collective-permute-done.11.refs_1_, bf16[1024,1024]{1,0:T(8,128)(2,1)S(1)} %bitcast.6, bf16[1024,1024]{1,0:T(8,128)(2,1)S(1)} %collective-permute-done.12.refs_3_, ...), custom_call_target="tpu_custom_call" | custom-call | tf_op jit(solution)/shard_map/pallas_call | solution.py:328
  49.0 0.6 collective-permute-start.14
  49.6 0.0 copy-start.6
  49.6 0.4 multiply_add_fusion
  50.1 0.2 copy-done.6
  50.3 3.1 %collective-permute-done.14 = bf16[64,512]{1,0:T(8,128)(2,1)S(1)} collective-permute-done((bf16[64,512]{1,0:T(8,128)(2,1)S(1)}, bf16[64,512]{1,0:T(8,128)(2,1)S(1)}, u32[]{:S(2)}, u32[]{:S(2)}) %collective-permute-start.14) | collective-permute-done | bytes 65568 | tf_op jit(solution)/shard_map/ppermute | solution.py:51
  53.4 0.0 collective-permute-done.4.refs_8_
  53.4 0.3 collective-permute-done.3.refs_7_
  53.6 0.5 collective-permute-start.15
  54.1 3.8 %collective-permute-done.15 = bf16[64,512]{1,0:T(8,128)(2,1)S(1)} collective-permute-done((bf16[64,512]{1,0:T(8,128)(2,1)S(1)}, bf16[64,512]{1,0:T(8,128)(2,1)S(1)}, u32[]{:S(2)}, u32[]{:S(2)}) %collective-permute-start.15) | collective-permute-done | bytes 65568 | tf_op jit(solution)/shard_map/ppermute | solution.py:51
  57.9 2.3 %collective-permute-start.18 = (bf16[128,512]{1,0:T(8,128)(2,1)S(1)}, bf16[128,512]{1,0:T(8,128)(2,1)S(1)}, u32[]{:S(2)}, u32[]{:S(2)}) collective-permute-start(bf16[128,512]{1,0:T(8,128)(2,1)S(1)} %constant_dynamic-update-slice_fusion.refs_5_), channel_id=1, source_target_pairs={{0,6},{1,7},{2,4},{3,5},{4,2},{5,3},{6,0},{7,1},{8,14},{9,15},{10,... | collective-permute-start | bytes 393224 | tf_op jit(solution)/shard_map/ppermute | solution.py:51
  60.2 0.9 %collective-permute-start.17 = (bf16[128,512]{1,0:T(8,128)(2,1)S(1)}, bf16[128,512]{1,0:T(8,128)(2,1)S(1)}, u32[]{:S(2)}, u32[]{:S(2)}) collective-permute-start(bf16[128,512]{1,0:T(8,128)(2,1)S(1)} %constant_dynamic-update-slice_fusion.refs_5_), channel_id=1, source_target_pairs={{0,4},{1,5},{2,6},{3,7},{4,0},{5,1},{6,2},{7,3},{8,12},{9,13},{10,... | collective-permute-start | bytes 393224 | tf_op jit(solution)/shard_map/ppermute | solution.py:51
  61.1 1.2 %collective-permute-start.16 = (bf16[128,512]{1,0:T(8,128)(2,1)S(1)}, bf16[128,512]{1,0:T(8,128)(2,1)S(1)}, u32[]{:S(2)}, u32[]{:S(2)}) collective-permute-start(bf16[128,512]{1,0:T(8,128)(2,1)S(1)} %constant_dynamic-update-slice_fusion.refs_5_), channel_id=1, source_target_pairs={{0,2},{1,3},{2,0},{3,1},{4,6},{5,7},{6,4},{7,5},{8,10},{9,11},{10,... | collective-permute-start | bytes 393224 | tf_op jit(solution)/shard_map/ppermute | solution.py:51
  62.3 0.4 fusion.refs_2_
  62.7 0.3 copy-done.5
  63.0 2.2 %shard_map.92 = (bf16[2048,512]{1,0:T(8,128)(2,1)S(1)}, bf16[2048,512]{1,0:T(8,128)(2,1)S(1)}) custom-call(s32[1]{0:T(128)} %bitcast.refs_0_, s32[1,2048]{1,0:T(1,128)S(1)} %copy-done.5, bf16[2048,512]{1,0:T(8,128)(2,1)S(1)} %fusion.refs_2_, bf16[256,512]{1,0:T(8,128)(2,1)S(1)} %get-tuple-element.27.refs_3_, ...), custom_call_target="tpu_custom_call" | custom-call | tf_op jit(solution)/shard_map/pallas_call | solution.py:370
  65.2 0.0 collective-permute-done.18.refs_8_
  65.2 3.1 %collective-permute-done.17.refs_7_ = bf16[128,512]{1,0:T(8,128)(2,1)S(1)} collective-permute-done((bf16[128,512]{1,0:T(8,128)(2,1)S(1)}, bf16[128,512]{1,0:T(8,128)(2,1)S(1)}, u32[]{:S(2)}, u32[]{:S(2)}) %collective-permute-start.17) | collective-permute-done | bytes 131104 | tf_op jit(solution)/shard_map/ppermute | solution.py:51
  68.3 0.0 collective-permute-done.16.refs_6_
  68.3 0.0 copy-done.2
  68.3 0.0 copy-done.4
  68.3 15.8 %shard_map.101 = bf16[256,512]{1,0:T(8,128)(2,1)} custom-call(s32[1]{0:T(128)} %bitcast.refs_0_, bf16[2048,512]{1,0:T(8,128)(2,1)S(1)} %get-tuple-element.28.refs_1_, bf16[2048,512]{1,0:T(8,128)(2,1)S(1)} %get-tuple-element.29.refs_2_, bf16[512,1536]{1,0:T(8,128)(2,1)S(1)} %copy-done.2, bf16[512,512]{1,0:T(8,128)(2,1)S(1)} %copy-done.4, ...), custom_call_target="tpu_custom_call" | custom-call | tf_op jit(solution)/shard_map/pallas_call | solution.py:439
  (17 shorter events, 0.2 us)
Async XLA Ops:
  0.0 45.9 %collective-permute-start.12 = (bf16[1024,1024]{1,0:T(8,128)(2,1)}, bf16[1024,1024]{1,0:T(8,128)(2,1)S(1)}, u32[]{:S(2)}, u32[]{:S(2)}) collective-permute-start(bf16[1024,1024]{1,0:T(8,128)(2,1)} %bitcast.5), channel_id=1, source_target_pairs={{0,8},{8,0},{16,24},{24,16},{1,9},{9,1},{17,25},{25,17},{2,10},{10... | collective-permute-start | bytes 6291464 | tf_op jit(solution)/shard_map/ppermute | solution.py:51
  0.5 45.4 %collective-permute-start.13 = (bf16[1024,1024]{1,0:T(8,128)(2,1)}, bf16[1024,1024]{1,0:T(8,128)(2,1)}, u32[]{:S(2)}, u32[]{:S(2)}) collective-permute-start(bf16[1024,1024]{1,0:T(8,128)(2,1)} %bitcast.7), channel_id=1, source_target_pairs={{0,8},{8,0},{16,24},{24,16},{1,9},{9,1},{17,25},{25,17},{2,10},{10... | collective-permute-start | bytes 6291464 | tf_op jit(solution)/shard_map/ppermute | solution.py:51
  5.7 9.8 %collective-permute-start.5 = (bf16[64,1152]{1,0:T(8,128)(2,1)S(1)}, bf16[64,1152]{1,0:T(8,128)(2,1)S(1)}, u32[]{:S(2)}, u32[]{:S(2)}) collective-permute-start(bf16[64,1152]{1,0:T(8,128)(2,1)S(1)} %get-tuple-element.33), channel_id=1, source_target_pairs={{0,2},{1,3},{2,0},{3,1},{4,6},{5,7},{6,4},{7,5},{8,10},{9,11},{10,... | collective-permute-start | bytes 442376 | tf_op jit(solution)/shard_map/ppermute | solution.py:51
  8.8 16.3 %collective-permute-start = (bf16[256,512]{1,0:T(8,128)(2,1)S(1)}, bf16[256,512]{1,0:T(8,128)(2,1)S(1)}, u32[]{:S(2)}, u32[]{:S(2)}) collective-permute-start(bf16[256,512]{1,0:T(8,128)(2,1)S(1)} %get-tuple-element.27.refs_3_), channel_id=1, source_target_pairs={{0,4},{1,5},{2,6},{3,7},{4,0},{5,1},{6,2},{7,3},{8,12},{9,13},{10,... | collective-permute-start | bytes 786440 | tf_op jit(solution)/shard_map/ppermute | solution.py:51
  11.4 13.8 %collective-permute-start.8 = (bf16[192,1152]{1,0:T(8,128)(2,1)S(1)}, bf16[192,1152]{1,0:T(8,128)(2,1)S(1)}, u32[]{:S(2)}, u32[]{:S(2)}) collective-permute-start(bf16[192,1152]{1,0:T(8,128)(2,1)S(1)} %get-tuple-element.39), channel_id=1, source_target_pairs={{0,1},{1,0},{2,3},{3,2},{4,5},{5,4},{6,7},{7,6},{8,9},{9,8},{10,11... | collective-permute-start | bytes 1327112 | tf_op jit(solution)/shard_map/ppermute | solution.py:51
  15.8 8.7 %collective-permute-start.6 = (bf16[32,1152]{1,0:T(8,128)(2,1)S(1)}, bf16[32,1152]{1,0:T(8,128)(2,1)S(1)}, u32[]{:S(2)}, u32[]{:S(2)}) collective-permute-start(bf16[32,1152]{1,0:T(8,128)(2,1)S(1)} %get-tuple-element.35), channel_id=1, source_target_pairs={{0,1},{1,0},{2,3},{3,2},{4,5},{5,4},{6,7},{7,6},{8,9},{9,8},{10,11... | collective-permute-start | bytes 221192 | tf_op jit(solution)/shard_map/ppermute | solution.py:51
  24.7 8.0 %collective-permute-start.7 = (bf16[16,1152]{1,0:T(8,128)(2,1)S(1)}, bf16[16,1152]{1,0:T(8,128)(2,1)S(1)}, u32[]{:S(2)}, u32[]{:S(2)}) collective-permute-start(bf16[16,1152]{1,0:T(8,128)(2,1)S(1)} %get-tuple-element.37), channel_id=1, source_target_pairs={{0,4},{1,5},{2,6},{3,7},{4,0},{5,1},{6,2},{7,3},{8,12},{9,13},{10,... | collective-permute-start | bytes 110600 | tf_op jit(solution)/shard_map/ppermute | solution.py:51
  25.1 20.8 %copy-start.3 = (bf16[1024,512]{1,0:T(8,128)(2,1)S(1)}, bf16[1024,512]{1,0:T(8,128)(2,1)}, u32[]{:S(2)}) copy-start(bf16[1024,512]{1,0:T(8,128)(2,1)} %refs_6_.1) | copy-start | bytes 3145732
  25.6 6.4 %collective-permute-start.9 = (bf16[96,1152]{1,0:T(8,128)(2,1)S(1)}, bf16[96,1152]{1,0:T(8,128)(2,1)S(1)}, u32[]{:S(2)}, u32[]{:S(2)}) collective-permute-start(bf16[96,1152]{1,0:T(8,128)(2,1)S(1)} %get-tuple-element.41), channel_id=1, source_target_pairs={{0,2},{1,3},{2,0},{3,1},{4,6},{5,7},{6,4},{7,5},{8,10},{9,11},{10,... | collective-permute-start | bytes 663560 | tf_op jit(solution)/shard_map/ppermute | solution.py:51
  26.1 19.8 %copy-start = (bf16[1,1024,1024]{2,1,0:T(8,128)(2,1)S(1)}, bf16[1,1024,1024]{2,1,0:T(8,128)(2,1)}, u32[]{:S(2)}) copy-start(bf16[1,1024,1024]{2,1,0:T(8,128)(2,1)} %param.11) | copy-start | bytes 6291460
  26.1 19.8 %copy-start.1 = (bf16[1,1024,1024]{2,1,0:T(8,128)(2,1)S(1)}, bf16[1,1024,1024]{2,1,0:T(8,128)(2,1)}, u32[]{:S(2)}) copy-start(bf16[1,1024,1024]{2,1,0:T(8,128)(2,1)} %param.12) | copy-start | bytes 6291460
  26.1 16.4 %collective-permute-start.1 = (bf16[256,512]{1,0:T(8,128)(2,1)S(1)}, bf16[256,512]{1,0:T(8,128)(2,1)S(1)}, u32[]{:S(2)}, u32[]{:S(2)}) collective-permute-start(bf16[256,512]{1,0:T(8,128)(2,1)S(1)} %pad_maximum_fusion.2), channel_id=1, source_target_pairs={{0,1},{1,0},{2,3},{3,2},{4,5},{5,4},{6,7},{7,6},{8,9},{9,8},{10,11... | collective-permute-start | bytes 786440 | tf_op jit(solution)/shard_map/ppermute | solution.py:51
  32.1 8.8 %collective-permute-start.2 = (bf16[256,512]{1,0:T(8,128)(2,1)S(1)}, bf16[256,512]{1,0:T(8,128)(2,1)S(1)}, u32[]{:S(2)}, u32[]{:S(2)}) collective-permute-start(bf16[256,512]{1,0:T(8,128)(2,1)S(1)} %pad_maximum_fusion.3), channel_id=1, source_target_pairs={{0,2},{1,3},{2,0},{3,1},{4,6},{5,7},{6,4},{7,5},{8,10},{9,11},{10,... | collective-permute-start | bytes 786440 | tf_op jit(solution)/shard_map/ppermute | solution.py:51
  32.7 6.3 %collective-permute-start.10 = (bf16[48,1152]{1,0:T(8,128)(2,1)S(1)}, bf16[48,1152]{1,0:T(8,128)(2,1)S(1)}, u32[]{:S(2)}, u32[]{:S(2)}) collective-permute-start(bf16[48,1152]{1,0:T(8,128)(2,1)S(1)} %get-tuple-element.43), channel_id=1, source_target_pairs={{0,4},{1,5},{2,6},{3,7},{4,0},{5,1},{6,2},{7,3},{8,12},{9,13},{10,... | collective-permute-start | bytes 331784 | tf_op jit(solution)/shard_map/ppermute | solution.py:51
  39.3 6.5 %collective-permute-start.11 = (bf16[64,1024]{1,0:T(8,128)(2,1)S(1)}, bf16[64,1024]{1,0:T(8,128)(2,1)S(1)}, u32[]{:S(2)}, u32[]{:S(2)}) collective-permute-start(bf16[64,1024]{1,0:T(8,128)(2,1)S(1)} %pad_maximum_fusion.4.refs_0_), channel_id=1, source_target_pairs={{0,16},{8,24},{16,0},{24,8},{1,17},{9,25},{17,1},{25,9},{2,18},{10... | collective-permute-start | bytes 393224 | tf_op jit(solution)/shard_map/ppermute | solution.py:51
  40.9 12.5 %collective-permute-start.4 = (bf16[512,512]{1,0:T(8,128)(2,1)S(1)}, bf16[512,512]{1,0:T(8,128)(2,1)S(1)}, u32[]{:S(2)}, u32[]{:S(2)}) collective-permute-start(bf16[512,512]{1,0:T(8,128)(2,1)S(1)} %pad_maximum_fusion.1), channel_id=1, source_target_pairs={{0,1},{1,0},{2,3},{3,2},{4,5},{5,4},{6,7},{7,6},{8,9},{9,8},{10,11... | collective-permute-start | bytes 1572872 | tf_op jit(solution)/shard_map/ppermute | solution.py:51
  42.5 11.1 %collective-permute-start.3 = (bf16[512,512]{1,0:T(8,128)(2,1)S(1)}, bf16[512,512]{1,0:T(8,128)(2,1)S(1)}, u32[]{:S(2)}, u32[]{:S(2)}) collective-permute-start(bf16[512,512]{1,0:T(8,128)(2,1)S(1)} %pad_maximum_fusion), channel_id=1, source_target_pairs={{0,2},{1,3},{2,0},{3,1},{4,6},{5,7},{6,4},{7,5},{8,10},{9,11},{10,... | collective-permute-start | bytes 1572872 | tf_op jit(solution)/shard_map/ppermute | solution.py:51
  49.0 4.3 %collective-permute-start.14 = (bf16[64,512]{1,0:T(8,128)(2,1)S(1)}, bf16[64,512]{1,0:T(8,128)(2,1)S(1)}, u32[]{:S(2)}, u32[]{:S(2)}) collective-permute-start(bf16[64,512]{1,0:T(8,128)(2,1)S(1)} %get-tuple-element.47), channel_id=1, source_target_pairs={{0,16},{8,24},{16,0},{24,8},{1,17},{9,25},{17,1},{25,9},{2,18},{10... | collective-permute-start | bytes 196616 | tf_op jit(solution)/shard_map/ppermute | solution.py:51
  49.6 0.7 copy-start.6
  53.6 4.3 %collective-permute-start.15 = (bf16[64,512]{1,0:T(8,128)(2,1)S(1)}, bf16[64,512]{1,0:T(8,128)(2,1)S(1)}, u32[]{:S(2)}, u32[]{:S(2)}) collective-permute-start(bf16[64,512]{1,0:T(8,128)(2,1)S(1)} %add_convert_fusion), channel_id=1, source_target_pairs={{0,1},{1,0},{2,3},{3,2},{4,5},{5,4},{6,7},{7,6},{8,9},{9,8},{10,11... | collective-permute-start | bytes 196616 | tf_op jit(solution)/shard_map/ppermute | solution.py:51
  57.9 7.3 %collective-permute-start.18 = (bf16[128,512]{1,0:T(8,128)(2,1)S(1)}, bf16[128,512]{1,0:T(8,128)(2,1)S(1)}, u32[]{:S(2)}, u32[]{:S(2)}) collective-permute-start(bf16[128,512]{1,0:T(8,128)(2,1)S(1)} %constant_dynamic-update-slice_fusion.refs_5_), channel_id=1, source_target_pairs={{0,6},{1,7},{2,4},{3,5},{4,2},{5,3},{6,0},{7,1},{8,14},{9,15},{10,... | collective-permute-start | bytes 393224 | tf_op jit(solution)/shard_map/ppermute | solution.py:51
  60.2 8.1 %collective-permute-start.17 = (bf16[128,512]{1,0:T(8,128)(2,1)S(1)}, bf16[128,512]{1,0:T(8,128)(2,1)S(1)}, u32[]{:S(2)}, u32[]{:S(2)}) collective-permute-start(bf16[128,512]{1,0:T(8,128)(2,1)S(1)} %constant_dynamic-update-slice_fusion.refs_5_), channel_id=1, source_target_pairs={{0,4},{1,5},{2,6},{3,7},{4,0},{5,1},{6,2},{7,3},{8,12},{9,13},{10,... | collective-permute-start | bytes 393224 | tf_op jit(solution)/shard_map/ppermute | solution.py:51
  61.1 7.2 %collective-permute-start.16 = (bf16[128,512]{1,0:T(8,128)(2,1)S(1)}, bf16[128,512]{1,0:T(8,128)(2,1)S(1)}, u32[]{:S(2)}, u32[]{:S(2)}) collective-permute-start(bf16[128,512]{1,0:T(8,128)(2,1)S(1)} %constant_dynamic-update-slice_fusion.refs_5_), channel_id=1, source_target_pairs={{0,2},{1,3},{2,0},{3,1},{4,6},{5,7},{6,4},{7,5},{8,10},{9,11},{10,... | collective-permute-start | bytes 393224 | tf_op jit(solution)/shard_map/ppermute | solution.py:51
  62.3 0.7 copy-start.5
  63.0 5.3 %copy-start.2 = (bf16[512,1536]{1,0:T(8,128)(2,1)S(1)}, bf16[512,1536]{1,0:T(8,128)(2,1)}, u32[]{:S(2)}) copy-start(bf16[512,1536]{1,0:T(8,128)(2,1)} %refs_3_.3) | copy-start | bytes 4718596
  63.0 5.3 %copy-start.4 = (bf16[512,512]{1,0:T(8,128)(2,1)S(1)}, bf16[512,512]{1,0:T(8,128)(2,1)}, u32[]{:S(2)}) copy-start(bf16[512,512]{1,0:T(8,128)(2,1)} %refs_4_.1) | copy-start | bytes 1572868

commit v7 on v6

--- a/solution.py
+++ b/solution.py
@@ -496,7 +496,6 @@
 
     others = [2 * step for step in range(1, n_clip // 2)]
     rows = [slot_in] + [swap(slot_in, "clip", mask) for mask in others]
-    rows = list(tie(rows, [array for group in brought[1:-1] for array in group]))
     results = experts(rows, first, first_other, second, second_other, w_proj)
     slot_proj = results[0].astype(F32)
     for mask, result in zip(others, results[1:]):

time: 84.3 us -> 84.3 us (level)
  no operation moved by 1% of the time
where the time goes in v7:
time: 84.3 us; the launch traced here: 84.1 us
  Pallas kernels  28.1 us (33%)
  starting transfers between devices  26.7 us (32%)
  waiting for transfers between devices  26.4 us (31%)
  other arithmetic  2.1 us (2%)
    ppermute x19, starting transfers between devices, swap(): lax.ppermute(values, axis, [(index, index ^ mask) for index in range(coun...  26.7 us
    ppermute x19, waiting for transfers between devices, swap(): lax.ppermute(values, axis, [(index, index ^ mask) for index in range(coun...  26.4 us
    pallas_call x1, Pallas kernels, tail(): pl.pallas_call(lambda *refs: tail_kernel(ranks, starts, half, *refs), out...  15.8 us
    pallas_call x1, Pallas kernels, rows_and_picks(): pl.pallas_call(lambda *refs: rows_kernel(count, *refs), out_shape=(jax.Sh...  4.03 us
    pallas_call x1, Pallas kernels, experts(): pl.pallas_call(lambda *refs: experts_kernel(count, *refs), out_shape=(jax...  3.08 us
    pallas_call x1, Pallas kernels, put_in_order(): pl.pallas_call(lambda *refs: order_kernel(ranks, starts, vis_dev, *refs),...  2.19 us
    pallas_call x6, Pallas kernels, merge(): pl.pallas_call(merge_kernel, out_shape=shape, in_specs=[VMEM, VMEM], out_...  1.83 us
  transfers between devices with their start and end apart: 19, of which 8 were waited for; matrix products, arithmetic and copies ran while one was open for 3% of the time, Pallas kernels for 15%

profile of v7, /device:TPU:0, one launch (start us, length us, event | category | flops | bytes accessed | tf_op | source)
XLA Modules:
  0.0 84.1 jit_solution(10285071734953003573)
XLA Ops:
  0.0 0.5 collective-permute-start.12
  0.5 0.1 collective-permute-start.13
  0.5 4.0 %shard_map.91 = (bf16[256,512]{1,0:T(8,128)(2,1)S(1)}, bf16[512,1024]{1,0:T(8,128)(2,1)S(1)}, f32[512,512]{1,0:T(8,128)S(1)}) custom-call(s32[1]{0:T(128)} %bitcast.refs_0_, s32[1,2048]{1,0:T(1,128)} %refs_1_.3, bf16[512,1024]{1,0:T(8,128)(2,1)} %refs_2_.1, bf16[1024,512]{1,0:T(8,128)(2,1)} %refs_3_.2), custom_call_target="tpu_custom_call" | custom-call | tf_op jit(solution)/shard_map/pallas_call | solution.py:191
  4.6 1.1 %shard_map.93 = (bf16[64,1152]{1,0:T(8,128)(2,1)S(1)}, bf16[64,1152]{1,0:T(8,128)(2,1)S(1)}, bf16[192,1152]{1,0:T(8,128)(2,1)S(1)}, bf16[192,1152]{1,0:T(8,128)(2,1)S(1)}) custom-call(s32[1]{0:T(128)} %bitcast.refs_0_, bf16[512,1024]{1,0:T(8,128)(2,1)S(1)} %get-tuple-element.28.refs_1_, f32[512,512]{1,0:T(8,128)S(1)} %get-tuple-element.29.refs_2_), custom_call_target="tpu_custom_call" | custom-call | tf_op jit(solution)/shard_map/pallas_call | solution.py:249
  5.7 3.1 %collective-permute-start.5 = (bf16[64,1152]{1,0:T(8,128)(2,1)S(1)}, bf16[64,1152]{1,0:T(8,128)(2,1)S(1)}, u32[]{:S(2)}, u32[]{:S(2)}) collective-permute-start(bf16[64,1152]{1,0:T(8,128)(2,1)S(1)} %get-tuple-element.31), channel_id=1, source_target_pairs={{0,2},{1,3},{2,0},{3,1},{4,6},{5,7},{6,4},{7,5},{8,10},{9,11},{10,... | collective-permute-start | bytes 442376 | tf_op jit(solution)/shard_map/ppermute | solution.py:51
  8.8 2.6 %collective-permute-start = (bf16[256,512]{1,0:T(8,128)(2,1)S(1)}, bf16[256,512]{1,0:T(8,128)(2,1)S(1)}, u32[]{:S(2)}, u32[]{:S(2)}) collective-permute-start(bf16[256,512]{1,0:T(8,128)(2,1)S(1)} %get-tuple-element.25.refs_3_), channel_id=1, source_target_pairs={{0,4},{1,5},{2,6},{3,7},{4,0},{5,1},{6,2},{7,3},{8,12},{9,13},{10,... | collective-permute-start | bytes 786440 | tf_op jit(solution)/shard_map/ppermute | solution.py:51
  11.4 1.5 %collective-permute-start.8 = (bf16[192,1152]{1,0:T(8,128)(2,1)S(1)}, bf16[192,1152]{1,0:T(8,128)(2,1)S(1)}, u32[]{:S(2)}, u32[]{:S(2)}) collective-permute-start(bf16[192,1152]{1,0:T(8,128)(2,1)S(1)} %get-tuple-element.37), channel_id=1, source_target_pairs={{0,1},{1,0},{2,3},{3,2},{4,5},{5,4},{6,7},{7,6},{8,9},{9,8},{10,11... | collective-permute-start | bytes 1327112 | tf_op jit(solution)/shard_map/ppermute | solution.py:51
  12.9 1.0 %multiply_cosine_fusion = (f32[256,256]{1,0:T(8,128)S(1)}, f32[256,256]{1,0:T(8,128)S(1)}) fusion(f32[256]{0:T(256)S(1)} %multiply_exponential_fusion, f32[256]{0:T(256)S(1)} %iota_convert_fusion), kind=kLoop, calls=%fused_computation.7 | loop fusion | flops 65536 | bytes 526336 | tf_op jit(solution)/shard_map/cos | solution.py:460
  13.9 1.6 %collective-permute-done.5.came_ref = bf16[64,1152]{1,0:T(8,128)(2,1)S(1)} collective-permute-done((bf16[64,1152]{1,0:T(8,128)(2,1)S(1)}, bf16[64,1152]{1,0:T(8,128)(2,1)S(1)}, u32[]{:S(2)}, u32[]{:S(2)}) %collective-permute-start.5) | collective-permute-done | bytes 147488 | tf_op jit(solution)/shard_map/ppermute | solution.py:51
  15.5 0.3 shard_map.94
  15.8 1.9 %collective-permute-start.6 = (bf16[32,1152]{1,0:T(8,128)(2,1)S(1)}, bf16[32,1152]{1,0:T(8,128)(2,1)S(1)}, u32[]{:S(2)}, u32[]{:S(2)}) collective-permute-start(bf16[32,1152]{1,0:T(8,128)(2,1)S(1)} %get-tuple-element.33), channel_id=1, source_target_pairs={{0,1},{1,0},{2,3},{3,2},{4,5},{5,4},{6,7},{7,6},{8,9},{9,8},{10,11... | collective-permute-start | bytes 221192 | tf_op jit(solution)/shard_map/ppermute | solution.py:51
  17.7 6.8 %collective-permute-done.6.came_ref = bf16[32,1152]{1,0:T(8,128)(2,1)S(1)} collective-permute-done((bf16[32,1152]{1,0:T(8,128)(2,1)S(1)}, bf16[32,1152]{1,0:T(8,128)(2,1)S(1)}, u32[]{:S(2)}, u32[]{:S(2)}) %collective-permute-start.6) | collective-permute-done | bytes 73760 | tf_op jit(solution)/shard_map/ppermute | solution.py:51
  24.5 0.3 shard_map.95
  24.7 0.4 collective-permute-start.7
  25.1 0.0 collective-permute-done.refs_4_
  25.1 0.0 copy-start.3
  25.1 0.0 collective-permute-done.8.came_ref
  25.1 0.5 shard_map.97
  25.6 0.5 collective-permute-start.9
  26.1 0.0 copy-start
  26.1 0.0 copy-start.1
  26.1 1.6 %collective-permute-start.1 = (bf16[256,512]{1,0:T(8,128)(2,1)S(1)}, bf16[256,512]{1,0:T(8,128)(2,1)S(1)}, u32[]{:S(2)}, u32[]{:S(2)}) collective-permute-start(bf16[256,512]{1,0:T(8,128)(2,1)S(1)} %pad_maximum_fusion.2), channel_id=1, source_target_pairs={{0,1},{1,0},{2,3},{3,2},{4,5},{5,4},{6,7},{7,6},{8,9},{9,8},{10,11... | collective-permute-start | bytes 786440 | tf_op jit(solution)/shard_map/ppermute | solution.py:51
  27.8 4.3 %collective-permute-done.9.came_ref = bf16[96,1152]{1,0:T(8,128)(2,1)S(1)} collective-permute-done((bf16[96,1152]{1,0:T(8,128)(2,1)S(1)}, bf16[96,1152]{1,0:T(8,128)(2,1)S(1)}, u32[]{:S(2)}, u32[]{:S(2)}) %collective-permute-start.9) | collective-permute-done | bytes 221216 | tf_op jit(solution)/shard_map/ppermute | solution.py:51
  32.1 0.3 collective-permute-start.2
  32.4 0.3 shard_map.98
  32.7 0.0 collective-permute-done.7.came_ref
  32.7 2.4 %collective-permute-start.10 = (bf16[48,1152]{1,0:T(8,128)(2,1)S(1)}, bf16[48,1152]{1,0:T(8,128)(2,1)S(1)}, u32[]{:S(2)}, u32[]{:S(2)}) collective-permute-start(bf16[48,1152]{1,0:T(8,128)(2,1)S(1)} %get-tuple-element.41), channel_id=1, source_target_pairs={{0,4},{1,5},{2,6},{3,7},{4,0},{5,1},{6,2},{7,3},{8,12},{9,13},{10,... | collective-permute-start | bytes 331784 | tf_op jit(solution)/shard_map/ppermute | solution.py:51
  35.1 0.1 multiply_sine_fusion.1
  35.2 0.2 shard_map.96
  35.5 3.6 %collective-permute-done.10.came_ref = bf16[48,1152]{1,0:T(8,128)(2,1)S(1)} collective-permute-done((bf16[48,1152]{1,0:T(8,128)(2,1)S(1)}, bf16[48,1152]{1,0:T(8,128)(2,1)S(1)}, u32[]{:S(2)}, u32[]{:S(2)}) %collective-permute-start.10) | collective-permute-done | bytes 110624 | tf_op jit(solution)/shard_map/ppermute | solution.py:51
  39.1 0.3 shard_map.99
  39.3 1.5 %collective-permute-start.11 = (bf16[64,1024]{1,0:T(8,128)(2,1)S(1)}, bf16[64,1024]{1,0:T(8,128)(2,1)S(1)}, u32[]{:S(2)}, u32[]{:S(2)}) collective-permute-start(bf16[64,1024]{1,0:T(8,128)(2,1)S(1)} %pad_maximum_fusion.4.refs_0_), channel_id=1, source_target_pairs={{0,16},{8,24},{16,0},{24,8},{1,17},{9,25},{17,1},{25,9},{2,18},{10... | collective-permute-start | bytes 393224 | tf_op jit(solution)/shard_map/ppermute | solution.py:51
  40.9 0.0 collective-permute-done.2.refs_6_
  40.9 1.6 %collective-permute-start.4 = (bf16[512,512]{1,0:T(8,128)(2,1)S(1)}, bf16[512,512]{1,0:T(8,128)(2,1)S(1)}, u32[]{:S(2)}, u32[]{:S(2)}) collective-permute-start(bf16[512,512]{1,0:T(8,128)(2,1)S(1)} %pad_maximum_fusion.1), channel_id=1, source_target_pairs={{0,1},{1,0},{2,3},{3,2},{4,5},{5,4},{6,7},{7,6},{8,9},{9,8},{10,11... | collective-permute-start | bytes 1572872 | tf_op jit(solution)/shard_map/ppermute | solution.py:51
  42.5 0.0 collective-permute-done.1.refs_5_
  42.5 3.3 %collective-permute-start.3 = (bf16[512,512]{1,0:T(8,128)(2,1)S(1)}, bf16[512,512]{1,0:T(8,128)(2,1)S(1)}, u32[]{:S(2)}, u32[]{:S(2)}) collective-permute-start(bf16[512,512]{1,0:T(8,128)(2,1)S(1)} %pad_maximum_fusion), channel_id=1, source_target_pairs={{0,2},{1,3},{2,0},{3,1},{4,6},{5,7},{6,4},{7,5},{8,10},{9,11},{10,... | collective-permute-start | bytes 1572872 | tf_op jit(solution)/shard_map/ppermute | solution.py:51
  45.9 0.0 collective-permute-done.11.refs_1_
  45.9 0.0 collective-permute-done.12.refs_3_
  45.9 0.0 collective-permute-done.13.refs_5_
  45.9 0.0 copy-done.3
  45.9 0.0 copy-done
  45.9 0.0 copy-done.1
  45.9 3.1 %shard_map.100 = (bf16[64,512]{1,0:T(8,128)(2,1)S(1)}, bf16[64,512]{1,0:T(8,128)(2,1)S(1)}) custom-call(bf16[64,1024]{1,0:T(8,128)(2,1)S(1)} %pad_maximum_fusion.4.refs_0_, bf16[64,1024]{1,0:T(8,128)(2,1)S(1)} %collective-permute-done.11.refs_1_, bf16[1024,1024]{1,0:T(8,128)(2,1)S(1)} %bitcast.6, bf16[1024,1024]{1,0:T(8,128)(2,1)S(1)} %collective-permute-done.12.refs_3_, ...), custom_call_target="tpu_custom_call" | custom-call | tf_op jit(solution)/shard_map/pallas_call | solution.py:328
  49.0 0.6 collective-permute-start.14
  49.6 0.0 copy-start.6
  49.6 0.4 multiply_add_fusion
  50.1 0.2 copy-done.6
  50.3 3.1 %collective-permute-done.14 = bf16[64,512]{1,0:T(8,128)(2,1)S(1)} collective-permute-done((bf16[64,512]{1,0:T(8,128)(2,1)S(1)}, bf16[64,512]{1,0:T(8,128)(2,1)S(1)}, u32[]{:S(2)}, u32[]{:S(2)}) %collective-permute-start.14) | collective-permute-done | bytes 65568 | tf_op jit(solution)/shard_map/ppermute | solution.py:51
  53.4 0.0 collective-permute-done.4.refs_8_
  53.4 0.3 collective-permute-done.3.refs_7_
  53.6 0.5 collective-permute-start.15
  54.1 3.8 %collective-permute-done.15 = bf16[64,512]{1,0:T(8,128)(2,1)S(1)} collective-permute-done((bf16[64,512]{1,0:T(8,128)(2,1)S(1)}, bf16[64,512]{1,0:T(8,128)(2,1)S(1)}, u32[]{:S(2)}, u32[]{:S(2)}) %collective-permute-start.15) | collective-permute-done | bytes 65568 | tf_op jit(solution)/shard_map/ppermute | solution.py:51
  57.9 2.3 %collective-permute-start.18 = (bf16[128,512]{1,0:T(8,128)(2,1)S(1)}, bf16[128,512]{1,0:T(8,128)(2,1)S(1)}, u32[]{:S(2)}, u32[]{:S(2)}) collective-permute-start(bf16[128,512]{1,0:T(8,128)(2,1)S(1)} %constant_dynamic-update-slice_fusion.refs_5_), channel_id=1, source_target_pairs={{0,6},{1,7},{2,4},{3,5},{4,2},{5,3},{6,0},{7,1},{8,14},{9,15},{10,... | collective-permute-start | bytes 393224 | tf_op jit(solution)/shard_map/ppermute | solution.py:51
  60.2 0.9 %collective-permute-start.17 = (bf16[128,512]{1,0:T(8,128)(2,1)S(1)}, bf16[128,512]{1,0:T(8,128)(2,1)S(1)}, u32[]{:S(2)}, u32[]{:S(2)}) collective-permute-start(bf16[128,512]{1,0:T(8,128)(2,1)S(1)} %constant_dynamic-update-slice_fusion.refs_5_), channel_id=1, source_target_pairs={{0,4},{1,5},{2,6},{3,7},{4,0},{5,1},{6,2},{7,3},{8,12},{9,13},{10,... | collective-permute-start | bytes 393224 | tf_op jit(solution)/shard_map/ppermute | solution.py:51
  61.1 1.2 %collective-permute-start.16 = (bf16[128,512]{1,0:T(8,128)(2,1)S(1)}, bf16[128,512]{1,0:T(8,128)(2,1)S(1)}, u32[]{:S(2)}, u32[]{:S(2)}) collective-permute-start(bf16[128,512]{1,0:T(8,128)(2,1)S(1)} %constant_dynamic-update-slice_fusion.refs_5_), channel_id=1, source_target_pairs={{0,2},{1,3},{2,0},{3,1},{4,6},{5,7},{6,4},{7,5},{8,10},{9,11},{10,... | collective-permute-start | bytes 393224 | tf_op jit(solution)/shard_map/ppermute | solution.py:51
  62.3 0.4 fusion.refs_2_
  62.7 0.3 copy-done.5
  63.0 2.2 %shard_map.92 = (bf16[2048,512]{1,0:T(8,128)(2,1)S(1)}, bf16[2048,512]{1,0:T(8,128)(2,1)S(1)}) custom-call(s32[1]{0:T(128)} %bitcast.refs_0_, s32[1,2048]{1,0:T(1,128)S(1)} %copy-done.5, bf16[2048,512]{1,0:T(8,128)(2,1)S(1)} %fusion.refs_2_, bf16[256,512]{1,0:T(8,128)(2,1)S(1)} %get-tuple-element.25.refs_3_, ...), custom_call_target="tpu_custom_call" | custom-call | tf_op jit(solution)/shard_map/pallas_call | solution.py:370
  65.2 0.0 collective-permute-done.18.refs_8_
  65.2 3.1 %collective-permute-done.17.refs_7_ = bf16[128,512]{1,0:T(8,128)(2,1)S(1)} collective-permute-done((bf16[128,512]{1,0:T(8,128)(2,1)S(1)}, bf16[128,512]{1,0:T(8,128)(2,1)S(1)}, u32[]{:S(2)}, u32[]{:S(2)}) %collective-permute-start.17) | collective-permute-done | bytes 131104 | tf_op jit(solution)/shard_map/ppermute | solution.py:51
  68.3 0.0 collective-permute-done.16.refs_6_
  68.3 0.0 copy-done.2
  68.3 0.0 copy-done.4
  68.3 15.8 %shard_map.101 = bf16[256,512]{1,0:T(8,128)(2,1)} custom-call(s32[1]{0:T(128)} %bitcast.refs_0_, bf16[2048,512]{1,0:T(8,128)(2,1)S(1)} %get-tuple-element.26.refs_1_, bf16[2048,512]{1,0:T(8,128)(2,1)S(1)} %get-tuple-element.27.refs_2_, bf16[512,1536]{1,0:T(8,128)(2,1)S(1)} %copy-done.2, bf16[512,512]{1,0:T(8,128)(2,1)S(1)} %copy-done.4, ...), custom_call_target="tpu_custom_call" | custom-call | tf_op jit(solution)/shard_map/pallas_call | solution.py:439
  (17 shorter events, 0.2 us)
Async XLA Ops:
  0.0 45.9 %collective-permute-start.12 = (bf16[1024,1024]{1,0:T(8,128)(2,1)}, bf16[1024,1024]{1,0:T(8,128)(2,1)S(1)}, u32[]{:S(2)}, u32[]{:S(2)}) collective-permute-start(bf16[1024,1024]{1,0:T(8,128)(2,1)} %bitcast.5), channel_id=1, source_target_pairs={{0,8},{8,0},{16,24},{24,16},{1,9},{9,1},{17,25},{25,17},{2,10},{10... | collective-permute-start | bytes 6291464 | tf_op jit(solution)/shard_map/ppermute | solution.py:51
  0.5 45.4 %collective-permute-start.13 = (bf16[1024,1024]{1,0:T(8,128)(2,1)}, bf16[1024,1024]{1,0:T(8,128)(2,1)}, u32[]{:S(2)}, u32[]{:S(2)}) collective-permute-start(bf16[1024,1024]{1,0:T(8,128)(2,1)} %bitcast.7), channel_id=1, source_target_pairs={{0,8},{8,0},{16,24},{24,16},{1,9},{9,1},{17,25},{25,17},{2,10},{10... | collective-permute-start | bytes 6291464 | tf_op jit(solution)/shard_map/ppermute | solution.py:51
  5.7 9.8 %collective-permute-start.5 = (bf16[64,1152]{1,0:T(8,128)(2,1)S(1)}, bf16[64,1152]{1,0:T(8,128)(2,1)S(1)}, u32[]{:S(2)}, u32[]{:S(2)}) collective-permute-start(bf16[64,1152]{1,0:T(8,128)(2,1)S(1)} %get-tuple-element.31), channel_id=1, source_target_pairs={{0,2},{1,3},{2,0},{3,1},{4,6},{5,7},{6,4},{7,5},{8,10},{9,11},{10,... | collective-permute-start | bytes 442376 | tf_op jit(solution)/shard_map/ppermute | solution.py:51
  8.8 16.3 %collective-permute-start = (bf16[256,512]{1,0:T(8,128)(2,1)S(1)}, bf16[256,512]{1,0:T(8,128)(2,1)S(1)}, u32[]{:S(2)}, u32[]{:S(2)}) collective-permute-start(bf16[256,512]{1,0:T(8,128)(2,1)S(1)} %get-tuple-element.25.refs_3_), channel_id=1, source_target_pairs={{0,4},{1,5},{2,6},{3,7},{4,0},{5,1},{6,2},{7,3},{8,12},{9,13},{10,... | collective-permute-start | bytes 786440 | tf_op jit(solution)/shard_map/ppermute | solution.py:51
  11.4 13.8 %collective-permute-start.8 = (bf16[192,1152]{1,0:T(8,128)(2,1)S(1)}, bf16[192,1152]{1,0:T(8,128)(2,1)S(1)}, u32[]{:S(2)}, u32[]{:S(2)}) collective-permute-start(bf16[192,1152]{1,0:T(8,128)(2,1)S(1)} %get-tuple-element.37), channel_id=1, source_target_pairs={{0,1},{1,0},{2,3},{3,2},{4,5},{5,4},{6,7},{7,6},{8,9},{9,8},{10,11... | collective-permute-start | bytes 1327112 | tf_op jit(solution)/shard_map/ppermute | solution.py:51
  15.8 8.7 %collective-permute-start.6 = (bf16[32,1152]{1,0:T(8,128)(2,1)S(1)}, bf16[32,1152]{1,0:T(8,128)(2,1)S(1)}, u32[]{:S(2)}, u32[]{:S(2)}) collective-permute-start(bf16[32,1152]{1,0:T(8,128)(2,1)S(1)} %get-tuple-element.33), channel_id=1, source_target_pairs={{0,1},{1,0},{2,3},{3,2},{4,5},{5,4},{6,7},{7,6},{8,9},{9,8},{10,11... | collective-permute-start | bytes 221192 | tf_op jit(solution)/shard_map/ppermute | solution.py:51
  24.7 8.0 %collective-permute-start.7 = (bf16[16,1152]{1,0:T(8,128)(2,1)S(1)}, bf16[16,1152]{1,0:T(8,128)(2,1)S(1)}, u32[]{:S(2)}, u32[]{:S(2)}) collective-permute-start(bf16[16,1152]{1,0:T(8,128)(2,1)S(1)} %get-tuple-element.35), channel_id=1, source_target_pairs={{0,4},{1,5},{2,6},{3,7},{4,0},{5,1},{6,2},{7,3},{8,12},{9,13},{10,... | collective-permute-start | bytes 110600 | tf_op jit(solution)/shard_map/ppermute | solution.py:51
  25.1 20.8 %copy-start.3 = (bf16[1024,512]{1,0:T(8,128)(2,1)S(1)}, bf16[1024,512]{1,0:T(8,128)(2,1)}, u32[]{:S(2)}) copy-start(bf16[1024,512]{1,0:T(8,128)(2,1)} %refs_6_.1) | copy-start | bytes 3145732
  25.6 6.4 %collective-permute-start.9 = (bf16[96,1152]{1,0:T(8,128)(2,1)S(1)}, bf16[96,1152]{1,0:T(8,128)(2,1)S(1)}, u32[]{:S(2)}, u32[]{:S(2)}) collective-permute-start(bf16[96,1152]{1,0:T(8,128)(2,1)S(1)} %get-tuple-element.39), channel_id=1, source_target_pairs={{0,2},{1,3},{2,0},{3,1},{4,6},{5,7},{6,4},{7,5},{8,10},{9,11},{10,... | collective-permute-start | bytes 663560 | tf_op jit(solution)/shard_map/ppermute | solution.py:51
  26.1 19.8 %copy-start = (bf16[1,1024,1024]{2,1,0:T(8,128)(2,1)S(1)}, bf16[1,1024,1024]{2,1,0:T(8,128)(2,1)}, u32[]{:S(2)}) copy-start(bf16[1,1024,1024]{2,1,0:T(8,128)(2,1)} %param.11) | copy-start | bytes 6291460
  26.1 19.8 %copy-start.1 = (bf16[1,1024,1024]{2,1,0:T(8,128)(2,1)S(1)}, bf16[1,1024,1024]{2,1,0:T(8,128)(2,1)}, u32[]{:S(2)}) copy-start(bf16[1,1024,1024]{2,1,0:T(8,128)(2,1)} %param.12) | copy-start | bytes 6291460
  26.1 16.4 %collective-permute-start.1 = (bf16[256,512]{1,0:T(8,128)(2,1)S(1)}, bf16[256,512]{1,0:T(8,128)(2,1)S(1)}, u32[]{:S(2)}, u32[]{:S(2)}) collective-permute-start(bf16[256,512]{1,0:T(8,128)(2,1)S(1)} %pad_maximum_fusion.2), channel_id=1, source_target_pairs={{0,1},{1,0},{2,3},{3,2},{4,5},{5,4},{6,7},{7,6},{8,9},{9,8},{10,11... | collective-permute-start | bytes 786440 | tf_op jit(solution)/shard_map/ppermute | solution.py:51
  32.1 8.8 %collective-permute-start.2 = (bf16[256,512]{1,0:T(8,128)(2,1)S(1)}, bf16[256,512]{1,0:T(8,128)(2,1)S(1)}, u32[]{:S(2)}, u32[]{:S(2)}) collective-permute-start(bf16[256,512]{1,0:T(8,128)(2,1)S(1)} %pad_maximum_fusion.3), channel_id=1, source_target_pairs={{0,2},{1,3},{2,0},{3,1},{4,6},{5,7},{6,4},{7,5},{8,10},{9,11},{10,... | collective-permute-start | bytes 786440 | tf_op jit(solution)/shard_map/ppermute | solution.py:51
  32.7 6.3 %collective-permute-start.10 = (bf16[48,1152]{1,0:T(8,128)(2,1)S(1)}, bf16[48,1152]{1,0:T(8,128)(2,1)S(1)}, u32[]{:S(2)}, u32[]{:S(2)}) collective-permute-start(bf16[48,1152]{1,0:T(8,128)(2,1)S(1)} %get-tuple-element.41), channel_id=1, source_target_pairs={{0,4},{1,5},{2,6},{3,7},{4,0},{5,1},{6,2},{7,3},{8,12},{9,13},{10,... | collective-permute-start | bytes 331784 | tf_op jit(solution)/shard_map/ppermute | solution.py:51
  39.3 6.5 %collective-permute-start.11 = (bf16[64,1024]{1,0:T(8,128)(2,1)S(1)}, bf16[64,1024]{1,0:T(8,128)(2,1)S(1)}, u32[]{:S(2)}, u32[]{:S(2)}) collective-permute-start(bf16[64,1024]{1,0:T(8,128)(2,1)S(1)} %pad_maximum_fusion.4.refs_0_), channel_id=1, source_target_pairs={{0,16},{8,24},{16,0},{24,8},{1,17},{9,25},{17,1},{25,9},{2,18},{10... | collective-permute-start | bytes 393224 | tf_op jit(solution)/shard_map/ppermute | solution.py:51
  40.9 12.5 %collective-permute-start.4 = (bf16[512,512]{1,0:T(8,128)(2,1)S(1)}, bf16[512,512]{1,0:T(8,128)(2,1)S(1)}, u32[]{:S(2)}, u32[]{:S(2)}) collective-permute-start(bf16[512,512]{1,0:T(8,128)(2,1)S(1)} %pad_maximum_fusion.1), channel_id=1, source_target_pairs={{0,1},{1,0},{2,3},{3,2},{4,5},{5,4},{6,7},{7,6},{8,9},{9,8},{10,11... | collective-permute-start | bytes 1572872 | tf_op jit(solution)/shard_map/ppermute | solution.py:51
  42.5 11.1 %collective-permute-start.3 = (bf16[512,512]{1,0:T(8,128)(2,1)S(1)}, bf16[512,512]{1,0:T(8,128)(2,1)S(1)}, u32[]{:S(2)}, u32[]{:S(2)}) collective-permute-start(bf16[512,512]{1,0:T(8,128)(2,1)S(1)} %pad_maximum_fusion), channel_id=1, source_target_pairs={{0,2},{1,3},{2,0},{3,1},{4,6},{5,7},{6,4},{7,5},{8,10},{9,11},{10,... | collective-permute-start | bytes 1572872 | tf_op jit(solution)/shard_map/ppermute | solution.py:51
  49.0 4.3 %collective-permute-start.14 = (bf16[64,512]{1,0:T(8,128)(2,1)S(1)}, bf16[64,512]{1,0:T(8,128)(2,1)S(1)}, u32[]{:S(2)}, u32[]{:S(2)}) collective-permute-start(bf16[64,512]{1,0:T(8,128)(2,1)S(1)} %get-tuple-element.43), channel_id=1, source_target_pairs={{0,16},{8,24},{16,0},{24,8},{1,17},{9,25},{17,1},{25,9},{2,18},{10... | collective-permute-start | bytes 196616 | tf_op jit(solution)/shard_map/ppermute | solution.py:51
  49.6 0.7 copy-start.6
  53.6 4.3 %collective-permute-start.15 = (bf16[64,512]{1,0:T(8,128)(2,1)S(1)}, bf16[64,512]{1,0:T(8,128)(2,1)S(1)}, u32[]{:S(2)}, u32[]{:S(2)}) collective-permute-start(bf16[64,512]{1,0:T(8,128)(2,1)S(1)} %add_convert_fusion), channel_id=1, source_target_pairs={{0,1},{1,0},{2,3},{3,2},{4,5},{5,4},{6,7},{7,6},{8,9},{9,8},{10,11... | collective-permute-start | bytes 196616 | tf_op jit(solution)/shard_map/ppermute | solution.py:51
  57.9 7.3 %collective-permute-start.18 = (bf16[128,512]{1,0:T(8,128)(2,1)S(1)}, bf16[128,512]{1,0:T(8,128)(2,1)S(1)}, u32[]{:S(2)}, u32[]{:S(2)}) collective-permute-start(bf16[128,512]{1,0:T(8,128)(2,1)S(1)} %constant_dynamic-update-slice_fusion.refs_5_), channel_id=1, source_target_pairs={{0,6},{1,7},{2,4},{3,5},{4,2},{5,3},{6,0},{7,1},{8,14},{9,15},{10,... | collective-permute-start | bytes 393224 | tf_op jit(solution)/shard_map/ppermute | solution.py:51
  60.2 8.1 %collective-permute-start.17 = (bf16[128,512]{1,0:T(8,128)(2,1)S(1)}, bf16[128,512]{1,0:T(8,128)(2,1)S(1)}, u32[]{:S(2)}, u32[]{:S(2)}) collective-permute-start(bf16[128,512]{1,0:T(8,128)(2,1)S(1)} %constant_dynamic-update-slice_fusion.refs_5_), channel_id=1, source_target_pairs={{0,4},{1,5},{2,6},{3,7},{4,0},{5,1},{6,2},{7,3},{8,12},{9,13},{10,... | collective-permute-start | bytes 393224 | tf_op jit(solution)/shard_map/ppermute | solution.py:51
  61.1 7.2 %collective-permute-start.16 = (bf16[128,512]{1,0:T(8,128)(2,1)S(1)}, bf16[128,512]{1,0:T(8,128)(2,1)S(1)}, u32[]{:S(2)}, u32[]{:S(2)}) collective-permute-start(bf16[128,512]{1,0:T(8,128)(2,1)S(1)} %constant_dynamic-update-slice_fusion.refs_5_), channel_id=1, source_target_pairs={{0,2},{1,3},{2,0},{3,1},{4,6},{5,7},{6,4},{7,5},{8,10},{9,11},{10,... | collective-permute-start | bytes 393224 | tf_op jit(solution)/shard_map/ppermute | solution.py:51
  62.3 0.7 copy-start.5
  63.0 5.3 %copy-start.2 = (bf16[512,1536]{1,0:T(8,128)(2,1)S(1)}, bf16[512,1536]{1,0:T(8,128)(2,1)}, u32[]{:S(2)}) copy-start(bf16[512,1536]{1,0:T(8,128)(2,1)} %refs_3_.3) | copy-start | bytes 4718596
  63.0 5.3 %copy-start.4 = (bf16[512,512]{1,0:T(8,128)(2,1)S(1)}, bf16[512,512]{1,0:T(8,128)(2,1)}, u32[]{:S(2)}) copy-start(bf16[512,512]{1,0:T(8,128)(2,1)} %refs_4_.1) | copy-start | bytes 1572868
